TPU v7x, 32 devices: a whole 2x2x4 slice. The times are simulated.
32 devices in a mesh: dp: 4 (over y, core), tp: 8 (over z, x).
Axes of the slice: x: 2, y: 2, z: 4, core: 2. Of those that a mesh axis runs over, the one named last changes fastest.
Arguments:
- tokens: bfloat16 [8192, 2048], P(('dp', 'tp')), may hold values from -6 to 6
- group_ids: int32 [8192], P(('dp', 'tp')), may hold values from 0 to 7
- mixture_counts: int32 [8], replicated, may hold values from 64 to 1024
- grad_out: bfloat16 [8192, 2048], P(('dp', 'tp')), may hold values from -6 to 6
- norm1_gain: bfloat16 [2048], replicated, may hold values from 0.5 to 1.5
- w_query: bfloat16 [2048, 2048], P(None, 'tp'), may hold values from -0.125 to 0.125
- w_key: bfloat16 [2048, 2048], P(None, 'tp'), may hold values from -0.125 to 0.125
- w_value: bfloat16 [2048, 2048], P(None, 'tp'), may hold values from -0.125 to 0.125
- w_gate_mix: bfloat16 [2048, 2048], P(None, 'tp'), may hold values from -0.125 to 0.125
- w_beta: bfloat16 [2048, 16], P(None, 'tp'), may hold values from -0.125 to 0.125
- conv_query: bfloat16 [4, 2048], P(None, 'tp'), may hold values from -3 to 3
- conv_key: bfloat16 [4, 2048], P(None, 'tp'), may hold values from -3 to 3
- conv_value: bfloat16 [4, 2048], P(None, 'tp'), may hold values from -3 to 3
- out_gain: bfloat16 [128], replicated, may hold values from 0.5 to 1.5
- w_out: bfloat16 [2048, 2048], P('tp'), may hold values from -0.125 to 0.125
- norm2_gain: bfloat16 [2048], replicated, may hold values from 0.5 to 1.5
- w_gate: bfloat16 [2048, 5632], P(None, 'tp'), may hold values from -0.125 to 0.125
- w_up: bfloat16 [2048, 5632], P(None, 'tp'), may hold values from -0.125 to 0.125
- w_down: bfloat16 [5632, 2048], P('tp'), may hold values from -0.078125 to 0.078125
Outputs:
- output: bfloat16 [8192, 2048], P(('dp', 'tp'))
- grad_tokens: bfloat16 [8192, 2048], P(('dp', 'tp'))
- grad_norm1_gain: float32 [2048], replicated
- grad_w_query: float32 [2048, 2048], P(None, 'tp')
- grad_w_key: float32 [2048, 2048], P(None, 'tp')
- grad_w_value: float32 [2048, 2048], P(None, 'tp')
- grad_w_gate_mix: float32 [2048, 2048], P(None, 'tp')
- grad_w_beta: float32 [2048, 16], P(None, 'tp')
- grad_conv_query: float32 [4, 2048], P(None, 'tp')
- grad_conv_key: float32 [4, 2048], P(None, 'tp')
- grad_conv_value: float32 [4, 2048], P(None, 'tp')
- grad_out_gain: float32 [128], replicated
- grad_w_out: float32 [2048, 2048], P('tp')
- grad_norm2_gain: float32 [2048], replicated
- grad_w_gate: float32 [2048, 5632], P(None, 'tp')
- grad_w_up: float32 [2048, 5632], P(None, 'tp')
- grad_w_down: float32 [5632, 2048], P('tp')
All inputs are finite; a program needn't handle non-finite values.
Results may differ from a plain program's by a relative error of at most 0.02.
Values may be sent and summed in bfloat16 or wider, within the bound.
A program may use at most 384 MiB of HBM per device.

v0:
```python
import jax
import jax.numpy as jnp
from jax import lax
from jax.sharding import PartitionSpec as P

HEAD_DIM = 128
SPAN = 64
SEQ_LEN = 2048
GROUPS = 8


HIGH = lax.Precision.HIGHEST
F32 = jnp.float32
BF16 = jnp.bfloat16


def rms_scale(values, gain):
    return values * lax.rsqrt(jnp.mean(values * values, -1, keepdims=True) + 1e-05) * gain


def short_conv(projected, kernel):
    row_count, channels = projected.shape
    seq_count = row_count // SEQ_LEN
    shaped = projected.reshape(seq_count, SEQ_LEN, channels)
    padded = jnp.pad(shaped, ((0, 0), (3, 0), (0, 0)))
    summed = kernel[0] * padded[:, 0:SEQ_LEN]
    for offset in range(1, 4):
        summed = summed + kernel[offset] * padded[:, offset : offset + SEQ_LEN]
    return jax.nn.silu(summed).reshape(row_count, channels)


def unit_rows(values):
    return values * lax.rsqrt(jnp.sum(values * values, -1, keepdims=True) + 1e-06)


def block_step(memory, block):
    query_rows, key_rows, value_rows, beta_rows = block
    key_beta = key_rows * beta_rows[..., None]
    value_beta = value_rows * beta_rows[..., None]
    row_ids = lax.broadcasted_iota(jnp.int32, (SPAN, SPAN), 0)
    col_ids = lax.broadcasted_iota(jnp.int32, (SPAN, SPAN), 1)
    inner_prod = jnp.einsum("bid,bjd->bij", key_beta, key_rows, precision=HIGH)
    system = jnp.eye(SPAN, dtype=F32) + jnp.where(row_ids > col_ids, inner_prod, 0.0)
    solved = jax.scipy.linalg.solve_triangular(
        system, jnp.concatenate([key_beta, value_beta], -1), lower=True, unit_diagonal=True
    )
    head_width = key_rows.shape[-1]
    w_factors = solved[..., :head_width]
    u_factors = solved[..., head_width:]
    fresh_values = u_factors - jnp.einsum("bid,bde->bie", w_factors, memory, precision=HIGH)
    scores = jnp.einsum("bid,bjd->bij", query_rows, key_rows, precision=HIGH)
    scores = jnp.where(row_ids >= col_ids, scores, 0.0)
    result = jnp.einsum("bid,bde->bie", query_rows, memory, precision=HIGH) + jnp.einsum(
        "bij,bje->bie", scores, fresh_values, precision=HIGH
    )
    memory = memory + jnp.einsum("bid,bie->bde", key_rows, fresh_values, precision=HIGH)
    return (memory, result)


def delta_rule(queries, keys_all, values_all, betas):
    batch, length, head_width = queries.shape
    blocks = length // SPAN

    def to_blocks(values):
        return values.reshape(batch, blocks, SPAN, head_width).transpose(1, 0, 2, 3)

    beta_blocks = betas.reshape(batch, blocks, SPAN).transpose(1, 0, 2)
    start_memory = jnp.zeros((batch, head_width, head_width), F32)
    final_memory, results = lax.scan(
        jax.checkpoint(block_step),
        start_memory,
        (to_blocks(queries), to_blocks(keys_all), to_blocks(values_all), beta_blocks),
    )
    return results.transpose(1, 0, 2, 3).reshape(batch, length, head_width)


def core_mixer(
    query_raw, key_raw, value_raw, gate_raw, beta_raw, conv_query, conv_key, conv_value, out_gain
):
    row_count, channels = query_raw.shape
    heads = channels // HEAD_DIM
    seq_count = row_count // SEQ_LEN

    def split_heads(values):
        shaped = values.reshape(seq_count, SEQ_LEN, heads, HEAD_DIM).transpose(0, 2, 1, 3)
        return shaped.reshape(seq_count * heads, SEQ_LEN, HEAD_DIM)

    queries = unit_rows(split_heads(short_conv(query_raw, conv_query))) * HEAD_DIM ** (-0.5)
    keys_all = unit_rows(split_heads(short_conv(key_raw, conv_key)))
    values_all = split_heads(short_conv(value_raw, conv_value))
    betas = (
        jax.nn.sigmoid(beta_raw)
        .reshape(seq_count, SEQ_LEN, heads)
        .transpose(0, 2, 1)
        .reshape(seq_count * heads, SEQ_LEN)
    )
    delta = delta_rule(queries, keys_all, values_all, betas)
    delta = (
        delta.reshape(seq_count, heads, SEQ_LEN, HEAD_DIM)
        .transpose(0, 2, 1, 3)
        .reshape(row_count, heads, HEAD_DIM)
    )
    normed = delta * lax.rsqrt(jnp.mean(delta * delta, -1, keepdims=True) + 1e-05) * out_gain
    gated = normed * jax.nn.silu(gate_raw.reshape(row_count, heads, HEAD_DIM))
    return gated.reshape(row_count, channels)


def swiglu(gate, up_vals):
    return jax.nn.silu(gate) * up_vals


def left_product(left, right):
    return lax.dot_general(left, right, (((0,), (0,)), ((), ())), preferred_element_type=F32)


def right_product(left, right):
    return lax.dot_general(left, right, (((1,), (1,)), ((), ())), preferred_element_type=F32)


def make_fold(kept_rows, weight, piece):
    weight_grad = left_product(kept_rows, piece)
    rows_grad = right_product(piece, weight)
    return (weight_grad, rows_grad)


def make_rows(source, weight, transposed):
    if transposed:
        return right_product(source, weight)
    return jnp.dot(source, weight, preferred_element_type=F32)


def shards(
    tokens,
    group_ids,
    mixture_counts,
    grad_out,
    norm1_gain,
    w_query,
    w_key,
    w_value,
    w_gate_mix,
    w_beta,
    conv_query,
    conv_key,
    conv_value,
    out_gain,
    w_out,
    norm2_gain,
    w_gate,
    w_up,
    w_down,
):
    inputs = tokens.astype(F32)
    normed, norm1_back = jax.vjp(rms_scale, inputs, norm1_gain.astype(F32))
    gathered = lax.all_gather(normed.astype(BF16), "tp", axis=0, tiled=True)
    mix_weights = jnp.concatenate([w_query, w_key, w_value, w_gate_mix, w_beta], 1)
    projected = jnp.dot(gathered, mix_weights, preferred_element_type=F32)
    head_cols = w_query.shape[1]
    query_raw = projected[:, 0:head_cols]
    key_raw = projected[:, head_cols : 2 * head_cols]
    value_raw = projected[:, 2 * head_cols : 3 * head_cols]
    gate_raw = projected[:, 3 * head_cols : 4 * head_cols]
    beta_raw = projected[:, 4 * head_cols :]
    mixed_full, core_back = jax.vjp(
        core_mixer,
        query_raw,
        key_raw,
        value_raw,
        gate_raw,
        beta_raw,
        conv_query.astype(F32),
        conv_key.astype(F32),
        conv_value.astype(F32),
        out_gain.astype(F32),
    )
    mixed = mixed_full.astype(BF16)
    attn = lax.psum_scatter(
        make_rows(mixed, w_out, False).astype(jnp.bfloat16), "tp", scatter_dimension=0, tiled=True
    ).astype(jnp.float32)
    resid = inputs + attn
    normed_mlp, norm2_back = jax.vjp(rms_scale, resid, norm2_gain.astype(F32))
    gathered_mlp = lax.all_gather(normed_mlp.astype(BF16), "tp", axis=0, tiled=True)
    pair_weights = jnp.concatenate([w_gate, w_up], 1)
    ff_cols = w_gate.shape[1]
    paired = jnp.dot(gathered_mlp, pair_weights, preferred_element_type=F32)
    hidden_full, swiglu_back = jax.vjp(swiglu, paired[:, :ff_cols], paired[:, ff_cols:])
    hidden = hidden_full.astype(BF16)
    mlp_out = lax.psum_scatter(
        make_rows(hidden, w_down, False).astype(jnp.bfloat16), "tp", scatter_dimension=0, tiled=True
    ).astype(jnp.float32)
    output = (resid + mlp_out).astype(BF16)
    group_cols = lax.broadcasted_iota(jnp.int32, (1, GROUPS), 1)
    counts = mixture_counts.astype(F32)
    group_scale = jnp.sqrt(jnp.mean(counts) / counts)
    token_scale = jnp.sum(jnp.where(group_ids[:, None] == group_cols, group_scale[None, :], 0.0), 1)
    grad_rows = grad_out.astype(F32) * token_scale[:, None]
    grad_mlp = grad_rows.astype(BF16)
    grad_w_down, hidden_grad = make_fold(
        hidden, w_down, lax.all_gather(grad_mlp, "tp", axis=0, tiled=True)
    )
    gate_grad, up_grad = swiglu_back(hidden_grad)
    pair_grad = jnp.concatenate([gate_grad, up_grad], 1).astype(BF16)
    pair_weight_grad = left_product(gathered_mlp, pair_grad)
    normed_mlp_grad = lax.psum_scatter(
        make_rows(pair_grad, pair_weights, True).astype(jnp.bfloat16),
        "tp",
        scatter_dimension=0,
        tiled=True,
    ).astype(jnp.float32)
    resid_norm_grad, norm2_grad = norm2_back(normed_mlp_grad)
    resid_grad = grad_rows + resid_norm_grad
    attn_grad = resid_grad.astype(BF16)
    grad_w_out, mixed_grad = make_fold(
        mixed, w_out, lax.all_gather(attn_grad, "tp", axis=0, tiled=True)
    )
    core_grads = core_back(mixed_grad)
    raw_grad = jnp.concatenate(
        [core_grads[0], core_grads[1], core_grads[2], core_grads[3], core_grads[4]], 1
    ).astype(BF16)
    mix_weight_grad = left_product(gathered, raw_grad)
    normed_grad = lax.psum_scatter(
        make_rows(raw_grad, mix_weights, True).astype(jnp.bfloat16),
        "tp",
        scatter_dimension=0,
        tiled=True,
    ).astype(jnp.float32)
    input_norm_grad, norm1_grad = norm1_back(normed_grad)
    grad_tokens = (resid_grad + input_norm_grad).astype(BF16)
    summed = (
        lax.psum(mix_weight_grad.astype(jnp.bfloat16), "dp").astype(jnp.float32),
        lax.psum(core_grads[5].astype(jnp.bfloat16), "dp").astype(jnp.float32),
        lax.psum(core_grads[6].astype(jnp.bfloat16), "dp").astype(jnp.float32),
        lax.psum(core_grads[7].astype(jnp.bfloat16), "dp").astype(jnp.float32),
        lax.psum(grad_w_out.astype(jnp.bfloat16), "dp").astype(jnp.float32),
        lax.psum(pair_weight_grad.astype(jnp.bfloat16), "dp").astype(jnp.float32),
        lax.psum(grad_w_down.astype(jnp.bfloat16), "dp").astype(jnp.float32),
    )
    gains = lax.psum((norm1_grad, core_grads[8], norm2_grad), ("dp", "tp"))
    mix_total = summed[0]
    pair_total = summed[5]
    return (
        output,
        grad_tokens,
        gains[0],
        mix_total[:, 0:head_cols],
        mix_total[:, head_cols : 2 * head_cols],
        mix_total[:, 2 * head_cols : 3 * head_cols],
        mix_total[:, 3 * head_cols : 4 * head_cols],
        mix_total[:, 4 * head_cols :],
        summed[1],
        summed[2],
        summed[3],
        gains[1],
        summed[4],
        gains[2],
        pair_total[:, :ff_cols],
        pair_total[:, ff_cols:],
        summed[6],
    )


def solution(mesh):
    return jax.shard_map(
        shards,
        mesh=mesh,
        in_specs=(
            P(("dp", "tp"), None),
            P(("dp", "tp")),
            P(),
            P(("dp", "tp"), None),
            P(),
            P(None, "tp"),
            P(None, "tp"),
            P(None, "tp"),
            P(None, "tp"),
            P(None, "tp"),
            P(None, "tp"),
            P(None, "tp"),
            P(None, "tp"),
            P(),
            P("tp", None),
            P(),
            P(None, "tp"),
            P(None, "tp"),
            P("tp", None),
        ),
        out_specs=(
            P(("dp", "tp"), None),
            P(("dp", "tp"), None),
            P(),
            P(None, "tp"),
            P(None, "tp"),
            P(None, "tp"),
            P(None, "tp"),
            P(None, "tp"),
            P(None, "tp"),
            P(None, "tp"),
            P(None, "tp"),
            P(),
            P("tp", None),
            P(),
            P(None, "tp"),
            P(None, "tp"),
            P("tp", None),
        ),
        check_vma=False,
    )
```

profile of v0, /device:TPU:0, one launch (start us, length us, event | category | flops | bytes accessed | tf_op | source)
XLA Modules:
  0.0 3022.6 jit_solution(7801795868643242664)
XLA Ops:
  24.9 116.2 %all-gather.5.cloned.1.call-done = bf16[2048,2048]{1,0:T(8,128)(2,1)} async-done(((bf16[256,2048]{1,0:T(8,128)(2,1)}), bf16[2048,2048]{1,0:T(8,128)(2,1)}) %all-gather.5.cloned.1.call-update) | async-done | bytes 8388624 | tf_op jit(solution)/shard_map/all_gather | solution.py:155
  141.1 13.4 fusion.154
  158.4 11.5 fusion.115
  199.2 582.8 %while.40 = (s32[]{:T(128)}, f32[2,128,128]{2,1,0:T(8,128)S(1)}, f32[32,2,64,128]{3,2,0,1:T(8,128)}, f32[32,2,128,128]{3,2,1,0:T(8,128)}, f32[32,2,64,128]{3,2,1...) while((s32[]{:T(128)}, f32[2,128,128]{2,1,0:T(8,128)S(1)}, ...), condition=%wide.region_4.6_spmd.clone, body=%wide.region_3.5_spmd.clone.sunk | while | flops 138735680 | bytes 2446986 | solution.py:69
  202.2 9.8 custom-call.31
  220.4 9.8 custom-call.31
  238.6 9.8 custom-call.31
  256.8 9.8 custom-call.31
  275.0 9.8 custom-call.31
  293.2 9.8 custom-call.31
  311.4 9.8 custom-call.31
  329.6 9.8 custom-call.31
  347.8 9.8 custom-call.31
  366.0 9.8 custom-call.31
  384.3 9.8 custom-call.31
  402.5 9.8 custom-call.31
  420.7 9.8 custom-call.31
  438.9 9.8 custom-call.31
  457.2 9.8 custom-call.31
  475.3 9.8 custom-call.31
  493.5 9.8 custom-call.31
  693.8 9.8 custom-call.31
  766.7 9.8 custom-call.31
  797.6 146.7 %reduce-scatter.5.cloned.1.call-done = bf16[256,2048]{1,0:T(8,128)(2,1)} async-done(((bf16[2048,2048]{1,0:T(8,128)(2,1)}), bf16[256,2048]{1,0:T(8,128)(2,1)}) %reduce-scatter.5.cloned.1.call-update) | async-done | bytes 1048592 | tf_op jit(solution)/shard_map/reduce_scatter | solution.py:177
  957.7 114.4 %all-gather.7.cloned.1.call-done = bf16[2048,2048]{1,0:T(8,128)(2,1)} async-done(((bf16[256,2048]{1,0:T(8,128)(2,1)}), bf16[2048,2048]{1,0:T(8,128)(2,1)}) %all-gather.7.cloned.1.call-update) | async-done | bytes 8388624 | tf_op jit(solution)/shard_map/all_gather | solution.py:182
  1072.1 19.2 fusion.155
  1091.3 106.7 %all-gather.9.cloned.1.call-done = bf16[2048,2048]{1,0:T(8,128)(2,1)} async-done(((bf16[256,2048]{1,0:T(8,128)(2,1)}), bf16[2048,2048]{1,0:T(8,128)(2,1)}) %all-gather.9.cloned.1.call-update) | async-done | bytes 8388624 | tf_op jit(solution)/shard_map/all_gather | solution.py:199
  1198.0 14.6 fusion.77
  1215.1 18.0 convolution_convert_fusion.1
  1233.2 147.3 %reduce-scatter.9.cloned.1.call-done = bf16[256,2048]{1,0:T(8,128)(2,1)} async-done(((bf16[2048,2048]{1,0:T(8,128)(2,1)}), bf16[256,2048]{1,0:T(8,128)(2,1)}) %reduce-scatter.9.cloned.1.call-update) | async-done | bytes 1048592 | tf_op jit(solution)/shard_map/reduce_scatter | solution.py:204
  1388.6 10.8 convolution_convert_fusion.6
  1399.4 17.7 convolution_convert_fusion.4
  1417.1 94.3 %all-gather.11.cloned.1.call-done = bf16[2048,2048]{1,0:T(8,128)(2,1)} async-done(((bf16[256,2048]{1,0:T(8,128)(2,1)}), bf16[2048,2048]{1,0:T(8,128)(2,1)}) %all-gather.11.cloned.1.call-update) | async-done | bytes 8388624 | tf_op jit(solution)/shard_map/all_gather | solution.py:214
  1548.9 829.5 %while.41 = (s32[]{:T(128)}, f32[2,128,128]{2,1,0:T(8,128)}, f32[32,2,64,128]{3,2,0,1:T(8,128)}, f32[32,2,64,128]{3,2,0,1:T(8,128)}, f32[32,2,64,128]{3,2,0,1:T(...) while((s32[]{:T(128)}, f32[2,128,128]{2,1,0:T(8,128)}, ...), condition=%wide.region_17.19_spmd.clone, body=%wide.region_14.18_spmd.clone.sunk | while | flops 359223232 | bytes 6535395 | solution.py:69
  1658.6 9.8 custom-call.32
  1710.4 9.8 custom-call.32
  1736.3 9.8 custom-call.32
  1840.1 9.8 custom-call.32
  1970.0 9.8 custom-call.32
  2073.9 9.8 custom-call.32
  2400.8 16.7 multiply_reduce_fusion.5
  2450.4 11.1 convolution_convert_fusion
  2461.5 16.4 convolution_convert_fusion.5
  2478.0 11.2 convolution_convert_fusion.2
  2498.3 205.6 %all-reduce.34.cloned.1.call-done = (bf16[2048,1026]{0,1:T(8,128)(2,1)}, bf16[2048,1408]{1,0:T(8,128)(2,1)}, bf16[256,2048]{1,0:T(8,128)(2,1)}, bf16[704,2048]{1,0:T(8,128)(2,1)}) async-done(((bf16[2048,1026]{0,1:T(8,128)(2,1)}, bf16[2048,1408]{1,0:T(8,128)(2,1)}, bf16[256,2048]{1,0:T(8,128)(2,1)}, bf16[704,2048]{1,0:T(8,128)(2,1)}), (bf16[2048,1026]{0,1:T(8,128)(2,1)}, bf16[2048,1408]{1,0:T(8,128)(2,1)}, ...) | async-done | bytes 13901840 | tf_op jit(solution)/shard_map/psum | solution.py:230
  2751.4 105.7 %reduce-scatter.11.cloned.1.call-done = bf16[256,2048]{1,0:T(8,128)(2,1)} async-done(((bf16[2048,2048]{1,0:T(8,128)(2,1)}), bf16[256,2048]{1,0:T(8,128)(2,1)}) %reduce-scatter.11.cloned.1.call-update) | async-done | bytes 1048592 | tf_op jit(solution)/shard_map/reduce_scatter | solution.py:221
  2859.7 42.6 %all-reduce.29 = (f32[2048]{0:T(1024)}, f32[128]{0:T(128)}, f32[2048]{0:T(1024)}) all-reduce(f32[2048]{0:T(1024)S(1)} %get-tuple-element.603, f32[128]{0:T(128)S(1)} %copy-done.79, f32[2048]{0:T(1024)S(1)} %copy-done.39), channel_id=1, replica_groups=mesh['dp'=4,'tp'=8] {'dp','tp'}, use_global_device_ids=true, to_apply=%region_23.25 | all-reduce | flops 4224 | bytes 33792 | tf_op jit(solution)/shard_map/psum | solution.py:238
  2902.2 107.4 %reduce-scatter.7.cloned.1.call-done = bf16[256,2048]{1,0:T(8,128)(2,1)} async-done(((bf16[2048,2048]{1,0:T(8,128)(2,1)}), bf16[256,2048]{1,0:T(8,128)(2,1)}) %reduce-scatter.7.cloned.1.call-update) | async-done | bytes 1048592 | tf_op jit(solution)/shard_map/reduce_scatter | solution.py:188
  (1853 shorter events, 1404.6 us)
Async XLA Ops:
  7.2 1190.8 %copy-start = (bf16[704,2048]{1,0:T(8,128)(2,1)S(1)}, bf16[704,2048]{1,0:T(8,128)(2,1)}, u32[]{:S(2)}) copy-start(bf16[704,2048]{1,0:T(8,128)(2,1)} %param.43) | copy-start | bytes 8650756
  7.2 6.2 copy-start.74
  7.2 133.9 %all-gather.5.cloned.1.call-start = ((), (), s32[]{:S(2)}) async-start(), calls=%async_computation.4 | async-start | bytes 9437184 | tf_op jit(solution)/shard_map/all_gather | solution.py:155
  13.3 931.0 %reduce-scatter.5.cloned.1.call-start = ((), (), s32[]{:S(2)}) async-start(), calls=%async_computation.5 | async-start | bytes 9437184 | tf_op jit(solution)/shard_map/reduce_scatter | solution.py:177
  13.7 7.2 copy-start.27
  157.2 12.8 copy-start.6
  157.2 12.8 copy-start.7
  797.0 275.1 %all-gather.7.cloned.1.call-start = ((), (), s32[]{:S(2)}) async-start(), calls=%async_computation.6 | async-start | bytes 9437184 | tf_op jit(solution)/shard_map/all_gather | solution.py:182
  797.6 586.4 %copy-start.32 = (f32[2048]{0:T(1024)}, f32[2048]{0:T(1024)S(1)}, u32[]{:S(2)}) copy-start(f32[2048]{0:T(1024)S(1)} %convert_element_type.157) | copy-start | bytes 24580
  946.5 437.6 %copy-start.40 = (f32[256]{0:T(256)}, f32[256]{0:T(256)S(1)}, u32[]{:S(2)}) copy-start(f32[256]{0:T(256)S(1)} %fusion.133) | copy-start | bytes 3076
  948.0 250.0 %all-gather.9.cloned.1.call-start = ((), (), s32[]{:S(2)}) async-start(), calls=%async_computation.8 | async-start | bytes 9437184 | tf_op jit(solution)/shard_map/all_gather | solution.py:199
  949.5 434.6 %copy-start.44 = (f32[256]{0:T(256)}, f32[256]{0:T(256)S(1)}, u32[]{:S(2)}) copy-start(f32[256]{0:T(256)S(1)} %select_reduce_fusion) | copy-start | bytes 3076
  951.9 428.6 %reduce-scatter.9.cloned.1.call-start = ((), (), s32[]{:S(2)}) async-start(), calls=%async_computation.9 | async-start | bytes 9437184 | tf_op jit(solution)/shard_map/reduce_scatter | solution.py:204
  1233.1 278.2 %all-gather.11.cloned.1.call-start = ((), (), s32[]{:S(2)}) async-start(), calls=%async_computation.10 | async-start | bytes 9437184 | tf_op jit(solution)/shard_map/all_gather | solution.py:214
  1387.3 1316.6 %all-reduce.34.cloned.1.call-start = ((), (), s32[]{:S(2)}) async-start(), calls=%async_computation.12 | async-start | bytes 27852800 | tf_op jit(solution)/shard_map/psum | solution.py:230
  1388.6 10.9 copy-start.84
  1388.6 10.9 copy-start.86
  1511.4 6.1 copy-start.8
  1517.5 5.0 copy-start.9
  1590.6 4.5 copy-start.30
  1772.1 4.5 copy-start.30
  1798.1 4.5 copy-start.30
  2083.7 4.5 copy-start.30
  2265.3 4.5 copy-start.30
  2317.2 4.5 copy-start.30
  2400.8 16.8 copy-start.63
  2400.8 16.8 copy-start.65
  2400.8 16.8 copy-start.67
  2400.8 16.8 copy-start.69
  2429.7 5.3 copy-start.11
  2429.7 5.3 copy-start.12
  2429.7 5.3 copy-start.13
  2429.7 5.9 copy-start.14
  2439.1 11.3 slice-start
  2442.0 8.3 copy-start.31
  2442.0 8.3 slice-start.1
  2461.5 395.6 %reduce-scatter.11.cloned.1.call-start = ((), (), s32[]{:S(2)}) async-start(), calls=%async_computation.11 | async-start | bytes 9437184 | tf_op jit(solution)/shard_map/reduce_scatter | solution.py:221
  2477.9 531.8 %reduce-scatter.7.cloned.1.call-start = ((), (), s32[]{:S(2)}) async-start(), calls=%async_computation.7 | async-start | bytes 9437184 | tf_op jit(solution)/shard_map/reduce_scatter | solution.py:188
  2744.3 5.4 copy-start.26
  2749.8 107.3 %copy-start.36 = (f32[2048]{0:T(1024)S(1)}, f32[2048]{0:T(1024)}, u32[]{:S(2)}) copy-start(f32[2048]{0:T(1024)} %copy-done.35) | copy-start | bytes 24580
  2749.8 107.3 %copy-start.43 = (f32[256]{0:T(256)S(1)}, f32[256]{0:T(256)}, u32[]{:S(2)}) copy-start(f32[256]{0:T(256)} %copy-done.42) | copy-start | bytes 3076
  2749.8 109.9 %copy-start.39 = (f32[2048]{0:T(1024)S(1)}, f32[2048]{0:T(1024)}, u32[]{:S(2)}) copy-start(f32[2048]{0:T(1024)} %get-tuple-element.592) | copy-start | bytes 24580
  2749.8 109.9 %copy-start.79 = (f32[128]{0:T(128)S(1)}, f32[128]{0:T(128)}, u32[]{:S(2)}) copy-start(f32[128]{0:T(128)} %get-tuple-element.581) | copy-start | bytes 1540
  2749.8 152.5 %copy-start.71 = (f32[256]{0:T(256)S(1)}, f32[256]{0:T(256)}, u32[]{:S(2)}) copy-start(f32[256]{0:T(256)} %copy-done.70) | copy-start | bytes 3076
  2749.8 259.9 %copy-start.33 = (f32[2048]{0:T(1024)S(1)}, f32[2048]{0:T(1024)}, u32[]{:S(2)}) copy-start(f32[2048]{0:T(1024)} %copy-done.32) | copy-start | bytes 24580
  2749.8 259.9 %copy-start.41 = (f32[256]{0:T(256)S(1)}, f32[256]{0:T(256)}, u32[]{:S(2)}) copy-start(f32[256]{0:T(256)} %copy-done.40) | copy-start | bytes 3076
  2749.8 259.9 %copy-start.45 = (f32[256]{0:T(256)S(1)}, f32[256]{0:T(256)}, u32[]{:S(2)}) copy-start(f32[256]{0:T(256)} %copy-done.44) | copy-start | bytes 3076
  2749.8 259.9 %copy-start.73 = (f32[256]{0:T(256)S(1)}, f32[256]{0:T(256)}, u32[]{:S(2)}) copy-start(f32[256]{0:T(256)} %copy-done.72) | copy-start | bytes 3076
  (81 other events, 282.1 us)
Sparse Core Ops, SparseCore 0:
  13.5 127.6 all-gather.4
  797.1 147.2 reduce-scatter.4
  948.2 123.9 all-gather.6
  1074.9 123.1 all-gather.8
  1233.2 147.2 reduce-scatter.8
  1387.4 123.9 all-gather.10
  2461.6 242.2 all-reduce.33
  2708.0 149.0 reduce-scatter.10
  2860.7 148.9 reduce-scatter.6
where the time goes:
time: 3050 us; the launch traced here: 3020 us
  waiting for transfers between devices  1140 us (37%)
  other arithmetic  908 us (30%)
  matrix products  601 us (20%)
  local copies, waits for them, and re-layouts  295 us (10%)
  blocking collectives  49.8 us (2%)
    another operation x192, other arithmetic, block_step(): jax.scipy.linalg.solve_triangular(system, jnp.concatenate([key_beta, valu...  635 us
    psum x1, waiting for transfers between devices, shards(): lax.psum(mix_weight_grad.astype(jnp.bfloat16), 'dp').astype(jnp.float32)  206 us
    squeeze x160, local copies, waits for them, and re-layouts, delta_rule(): lax.scan(jax.checkpoint(block_step), start_memory, (to_blocks(queries), t...  152 us
    reduce_scatter x1, waiting for transfers between devices, shards(): lax.psum_scatter(make_rows(pair_grad, pair_weights, True).astype(jnp.bflo...  147 us
    reduce_scatter x1, waiting for transfers between devices, shards(): lax.psum_scatter(make_rows(mixed, w_out, False).astype(jnp.bfloat16), 'tp...  147 us
    all_gather x1, waiting for transfers between devices, shards(): gathered = lax.all_gather(normed.astype(BF16), 'tp', axis=0, tiled=True)  116 us
    all_gather x1, waiting for transfers between devices, shards(): lax.all_gather(normed_mlp.astype(BF16), 'tp', axis=0, tiled=True)  114 us
    reduce_scatter x1, waiting for transfers between devices, shards(): lax.psum_scatter(make_rows(hidden, w_down, False).astype(jnp.bfloat16), '...  107 us
  transfers between devices with their start and end apart: 9, of which 9 were waited for; matrix products, arithmetic and copies ran while one was open for 5% of the time, Pallas kernels for 0%

commit v1 on v0

v1 whole, which is shorter than its diff:
```python
import jax
import jax.numpy as jnp
from jax import lax
from jax.experimental import pallas as pl
from jax.experimental.pallas import tpu as pltpu
from jax.sharding import PartitionSpec as P

GROUPS = 8
HEAD_DIM = 128
SPAN = 64
SEQ_LEN = 2048
TILE = 256
F32 = jnp.float32
BF16 = jnp.bfloat16
NN = ((1,), (0,))
NT = ((1,), (1,))
TN = ((0,), (0,))


def split(values):
    high = values.astype(BF16)
    return high, (values - high.astype(F32)).astype(BF16)


def dot(left, right, dims):
    return lax.dot_general(left, right, (dims, ((), ())), preferred_element_type=F32)


def product(left, right, dims):
    return (
        dot(left[0], right[0], dims)
        + (dot(left[0], right[1], dims) + dot(left[1], right[0], dims))
    )


def quick(left, right, dims):
    return dot(left[0], right[0], dims)


def rows_of(pair, start, size):
    return pair[0][start : start + size], pair[1][start : start + size]


def sigmoid(values):
    return 1.0 / (1.0 + jnp.exp(-values))


def tile_masks():
    row = lax.broadcasted_iota(jnp.int32, (TILE, TILE), 0)
    col = lax.broadcasted_iota(jnp.int32, (TILE, TILE), 1)
    return row, col


def invert(lower, row, col):
    def level(size):
        return (row // (2 * size) == col // (2 * size)) & (row // size > col // size)

    inverse = jnp.where(row == col, 1.0, 0.0) - jnp.where(level(1), lower, 0.0)
    size = 2
    while size < SPAN:
        part = split(jnp.where(level(size), lower, 0.0))
        held = split(inverse)
        inverse = inverse - product(held, split(product(part, held, NN)), NN)
        size *= 2
    return inverse


def conv_rows(buffer, taps):
    total = taps[0:1] * buffer[pl.ds(5, TILE), :]
    for offset in range(1, 4):
        total = total + taps[offset : offset + 1] * buffer[pl.ds(5 + offset, TILE), :]
    return total


def mixer_forward_body(
    heads, proj_ref, conv_ref, gain_ref, mixed_ref, wu_ref, fresh_ref, out_ref, state_ref,
    inverse_ref, rows_buf, state,
):
    tile = pl.program_id(1)
    wide = heads * HEAD_DIM

    @pl.when(tile == 0)
    def _():
        rows_buf[0:8, :] = jnp.zeros((8, 3 * wide), F32)
        state[...] = jnp.zeros_like(state)

    @pl.when(tile > 0)
    def _():
        rows_buf[0:8, :] = rows_buf[TILE : TILE + 8, :]

    rows_buf[8 : 8 + TILE, :] = proj_ref[:, : 3 * wide]
    summed = conv_rows(rows_buf, conv_ref[...])
    active = summed * sigmoid(summed)
    row, col = tile_masks()
    same = row // SPAN == col // SPAN
    for head in range(heads):
        lo = head * HEAD_DIM
        query = active[:, lo : lo + HEAD_DIM]
        key = active[:, wide + lo : wide + lo + HEAD_DIM]
        value = active[:, 2 * wide + lo : 2 * wide + lo + HEAD_DIM]
        gate = proj_ref[:, 3 * wide + lo : 3 * wide + lo + HEAD_DIM]
        beta = sigmoid(proj_ref[:, 4 * wide + head : 4 * wide + head + 1])
        query = query * (
            lax.rsqrt(jnp.sum(query * query, -1, keepdims=True) + 1e-06) * HEAD_DIM ** (-0.5)
        )
        key = key * lax.rsqrt(jnp.sum(key * key, -1, keepdims=True) + 1e-06)
        key_beta = key * beta
        key_s = split(key)
        query_s = split(query)
        key_beta_s = split(key_beta)
        lower = jnp.where(same & (row > col), product(key_beta_s, key_s, NT), 0.0)
        inverse = invert(lower, row, col)
        inverse_ref[head] = inverse
        both = product(split(inverse), split(jnp.concatenate([key_beta, value * beta], 1)), NN)
        wu_ref[:, 2 * lo : 2 * lo + 2 * HEAD_DIM] = both
        scores = jnp.where(same & (row >= col), product(query_s, key_s, NT), 0.0)
        weights_s = split(both[:, :HEAD_DIM])
        fresh_all = []
        carried_all = []
        memory = state[head]
        for block in range(TILE // SPAN):
            start = block * SPAN
            state_ref[block, head] = memory
            stacked = tuple(
                jnp.concatenate([a[start : start + SPAN], b[start : start + SPAN]], 0)
                for a, b in zip(weights_s, query_s)
            )
            read = product(stacked, split(memory), NN)
            fresh = both[start : start + SPAN, HEAD_DIM:] - read[:SPAN]
            fresh_all.append(fresh)
            carried_all.append(read[SPAN:])
            memory = memory + product(rows_of(key_s, start, SPAN), split(fresh), TN)
        state[head] = memory
        fresh = jnp.concatenate(fresh_all, 0)
        fresh_ref[:, lo : lo + HEAD_DIM] = fresh
        out = jnp.concatenate(carried_all, 0) + product(split(scores), split(fresh), NN)
        out_ref[:, lo : lo + HEAD_DIM] = out
        scale = lax.rsqrt(jnp.mean(out * out, -1, keepdims=True) + 1e-05)
        mixed = out * scale * gain_ref[...] * (gate * sigmoid(gate))
        mixed_ref[:, lo : lo + HEAD_DIM] = mixed.astype(BF16)


def mixer_forward(proj, conv, gain, heads):
    rows = proj.shape[0]
    wide = heads * HEAD_DIM
    tiles = SEQ_LEN // TILE
    seqs = rows // SEQ_LEN
    blocks = TILE // SPAN

    def at(seq, tile):
        return (seq * tiles + tile, 0)

    return pl.pallas_call(
        lambda *refs: mixer_forward_body(heads, *refs),
        grid=(seqs, tiles),
        in_specs=[
            pl.BlockSpec((TILE, proj.shape[1]), at),
            pl.BlockSpec(conv.shape, lambda seq, tile: (0, 0)),
            pl.BlockSpec(gain.shape, lambda seq, tile: (0, 0)),
        ],
        out_specs=[
            pl.BlockSpec((TILE, wide), at),
            pl.BlockSpec((TILE, 2 * wide), at),
            pl.BlockSpec((TILE, wide), at),
            pl.BlockSpec((TILE, wide), at),
            pl.BlockSpec((blocks, heads, HEAD_DIM, HEAD_DIM), lambda s, t: (s * tiles + t, 0, 0, 0)),
            pl.BlockSpec((None, heads, TILE, TILE), lambda s, t: (s * tiles + t, 0, 0, 0)),
        ],
        out_shape=[
            jax.ShapeDtypeStruct((rows, wide), BF16),
            jax.ShapeDtypeStruct((rows, 2 * wide), F32),
            jax.ShapeDtypeStruct((rows, wide), F32),
            jax.ShapeDtypeStruct((rows, wide), F32),
            jax.ShapeDtypeStruct((rows // SPAN, heads, HEAD_DIM, HEAD_DIM), F32),
            jax.ShapeDtypeStruct((rows // TILE, heads, TILE, TILE), F32),
        ],
        scratch_shapes=[
            pltpu.VMEM((TILE + 8, 3 * wide), F32),
            pltpu.VMEM((heads, HEAD_DIM, HEAD_DIM), F32),
        ],
        compiler_params=pltpu.CompilerParams(vmem_limit_bytes=48 * 2**20),
        name="mixer_forward",
    )(proj, conv, gain)


def unit_back(raw, scale, grad):
    along = jnp.sum(raw * grad, -1, keepdims=True)
    return scale * grad - raw * (scale * scale * scale * along)


def mixer_backward_body(
    heads, proj_ref, before_ref, conv_ref, gain_ref, grad_ref, wu_ref, fresh_ref, out_ref,
    state_ref, inverse_ref, raw_grad_ref, conv_grad_ref, gain_grad_ref,
    rows_buf, grad_buf, state_grad,
):
    step = pl.program_id(1)
    steps = pl.num_programs(1)
    wide = heads * HEAD_DIM

    @pl.when((step == 0) & (pl.program_id(0) == 0))
    def _():
        conv_grad_ref[...] = jnp.zeros_like(conv_grad_ref)
        gain_grad_ref[...] = jnp.zeros_like(gain_grad_ref)

    @pl.when(step == 0)
    def _():
        grad_buf[TILE : TILE + 8, :] = jnp.zeros((8, 3 * wide), F32)
        state_grad[...] = jnp.zeros_like(state_grad)

    @pl.when(step > 0)
    def _():
        grad_buf[TILE : TILE + 8, :] = grad_buf[0:8, :]

    first = step == steps - 1
    rows_buf[0:8, :] = jnp.where(first, 0.0, before_ref[:, : 3 * wide])
    rows_buf[8 : 8 + TILE, :] = proj_ref[:, : 3 * wide]
    summed = conv_rows(rows_buf, conv_ref[...])
    smooth = sigmoid(summed)
    active = summed * smooth
    slope = smooth * (1.0 + summed * (1.0 - smooth))
    row, col = tile_masks()
    same = row // SPAN == col // SPAN
    lane = lax.broadcasted_iota(jnp.int32, (TILE, HEAD_DIM), 1)
    beta_grads = jnp.zeros((TILE, HEAD_DIM), F32)
    gain_total = jnp.zeros((1, HEAD_DIM), F32)
    for head in range(heads):
        lo = head * HEAD_DIM
        query_raw = active[:, lo : lo + HEAD_DIM]
        key_raw = active[:, wide + lo : wide + lo + HEAD_DIM]
        value = active[:, 2 * wide + lo : 2 * wide + lo + HEAD_DIM]
        gate = proj_ref[:, 3 * wide + lo : 3 * wide + lo + HEAD_DIM]
        beta = sigmoid(proj_ref[:, 4 * wide + head : 4 * wide + head + 1])
        query_scale = lax.rsqrt(jnp.sum(query_raw * query_raw, -1, keepdims=True) + 1e-06)
        key_scale = lax.rsqrt(jnp.sum(key_raw * key_raw, -1, keepdims=True) + 1e-06)
        query = query_raw * (query_scale * HEAD_DIM ** (-0.5))
        key = key_raw * key_scale
        key_beta = key * beta
        grad = grad_ref[:, lo : lo + HEAD_DIM]
        out = out_ref[:, lo : lo + HEAD_DIM]
        scale = lax.rsqrt(jnp.mean(out * out, -1, keepdims=True) + 1e-05)
        gate_s = sigmoid(gate)
        normed = out * scale
        gain_total = gain_total + jnp.sum(grad * normed * (gate * gate_s), 0, keepdims=True)
        gate_grad = grad * normed * gain_ref[...] * (gate_s * (1.0 + gate * (1.0 - gate_s)))
        normed_grad = grad * gain_ref[...] * (gate * gate_s)
        out_grad = scale * normed_grad - out * (
            scale * scale * scale * jnp.mean(out * normed_grad, -1, keepdims=True)
        )
        key_s = split(key)
        query_s = split(query)
        out_grad_s = split(out_grad)
        fresh = fresh_ref[:, lo : lo + HEAD_DIM]
        fresh_s = split(fresh)
        both = wu_ref[:, 2 * lo : 2 * lo + 2 * HEAD_DIM]
        both_s = split(both)
        weights_s = both_s[0][:, :HEAD_DIM], both_s[1][:, :HEAD_DIM]
        within = same & (row >= col)
        scores_s = split(jnp.where(within, product(query_s, key_s, NT), 0.0))
        scores_grad_s = split(jnp.where(within, product(out_grad_s, fresh_s, NT), 0.0))
        fresh_grad_in = product(scores_s, out_grad_s, TN)
        query_grad = product(scores_grad_s, key_s, NN)
        key_grad = product(scores_grad_s, query_s, TN)
        carry = state_grad[head]
        blocks = TILE // SPAN
        parts = [None] * blocks
        for block in range(blocks - 1, -1, -1):
            start = block * SPAN
            memory_s = split(state_ref[block, head])
            carry_s = split(carry)
            fresh_grad = fresh_grad_in[start : start + SPAN] + product(
                rows_of(key_s, start, SPAN), carry_s, NN
            )
            fresh_grad_s = split(fresh_grad)
            out_rows = rows_of(out_grad_s, start, SPAN)
            stacked = tuple(
                jnp.concatenate([a, b], 0) for a, b in zip(out_rows, fresh_grad_s)
            )
            back = product(stacked, memory_s, NT)
            through = product(rows_of(fresh_s, start, SPAN), carry_s, NT)
            parts[block] = (fresh_grad, back[:SPAN], -back[SPAN:], through)
            carry = carry + (
                product(rows_of(query_s, start, SPAN), out_rows, TN)
                - product(rows_of(weights_s, start, SPAN), fresh_grad_s, TN)
            )
        state_grad[head] = carry
        fresh_grad, query_more, weights_grad, key_more = (
            jnp.concatenate([part[i] for part in parts], 0) for i in range(4)
        )
        query_grad = query_grad + query_more
        key_grad = key_grad + key_more
        both_grad = jnp.concatenate([weights_grad, fresh_grad], 1)
        right_grad = product(split(inverse_ref[head]), split(both_grad), TN)
        lower_grad = jnp.where(
            same & (row > col), -product(split(right_grad), both_s, NT), 0.0
        )
        lower_grad_s = split(lower_grad)
        key_beta_grad = right_grad[:, :HEAD_DIM] + product(lower_grad_s, key_s, NN)
        value_beta_grad = right_grad[:, HEAD_DIM:]
        key_grad = key_grad + product(lower_grad_s, split(key_beta), TN) + key_beta_grad * beta
        beta_grad = jnp.sum(key_beta_grad * key + value_beta_grad * value, -1, keepdims=True)
        beta_grad = beta_grad * (beta * (1.0 - beta))
        beta_grads = jnp.where(lane == head, beta_grad, beta_grads)
        query_back = unit_back(query_raw, query_scale, query_grad * HEAD_DIM ** (-0.5))
        key_back = unit_back(key_raw, key_scale, key_grad)
        grad_buf[0:TILE, lo : lo + HEAD_DIM] = query_back * slope[:, lo : lo + HEAD_DIM]
        grad_buf[0:TILE, wide + lo : wide + lo + HEAD_DIM] = (
            key_back * slope[:, wide + lo : wide + lo + HEAD_DIM]
        )
        grad_buf[0:TILE, 2 * wide + lo : 2 * wide + lo + HEAD_DIM] = (
            value_beta_grad * beta * slope[:, 2 * wide + lo : 2 * wide + lo + HEAD_DIM]
        )
        raw_grad_ref[:, 3 * wide + lo : 3 * wide + lo + HEAD_DIM] = gate_grad.astype(BF16)
    raw_grad_ref[:, 4 * wide :] = beta_grads.astype(BF16)
    gain_grad_ref[0:1, :] += gain_total
    taps = conv_ref[...]
    here = grad_buf[0:TILE, :]
    total = taps[3:4] * here
    conv_grad_ref[3:4, :] += jnp.sum(here * rows_buf[8 : 8 + TILE, :], 0, keepdims=True)
    for offset in range(3):
        total = total + taps[offset : offset + 1] * grad_buf[pl.ds(3 - offset, TILE), :]
        conv_grad_ref[offset : offset + 1, :] += jnp.sum(
            here * rows_buf[pl.ds(5 + offset, TILE), :], 0, keepdims=True
        )
    raw_grad_ref[:, : 3 * wide] = total.astype(BF16)


def mixer_backward(proj, conv, gain, grad, wu, fresh, out, states, inverses, heads):
    rows = proj.shape[0]
    wide = heads * HEAD_DIM
    tiles = SEQ_LEN // TILE
    seqs = rows // SEQ_LEN
    blocks = TILE // SPAN

    def index(seq, step):
        return seq * tiles + tiles - 1 - step

    def at(seq, step):
        return (index(seq, step), 0)

    def ahead(seq, step):
        return (jnp.maximum(index(seq, step) * (TILE // 8) - 1, 0), 0)

    def fixed(seq, step):
        return (0, 0)

    return pl.pallas_call(
        lambda *refs: mixer_backward_body(heads, *refs),
        grid=(seqs, tiles),
        in_specs=[
            pl.BlockSpec((TILE, proj.shape[1]), at),
            pl.BlockSpec((8, proj.shape[1]), ahead),
            pl.BlockSpec(conv.shape, fixed),
            pl.BlockSpec(gain.shape, fixed),
            pl.BlockSpec((TILE, wide), at),
            pl.BlockSpec((TILE, 2 * wide), at),
            pl.BlockSpec((TILE, wide), at),
            pl.BlockSpec((TILE, wide), at),
            pl.BlockSpec(
                (blocks, heads, HEAD_DIM, HEAD_DIM), lambda s, t: (index(s, t), 0, 0, 0)
            ),
            pl.BlockSpec((None, heads, TILE, TILE), lambda s, t: (index(s, t), 0, 0, 0)),
        ],
        out_specs=[
            pl.BlockSpec((TILE, 4 * wide + 128), at),
            pl.BlockSpec((8, 3 * wide), fixed),
            pl.BlockSpec((8, HEAD_DIM), fixed),
        ],
        out_shape=[
            jax.ShapeDtypeStruct((rows, 4 * wide + 128), BF16),
            jax.ShapeDtypeStruct((8, 3 * wide), F32),
            jax.ShapeDtypeStruct((8, HEAD_DIM), F32),
        ],
        scratch_shapes=[
            pltpu.VMEM((TILE + 8, 3 * wide), F32),
            pltpu.VMEM((TILE + 8, 3 * wide), F32),
            pltpu.VMEM((heads, HEAD_DIM, HEAD_DIM), F32),
        ],
        compiler_params=pltpu.CompilerParams(vmem_limit_bytes=48 * 2**20),
        name="mixer_backward",
    )(proj, proj, conv, gain, grad, wu, fresh, out, states, inverses)


def rms_scale(values, gain):
    return values * lax.rsqrt(jnp.mean(values * values, -1, keepdims=True) + 1e-05) * gain


def swiglu(gate, up_vals):
    return jax.nn.silu(gate) * up_vals


def left_product(left, right):
    return lax.dot_general(left, right, (((0,), (0,)), ((), ())), preferred_element_type=F32)


def right_product(left, right):
    return lax.dot_general(left, right, (((1,), (1,)), ((), ())), preferred_element_type=F32)


def make_fold(kept_rows, weight, piece):
    weight_grad = left_product(kept_rows, piece)
    rows_grad = right_product(piece, weight)
    return (weight_grad, rows_grad)


def make_rows(source, weight, transposed):
    if transposed:
        return right_product(source, weight)
    return jnp.dot(source, weight, preferred_element_type=F32)


def shards(
    tokens,
    group_ids,
    mixture_counts,
    grad_out,
    norm1_gain,
    w_query,
    w_key,
    w_value,
    w_gate_mix,
    w_beta,
    conv_query,
    conv_key,
    conv_value,
    out_gain,
    w_out,
    norm2_gain,
    w_gate,
    w_up,
    w_down,
):
    inputs = tokens.astype(F32)
    normed, norm1_back = jax.vjp(rms_scale, inputs, norm1_gain.astype(F32))
    gathered = lax.all_gather(normed.astype(BF16), "tp", axis=0, tiled=True)
    heads = w_beta.shape[1]
    w_beta = jnp.pad(w_beta, ((0, 0), (0, 128 - heads)))
    mix_weights = jnp.concatenate([w_query, w_key, w_value, w_gate_mix, w_beta], 1)
    projected = jnp.dot(gathered, mix_weights, preferred_element_type=F32)
    head_cols = w_query.shape[1]
    conv = jnp.concatenate([conv_query, conv_key, conv_value], 1).astype(F32)
    gain = out_gain.astype(F32)[None]
    mixed, *kept = mixer_forward(projected, conv, gain, heads)
    attn = lax.psum_scatter(
        make_rows(mixed, w_out, False).astype(jnp.bfloat16), "tp", scatter_dimension=0, tiled=True
    ).astype(jnp.float32)
    resid = inputs + attn
    normed_mlp, norm2_back = jax.vjp(rms_scale, resid, norm2_gain.astype(F32))
    gathered_mlp = lax.all_gather(normed_mlp.astype(BF16), "tp", axis=0, tiled=True)
    pair_weights = jnp.concatenate([w_gate, w_up], 1)
    ff_cols = w_gate.shape[1]
    paired = jnp.dot(gathered_mlp, pair_weights, preferred_element_type=F32)
    hidden_full, swiglu_back = jax.vjp(swiglu, paired[:, :ff_cols], paired[:, ff_cols:])
    hidden = hidden_full.astype(BF16)
    mlp_out = lax.psum_scatter(
        make_rows(hidden, w_down, False).astype(jnp.bfloat16), "tp", scatter_dimension=0, tiled=True
    ).astype(jnp.float32)
    output = (resid + mlp_out).astype(BF16)
    group_cols = lax.broadcasted_iota(jnp.int32, (1, GROUPS), 1)
    counts = mixture_counts.astype(F32)
    group_scale = jnp.sqrt(jnp.mean(counts) / counts)
    token_scale = jnp.sum(jnp.where(group_ids[:, None] == group_cols, group_scale[None, :], 0.0), 1)
    grad_rows = grad_out.astype(F32) * token_scale[:, None]
    grad_mlp = grad_rows.astype(BF16)
    grad_w_down, hidden_grad = make_fold(
        hidden, w_down, lax.all_gather(grad_mlp, "tp", axis=0, tiled=True)
    )
    gate_grad, up_grad = swiglu_back(hidden_grad)
    pair_grad = jnp.concatenate([gate_grad, up_grad], 1).astype(BF16)
    pair_weight_grad = left_product(gathered_mlp, pair_grad)
    normed_mlp_grad = lax.psum_scatter(
        make_rows(pair_grad, pair_weights, True).astype(jnp.bfloat16),
        "tp",
        scatter_dimension=0,
        tiled=True,
    ).astype(jnp.float32)
    resid_norm_grad, norm2_grad = norm2_back(normed_mlp_grad)
    resid_grad = grad_rows + resid_norm_grad
    attn_grad = resid_grad.astype(BF16)
    grad_w_out, mixed_grad = make_fold(
        mixed, w_out, lax.all_gather(attn_grad, "tp", axis=0, tiled=True)
    )
    raw_grad, conv_grad, gain_grad = mixer_backward(
        projected, conv, gain, mixed_grad, *kept, heads
    )
    mix_weight_grad = left_product(gathered, raw_grad)
    normed_grad = lax.psum_scatter(
        make_rows(raw_grad, mix_weights, True).astype(jnp.bfloat16),
        "tp",
        scatter_dimension=0,
        tiled=True,
    ).astype(jnp.float32)
    input_norm_grad, norm1_grad = norm1_back(normed_grad)
    grad_tokens = (resid_grad + input_norm_grad).astype(BF16)
    summed = (
        lax.psum(mix_weight_grad.astype(jnp.bfloat16), "dp").astype(jnp.float32),
        lax.psum(grad_w_out.astype(jnp.bfloat16), "dp").astype(jnp.float32),
        lax.psum(pair_weight_grad.astype(jnp.bfloat16), "dp").astype(jnp.float32),
        lax.psum(grad_w_down.astype(jnp.bfloat16), "dp").astype(jnp.float32),
    )
    conv_total = lax.psum(conv_grad[:4], "dp")
    gains = lax.psum((norm1_grad, gain_grad[0], norm2_grad), ("dp", "tp"))
    mix_total = summed[0]
    pair_total = summed[2]
    return (
        output,
        grad_tokens,
        gains[0],
        mix_total[:, 0:head_cols],
        mix_total[:, head_cols : 2 * head_cols],
        mix_total[:, 2 * head_cols : 3 * head_cols],
        mix_total[:, 3 * head_cols : 4 * head_cols],
        mix_total[:, 4 * head_cols : 4 * head_cols + heads],
        conv_total[:, 0:head_cols],
        conv_total[:, head_cols : 2 * head_cols],
        conv_total[:, 2 * head_cols :],
        gains[1],
        summed[1],
        gains[2],
        pair_total[:, :ff_cols],
        pair_total[:, ff_cols:],
        summed[3],
    )


def solution(mesh):
    return jax.shard_map(
        shards,
        mesh=mesh,
        in_specs=(
            P(("dp", "tp"), None),
            P(("dp", "tp")),
            P(),
            P(("dp", "tp"), None),
            P(),
            P(None, "tp"),
            P(None, "tp"),
            P(None, "tp"),
            P(None, "tp"),
            P(None, "tp"),
            P(None, "tp"),
            P(None, "tp"),
            P(None, "tp"),
            P(),
            P("tp", None),
            P(),
            P(None, "tp"),
            P(None, "tp"),
            P("tp", None),
        ),
        out_specs=(
            P(("dp", "tp"), None),
            P(("dp", "tp"), None),
            P(),
            P(None, "tp"),
            P(None, "tp"),
            P(None, "tp"),
            P(None, "tp"),
            P(None, "tp"),
            P(None, "tp"),
            P(None, "tp"),
            P(None, "tp"),
            P(),
            P("tp", None),
            P(),
            P(None, "tp"),
            P(None, "tp"),
            P("tp", None),
        ),
        check_vma=False,
    )
```

time: 3050 us -> 1640 us (0.54)
  other arithmetic: 908 us -> 34.4 us
  matrix products: 601 us -> 158 us
  local copies, waits for them, and re-layouts: 295 us -> 51.5 us
  Pallas kernels: 0 us -> 154 us
    another operation x225 -> x0, other arithmetic: 668 us -> none  [the longest x192 635 us: block_step(): jax.scipy.linalg.solve_triangular(system, jnp.concatenate([key_beta, valu...]
    dot_general x704 -> x0, matrix products: 413 us -> none  [the longest x128 106 us: block_step(): inner_prod = jnp.einsum('bid,bjd->bij', key_beta, key_rows, precision=HIGH)]
    pallas_call x0 -> x2, Pallas kernels: none -> 154 us  [the longest x1 89.5 us: mixer_forward(): pl.pallas_call(lambda *refs: mixer_forward_body(heads, *refs), grid=(seqs...]
    squeeze x160 -> x1, local copies, waits for them, and re-layouts: 152 us -> 0.01 us  [shards(): gains = lax.psum((norm1_grad, gain_grad[0], norm2_grad), ('dp', 'tp'))]
    dynamic_update_slice x96 -> x0, other arithmetic: 62.2 us -> none  [delta_rule(): lax.scan(jax.checkpoint(block_step), start_memory, (to_blocks(queries), t...]
    reduce_sum x39 -> x0, other arithmetic: 57.4 us -> none  [the longest x32 25.5 us: block_step(): value_beta = value_rows * beta_rows[..., None]]
    mul x37 -> x0, other arithmetic: 53.7 us -> none  [the longest x32 30.3 us: block_step(): key_beta = key_rows * beta_rows[..., None]]
    another operation x128 -> x0, matrix products: 35.3 us -> none  [block_step(): jax.scipy.linalg.solve_triangular(system, jnp.concatenate([key_beta, valu...]
  transfers between devices with their start and end apart: 9 -> 9, of which waited for: 9 -> 9; matrix products, arithmetic and copies ran while one was open for 5% -> 8% of each run, Pallas kernels for 0% -> 0%
where the time goes in v1:
time: 1640 us; the launch traced here: 1630 us
  waiting for transfers between devices  1170 us (71%)
  matrix products  158 us (10%)
  Pallas kernels  154 us (9%)
  blocking collectives  55 us (3%)
  local copies, waits for them, and re-layouts  51.5 us (3%)
  other arithmetic  34.4 us (2%)
    psum x1, waiting for transfers between devices, shards(): lax.psum(mix_weight_grad.astype(jnp.bfloat16), 'dp').astype(jnp.float32)  209 us
    reduce_scatter x1, waiting for transfers between devices, shards(): lax.psum_scatter(make_rows(pair_grad, pair_weights, True).astype(jnp.bflo...  147 us
    reduce_scatter x1, waiting for transfers between devices, shards(): lax.psum_scatter(make_rows(mixed, w_out, False).astype(jnp.bfloat16), 'tp...  147 us
    all_gather x1, waiting for transfers between devices, shards(): gathered = lax.all_gather(normed.astype(BF16), 'tp', axis=0, tiled=True)  119 us
    reduce_scatter x1, waiting for transfers between devices, shards(): lax.psum_scatter(make_rows(raw_grad, mix_weights, True).astype(jnp.bfloat...  118 us
    all_gather x1, waiting for transfers between devices, shards(): lax.all_gather(normed_mlp.astype(BF16), 'tp', axis=0, tiled=True)  114 us
    reduce_scatter x1, waiting for transfers between devices, shards(): lax.psum_scatter(make_rows(hidden, w_down, False).astype(jnp.bfloat16), '...  108 us
    all_gather x1, waiting for transfers between devices, shards(): lax.all_gather(grad_mlp, 'tp', axis=0, tiled=True)  107 us
  transfers between devices with their start and end apart: 9, of which 9 were waited for; matrix products, arithmetic and copies ran while one was open for 8% of the time, Pallas kernels for 0%

profile of v1, /device:TPU:0, one launch (start us, length us, event | category | flops | bytes accessed | tf_op | source)
XLA Modules:
  0.0 1632.9 jit_solution(15778230977328405221)
XLA Ops:
  7.3 1.7 fusion.15
  10.8 2.5 fusion.8
  14.5 2.4 constant_dynamic-update-slice_fusion.3
  16.9 2.3 constant_dynamic-update-slice_fusion.2
  22.2 119.0 %all-gather.5.cloned.1.call-done = bf16[2048,2048]{1,0:T(8,128)(2,1)} async-done(((bf16[256,2048]{1,0:T(8,128)(2,1)}), bf16[2048,2048]{1,0:T(8,128)(2,1)}) %all-gather.5.cloned.1.call-update) | async-done | bytes 8388624 | tf_op jit(solution)/shard_map/all_gather | solution.py:434
  141.2 16.2 fusion.26.refs_0_.refs_1_
  157.4 89.5 %mixer_forward.1 = (bf16[2048,256]{1,0:T(8,128)(2,1)S(1)}, f32[2048,512]{1,0:T(8,128)}, f32[2048,256]{1,0:T(8,128)S(1)}, f32[2048,256]{1,0:T(8,128)S(1)}, f32[32...) custom-call(f32[2048,1152]{1,0:T(8,128)} %fusion.26.refs_0_.refs_1_, f32[4,768]{1,0:T(4,128)S(1)} %maximum_convert_fusion.refs_1_.refs_2_, ...), custom_call_target="tpu_custom_call" | custom-call | tf_op jit(solution)/shard_map/mixer_forward/pallas_call | solution.py:153
  246.9 1.3 copy-done.3
  250.5 5.6 convolution_convert_fusion.4
  256.8 146.7 %reduce-scatter.5.cloned.1.call-done = bf16[256,2048]{1,0:T(8,128)(2,1)} async-done(((bf16[2048,2048]{1,0:T(8,128)(2,1)}), bf16[256,2048]{1,0:T(8,128)(2,1)}) %reduce-scatter.5.cloned.1.call-update) | async-done | bytes 1048592 | tf_op jit(solution)/shard_map/reduce_scatter | solution.py:443
  403.5 2.0 multiply_reduce_fusion
  405.4 2.9 multiply_convert_fusion.2
  409.8 2.4 fusion.17
  412.3 3.9 constant_dynamic-update-slice_fusion.5
  416.2 1.8 constant_dynamic-update-slice_fusion.4
  418.0 114.4 %all-gather.7.cloned.1.call-done = bf16[2048,2048]{1,0:T(8,128)(2,1)} async-done(((bf16[256,2048]{1,0:T(8,128)(2,1)}), bf16[2048,2048]{1,0:T(8,128)(2,1)}) %all-gather.7.cloned.1.call-update) | async-done | bytes 8388624 | tf_op jit(solution)/shard_map/all_gather | solution.py:448
  532.4 18.8 %fusion.27 = f32[2048,1408]{0,1:T(8,128)} fusion(bf16[2048,2048]{1,0:T(8,128)(2,1)} %all-gather.7.cloned.1.call-done, bf16[2048,1408]{0,1:T(8,128)(2,1)} %constant_dynamic-update-slice_fusion.4), kind=kOutput, calls=%fused_computation.73 | convolution fusion | flops 11811160064 | bytes 25690112 | tf_op jit(solution)/shard_map/dot_general | solution.py:451
  551.3 107.1 %all-gather.9.cloned.1.call-done = bf16[2048,2048]{1,0:T(8,128)(2,1)} async-done(((bf16[256,2048]{1,0:T(8,128)(2,1)}), bf16[2048,2048]{1,0:T(8,128)(2,1)}) %all-gather.9.cloned.1.call-update) | async-done | bytes 8388624 | tf_op jit(solution)/shard_map/all_gather | solution.py:465
  658.4 14.6 fusion.2
  672.9 1.6 copy-done.25
  675.5 18.0 %convolution_convert_fusion.2 = bf16[2048,2048]{1,0:T(8,128)(2,1)} fusion(bf16[2048,1408]{0,1:T(8,128)(2,1)} %constant_dynamic-update-slice_fusion.4, bf16[2048,704]{0,1:T(8,128)(2,1)S(1)} %get-tuple-element.81, bf16[2048,704]{0,1:T(8,128)(2,1)S(1)} %get-tuple-element.80), kind=kOutput, calls=%fused_computation.3 | convolution fusion | flops 11826888704 | bytes 19922944 | tf_op jit(solution)/shard_map/dot_general | solution.py:396
  693.5 147.3 %reduce-scatter.9.cloned.1.call-done = bf16[256,2048]{1,0:T(8,128)(2,1)} async-done(((bf16[2048,2048]{1,0:T(8,128)(2,1)}), bf16[256,2048]{1,0:T(8,128)(2,1)}) %reduce-scatter.9.cloned.1.call-update) | async-done | bytes 1048592 | tf_op jit(solution)/shard_map/reduce_scatter | solution.py:470
  840.8 2.8 fusion.10
  843.7 4.0 fusion.22
  847.8 11.2 convolution_convert_fusion.6
  859.0 17.3 %convolution_convert_fusion.5 = bf16[2048,1408]{1,0:T(8,128)(2,1)} fusion(bf16[2048,2048]{1,0:T(8,128)(2,1)} %all-gather.7.cloned.1.call-done, bf16[2048,704]{0,1:T(8,128)(2,1)S(1)} %copy-done.28, bf16[2048,704]{0,1:T(8,128)(2,1)S(1)} %copy-done.26), kind=kOutput, calls=%fused_computation.6 | convolution fusion | flops 11825577984 | bytes 19922944 | tf_op jit(solution)/shard_map/dot_general | solution.py:392
  876.4 95.5 %all-gather.11.cloned.1.call-done = bf16[2048,2048]{1,0:T(8,128)(2,1)} async-done(((bf16[256,2048]{1,0:T(8,128)(2,1)}), bf16[2048,2048]{1,0:T(8,128)(2,1)}) %all-gather.11.cloned.1.call-update) | async-done | bytes 8388624 | tf_op jit(solution)/shard_map/all_gather | solution.py:480
  971.8 6.1 fusion.28.refs_4_
  978.0 64.1 %mixer_backward.1 = (bf16[2048,1152]{1,0:T(8,128)(2,1)}, f32[8,768]{1,0:T(8,128)S(1)}, f32[8,128]{1,0:T(8,128)S(1)}) custom-call(f32[2048,1152]{1,0:T(8,128)} %fusion.26.refs_0_.refs_1_, f32[2048,1152]{1,0:T(8,128)} %fusion.26.refs_0_.refs_1_, f32[4,768]{1,0:T(4,128)S(1)} %maximum_convert_fusion.refs_1_.refs_2_, ...), custom_call_target="tpu_custom_call" | custom-call | tf_op jit(solution)/shard_map/mixer_backward/pallas_call | solution.py:346
  1042.1 6.8 convolution_convert_fusion.7
  1048.9 15.2 convolution_convert_fusion
  1064.2 16.5 %convolution_convert_fusion.1 = bf16[2048,2048]{1,0:T(8,128)(2,1)} fusion(bf16[2048,1152]{1,0:T(8,128)(2,1)} %get-tuple-element.32, bf16[2048,1152]{1,0:T(8,128)(2,1)} %pad_dynamic-update-slice_fusion), kind=kOutput, calls=%fused_computation.2 | convolution fusion | flops 9667870720 | bytes 17825792 | tf_op jit(solution)/shard_map/dot_general | solution.py:396
  1080.8 11.1 convolution_convert_fusion.3
  1091.9 12.2 psum.58
  1104.7 209.4 %all-reduce.5.cloned.1.call-done = (bf16[2048,1152]{1,0:T(8,128)(2,1)}, bf16[2048,1408]{1,0:T(8,128)(2,1)}, bf16[256,2048]{1,0:T(8,128)(2,1)}, bf16[704,2048]{1,0:T(8,128)(2,1)}) async-done(((bf16[2048,1152]{1,0:T(8,128)(2,1)}, bf16[2048,1408]{1,0:T(8,128)(2,1)}, bf16[256,2048]{1,0:T(8,128)(2,1)}, bf16[704,2048]{1,0:T(8,128)(2,1)}), (bf16[2048,1152]{1,0:T(8,128)(2,1)}, bf16[2048,1408]{1,0:T(8,128)(2,1)}, ...) | async-done | bytes 14417936 | tf_op jit(solution)/shard_map/psum | solution.py:495
  1314.1 2.1 slice.62
  1316.2 2.2 copy.41
  1318.4 2.9 convert_element_type.115
  1321.3 3.3 convert_element_type.119
  1324.6 5.9 fusion.23
  1330.5 6.4 copy.43
  1336.9 6.4 copy.42
  1343.3 5.8 fusion.24
  1349.1 118.0 %reduce-scatter.11.cloned.1.call-done = bf16[256,2048]{1,0:T(8,128)(2,1)} async-done(((bf16[2048,2048]{1,0:T(8,128)(2,1)}), bf16[256,2048]{1,0:T(8,128)(2,1)}) %reduce-scatter.11.cloned.1.call-update) | async-done | bytes 1048592 | tf_op jit(solution)/shard_map/reduce_scatter | solution.py:486
  1467.0 2.6 fusion.11
  1469.6 42.8 %all-reduce.1 = (f32[2048]{0:T(1024)}, f32[128]{0:T(128)}, f32[2048]{0:T(1024)}) all-reduce(f32[2048]{0:T(1024)S(1)} %get-tuple-element.71, f32[128]{0:T(128)S(1)} %slice_bitcast_fusion, f32[2048]{0:T(1024)S(1)} %get-tuple-element.69), channel_id=1, replica_groups=mesh['dp'=4,'tp'=8] {'dp','tp'}, use_global_device_ids=true, to_apply=%region_11.12 | all-reduce | flops 4224 | bytes 33792 | tf_op jit(solution)/shard_map/psum | solution.py:501
  1512.4 107.6 %reduce-scatter.7.cloned.1.call-done = bf16[256,2048]{1,0:T(8,128)(2,1)} async-done(((bf16[2048,2048]{1,0:T(8,128)(2,1)}), bf16[256,2048]{1,0:T(8,128)(2,1)}) %reduce-scatter.7.cloned.1.call-update) | async-done | bytes 1048592 | tf_op jit(solution)/shard_map/reduce_scatter | solution.py:454
  1620.1 5.9 fusion.14
  (97 shorter events, 11.6 us)
Async XLA Ops:
  7.2 651.2 %copy-start = (bf16[704,2048]{1,0:T(8,128)(2,1)S(1)}, bf16[704,2048]{1,0:T(8,128)(2,1)}, u32[]{:S(2)}) copy-start(bf16[704,2048]{1,0:T(8,128)(2,1)} %param.37) | copy-start | bytes 8650756
  7.2 7.2 copy-start.18
  7.2 7.2 copy-start.19
  7.2 7.2 copy-start.20
  7.2 7.3 copy-start.23
  7.2 133.9 %all-gather.5.cloned.1.call-start = ((), (), s32[]{:S(2)}) async-start(), calls=%async_computation.4 | async-start | bytes 9437184 | tf_op jit(solution)/shard_map/all_gather | solution.py:434
  9.0 0.6 copy-start.15
  9.5 0.7 copy-start.13
  10.2 0.6 copy-start.11
  13.4 390.1 %reduce-scatter.5.cloned.1.call-start = ((), (), s32[]{:S(2)}) async-start(), calls=%async_computation.5 | async-start | bytes 9437184 | tf_op jit(solution)/shard_map/reduce_scatter | solution.py:443
  14.5 4.7 copy-start.8
  14.5 5.8 copy-start.9
  157.4 93.1 %copy-start.10 = (bf16[256,2048]{1,0:T(8,128)(2,1)S(1)}, bf16[256,2048]{1,0:T(8,128)(2,1)}, u32[]{:S(2)}) copy-start(bf16[256,2048]{1,0:T(8,128)(2,1)} %param.33) | copy-start | bytes 3145732
  246.9 1.3 copy-start.3
  248.2 1.3 copy-start.5
  249.5 1.0 copy-start.1
  256.1 0.7 copy-start.17
  256.1 152.3 %copy-start.24 = (s32[8]{0:T(128)S(1)}, s32[8]{0:T(128)}, u32[]{:S(2)}) copy-start(s32[8]{0:T(128)} %param.21) | copy-start | bytes 100
  256.1 153.6 %copy-start.21 = (s32[256]{0:T(256)S(1)}, s32[256]{0:T(256)}, u32[]{:S(2)}) copy-start(s32[256]{0:T(256)} %param.20) | copy-start | bytes 3076
  256.1 276.3 %all-gather.7.cloned.1.call-start = ((), (), s32[]{:S(2)}) async-start(), calls=%async_computation.6 | async-start | bytes 9437184 | tf_op jit(solution)/shard_map/all_gather | solution.py:448
  408.4 250.0 %all-gather.9.cloned.1.call-start = ((), (), s32[]{:S(2)}) async-start(), calls=%async_computation.8 | async-start | bytes 9437184 | tf_op jit(solution)/shard_map/all_gather | solution.py:465
  412.2 428.6 %reduce-scatter.9.cloned.1.call-start = ((), (), s32[]{:S(2)}) async-start(), calls=%async_computation.9 | async-start | bytes 9437184 | tf_op jit(solution)/shard_map/reduce_scatter | solution.py:470
  412.3 3.9 copy-start.6
  672.9 1.6 copy-start.25
  672.9 2.5 copy-start.27
  693.5 278.3 %all-gather.11.cloned.1.call-start = ((), (), s32[]{:S(2)}) async-start(), calls=%async_computation.10 | async-start | bytes 9437184 | tf_op jit(solution)/shard_map/all_gather | solution.py:480
  847.7 466.4 %all-reduce.5.cloned.1.call-start = ((), (), s32[]{:S(2)}) async-start(), calls=%async_computation.12 | async-start | bytes 28835840 | tf_op jit(solution)/shard_map/psum | solution.py:495
  847.8 11.3 copy-start.26
  847.8 11.3 copy-start.28
  971.8 6.2 copy-start.4
  978.0 64.1 %copy-start.2 = (bf16[2048,256]{1,0:T(8,128)(2,1)S(1)}, bf16[2048,256]{1,0:T(8,128)(2,1)}, u32[]{:S(2)}) copy-start(bf16[2048,256]{1,0:T(8,128)(2,1)} %copy-done.1) | copy-start | bytes 3145732
  1042.1 6.9 copy-start.22
  1064.1 402.9 %reduce-scatter.11.cloned.1.call-start = ((), (), s32[]{:S(2)}) async-start(), calls=%async_computation.11 | async-start | bytes 9437184 | tf_op jit(solution)/shard_map/reduce_scatter | solution.py:486
  1080.7 539.4 %reduce-scatter.7.cloned.1.call-start = ((), (), s32[]{:S(2)}) async-start(), calls=%async_computation.7 | async-start | bytes 9437184 | tf_op jit(solution)/shard_map/reduce_scatter | solution.py:454
  1318.4 2.9 copy-start.7
  1318.4 6.3 slice-start
  1321.3 3.3 slice-start.1
  1343.3 123.8 %copy-start.12 = (f32[2048]{0:T(1024)S(1)}, f32[2048]{0:T(1024)}, u32[]{:S(2)}) copy-start(f32[2048]{0:T(1024)} %copy-done.11) | copy-start | bytes 24580
  1343.3 123.8 %copy-start.14 = (f32[256]{0:T(256)S(1)}, f32[256]{0:T(256)}, u32[]{:S(2)}) copy-start(f32[256]{0:T(256)} %copy-done.13) | copy-start | bytes 3076
  1343.3 169.1 %copy-start.16 = (f32[256]{0:T(256)S(1)}, f32[256]{0:T(256)}, u32[]{:S(2)}) copy-start(f32[256]{0:T(256)} %copy-done.15) | copy-start | bytes 3076
Sparse Core Ops, SparseCore 0:
  13.5 127.6 all-gather.4
  256.2 147.1 reduce-scatter.4
  408.5 123.9 all-gather.6
  535.2 123.1 all-gather.8
  693.6 147.1 reduce-scatter.8
  847.9 123.9 all-gather.10
  1064.3 249.8 all-reduce.4
  1317.8 149.2 reduce-scatter.10
  1471.1 148.9 reduce-scatter.6

commit v2 on v1

--- a/solution.py
+++ b/solution.py
@@ -1,8 +1,11 @@
+import functools
+
 import jax
 import jax.numpy as jnp
 from jax import lax
 from jax.experimental import pallas as pl
 from jax.experimental.pallas import tpu as pltpu
+from jax.sharding import Mesh
 from jax.sharding import PartitionSpec as P
 
 GROUPS = 8
@@ -72,11 +75,39 @@
     return total
 
 
-def mixer_forward_body(
-    heads, proj_ref, conv_ref, gain_ref, mixed_ref, wu_ref, fresh_ref, out_ref, state_ref,
-    inverse_ref, rows_buf, state,
-):
+def run_errands(errands, plan, step, late):
+    if not errands:
+        return
+    if not late:
+        pl.when(step == 0)(lambda: greet(True))
+    for at in sorted({entry[0] for entry in plan}):
+
+        @pl.when(step == at)
+        def _(at=at):
+            for when, index, phase in plan:
+                if when == at and (phase == "finish") == late:
+                    getattr(errands[index], phase)()
+
+
+def errand_operands(errands):
+    kinds, sources = [e[0] for e in errands], [e[1] for e in errands]
+    specs = [pl.BlockSpec(memory_space=pl.ANY)] * len(errands)
+    shapes = [errand_target(*errand) for errand in errands]
+    return kinds, sources, specs, shapes, errand_scratch(kinds, sources) if errands else []
+
+
+def mixer_params(errands, collective_id):
+    extra = {"collective_id": collective_id, "has_side_effects": True} if errands else {}
+    return pltpu.CompilerParams(vmem_limit_bytes=48 * 2**20, **extra)
+
+
+def mixer_forward_body(heads, kinds, plan, *refs):
+    first_ref, refs, errands = take_errands(kinds, refs, 3, 6) if kinds else (refs[0], refs[1:], ())
+    proj_ref = first_ref
+    conv_ref, gain_ref, mixed_ref, wu_ref, fresh_ref, out_ref, state_ref, inverse_ref, *refs = refs
+    rows_buf, state = refs
     tile = pl.program_id(1)
+    run_errands(errands, plan, tile, False)
     wide = heads * HEAD_DIM
 
     @pl.when(tile == 0)
@@ -138,9 +169,10 @@
         scale = lax.rsqrt(jnp.mean(out * out, -1, keepdims=True) + 1e-05)
         mixed = out * scale * gain_ref[...] * (gate * sigmoid(gate))
         mixed_ref[:, lo : lo + HEAD_DIM] = mixed.astype(BF16)
-
-
-def mixer_forward(proj, conv, gain, heads):
+    run_errands(errands, plan, tile, True)
+
+
+def mixer_forward(proj, conv, gain, heads, errands=(), plan=(), collective_id=None):
     rows = proj.shape[0]
     wide = heads * HEAD_DIM
     tiles = SEQ_LEN // TILE
@@ -150,13 +182,15 @@
     def at(seq, tile):
         return (seq * tiles + tile, 0)
 
+    kinds, sources, specs, shapes, scratch = errand_operands(errands)
     return pl.pallas_call(
-        lambda *refs: mixer_forward_body(heads, *refs),
+        functools.partial(mixer_forward_body, heads, kinds, plan),
         grid=(seqs, tiles),
         in_specs=[
             pl.BlockSpec((TILE, proj.shape[1]), at),
             pl.BlockSpec(conv.shape, lambda seq, tile: (0, 0)),
             pl.BlockSpec(gain.shape, lambda seq, tile: (0, 0)),
+            *specs,
         ],
         out_specs=[
             pl.BlockSpec((TILE, wide), at),
@@ -165,6 +199,7 @@
             pl.BlockSpec((TILE, wide), at),
             pl.BlockSpec((blocks, heads, HEAD_DIM, HEAD_DIM), lambda s, t: (s * tiles + t, 0, 0, 0)),
             pl.BlockSpec((None, heads, TILE, TILE), lambda s, t: (s * tiles + t, 0, 0, 0)),
+            *specs,
         ],
         out_shape=[
             jax.ShapeDtypeStruct((rows, wide), BF16),
@@ -173,14 +208,16 @@
             jax.ShapeDtypeStruct((rows, wide), F32),
             jax.ShapeDtypeStruct((rows // SPAN, heads, HEAD_DIM, HEAD_DIM), F32),
             jax.ShapeDtypeStruct((rows // TILE, heads, TILE, TILE), F32),
+            *shapes,
         ],
         scratch_shapes=[
             pltpu.VMEM((TILE + 8, 3 * wide), F32),
             pltpu.VMEM((heads, HEAD_DIM, HEAD_DIM), F32),
+            *scratch,
         ],
-        compiler_params=pltpu.CompilerParams(vmem_limit_bytes=48 * 2**20),
+        compiler_params=mixer_params(errands, collective_id),
         name="mixer_forward",
-    )(proj, conv, gain)
+    )(proj, conv, gain, *sources)
 
 
 def unit_back(raw, scale, grad):
@@ -188,12 +225,14 @@
     return scale * grad - raw * (scale * scale * scale * along)
 
 
-def mixer_backward_body(
-    heads, proj_ref, before_ref, conv_ref, gain_ref, grad_ref, wu_ref, fresh_ref, out_ref,
-    state_ref, inverse_ref, raw_grad_ref, conv_grad_ref, gain_grad_ref,
-    rows_buf, grad_buf, state_grad,
-):
+def mixer_backward_body(heads, kinds, plan, *refs):
+    first_ref, refs, errands = take_errands(kinds, refs, 10, 3) if kinds else (refs[0], refs[1:], ())
+    proj_ref = first_ref
+    before_ref, conv_ref, gain_ref, grad_ref, wu_ref, fresh_ref, out_ref, *refs = refs
+    state_ref, inverse_ref, raw_grad_ref, conv_grad_ref, gain_grad_ref, *refs = refs
+    rows_buf, grad_buf, state_grad = refs
     step = pl.program_id(1)
+    run_errands(errands, plan, step, False)
     steps = pl.num_programs(1)
     wide = heads * HEAD_DIM
 
@@ -322,9 +361,13 @@
             here * rows_buf[pl.ds(5 + offset, TILE), :], 0, keepdims=True
         )
     raw_grad_ref[:, : 3 * wide] = total.astype(BF16)
-
-
-def mixer_backward(proj, conv, gain, grad, wu, fresh, out, states, inverses, heads):
+    run_errands(errands, plan, step, True)
+
+
+def mixer_backward(
+    proj, conv, gain, grad, wu, fresh, out, states, inverses, heads,
+    errands=(), plan=(), collective_id=None,
+):
     rows = proj.shape[0]
     wide = heads * HEAD_DIM
     tiles = SEQ_LEN // TILE
@@ -343,8 +386,9 @@
     def fixed(seq, step):
         return (0, 0)
 
+    kinds, sources, specs, shapes, scratch = errand_operands(errands)
     return pl.pallas_call(
-        lambda *refs: mixer_backward_body(heads, *refs),
+        functools.partial(mixer_backward_body, heads, kinds, plan),
         grid=(seqs, tiles),
         in_specs=[
             pl.BlockSpec((TILE, proj.shape[1]), at),
@@ -359,25 +403,1052 @@
                 (blocks, heads, HEAD_DIM, HEAD_DIM), lambda s, t: (index(s, t), 0, 0, 0)
             ),
             pl.BlockSpec((None, heads, TILE, TILE), lambda s, t: (index(s, t), 0, 0, 0)),
+            *specs,
         ],
         out_specs=[
             pl.BlockSpec((TILE, 4 * wide + 128), at),
             pl.BlockSpec((8, 3 * wide), fixed),
             pl.BlockSpec((8, HEAD_DIM), fixed),
+            *specs,
         ],
         out_shape=[
             jax.ShapeDtypeStruct((rows, 4 * wide + 128), BF16),
             jax.ShapeDtypeStruct((8, 3 * wide), F32),
             jax.ShapeDtypeStruct((8, HEAD_DIM), F32),
+            *shapes,
         ],
         scratch_shapes=[
             pltpu.VMEM((TILE + 8, 3 * wide), F32),
             pltpu.VMEM((TILE + 8, 3 * wide), F32),
             pltpu.VMEM((heads, HEAD_DIM, HEAD_DIM), F32),
+            *scratch,
         ],
-        compiler_params=pltpu.CompilerParams(vmem_limit_bytes=48 * 2**20),
+        compiler_params=mixer_params(errands, collective_id),
         name="mixer_backward",
-    )(proj, proj, conv, gain, grad, wu, fresh, out, states, inverses)
+    )(proj, proj, conv, gain, grad, wu, fresh, out, states, inverses, *sources)
+
+
+MESH = pl.DeviceIdType.MESH
+
+
+def place():
+    return lax.axis_index("core"), lax.axis_index("zl"), lax.axis_index("x")
+
+
+def slot_of(core, deep, wide):
+    own_core, own_deep, own_wide = place()
+    return (
+        jnp.where(core, 1 - own_core, own_core) * 4
+        + jnp.where(deep, 1 - own_deep, own_deep) * 2
+        + jnp.where(wide, 1 - own_wide, own_wide)
+    )
+
+
+def is_moved():
+    return lax.axis_index("core") != lax.axis_index("zh")
+
+
+def greet(everyone=False):
+    barrier = pltpu.get_barrier_semaphore()
+    axes = ("core", "zl", "x", "y", "zh") if everyone else ("core", "zl", "x")
+    for axis in axes:
+        pl.semaphore_signal(barrier, inc=1, device_id=neighbour(axis), device_id_type=MESH)
+    peers = len(axes)
+    if everyone:
+        pl.when(is_moved())(
+            lambda: pl.semaphore_signal(
+                barrier, inc=1, device_id=partner(), device_id_type=MESH
+            )
+        )
+        peers = peers + is_moved().astype(jnp.int32)
+    pl.semaphore_wait(barrier, peers)
+
+
+def partner():
+    return {"core": lax.axis_index("zh"), "zh": lax.axis_index("core")}
+
+
+def row_half(ref, index):
+    rows = ref.shape[0] // 2
+    return ref.at[pl.ds(pl.multiple_of(index * rows, 16), rows)]
+
+
+class Errand:
+    sems = 1
+    staged = True
+
+    def __init__(self, source, target, send, recv, local, stage=None):
+        self.source, self.target, self.stage = source, target, stage
+        self.send, self.recv, self.local = send, recv, local
+        self.y = lax.axis_index("y")
+
+    def remote(self, index, source, target, device):
+        return pltpu.make_async_remote_copy(
+            src_ref=source, dst_ref=target, send_sem=self.send.at[index],
+            recv_sem=self.recv.at[index], device_id=device, device_id_type=MESH,
+        )
+
+    def stays(self, action):
+        pl.when(jnp.logical_not(is_moved()))(action)
+
+    def own_target(self):
+        return self.target
+
+    def here(self):
+        source = self.source if self.stage is None else self.stage
+        return pltpu.make_async_copy(source, self.own_target(), self.local)
+
+    def stage_in(self):
+        return pltpu.make_async_copy(self.source, self.stage, self.local)
+
+    def start_here(self):
+        self.stays(lambda: (self.here() if self.stage is None else self.stage_in()).start())
+
+    def pass_here(self):
+        def action():
+            self.stage_in().wait()
+            self.here().start()
+
+        if self.stage is not None:
+            self.stays(action)
+
+    def finish_here(self):
+        self.stays(lambda: self.here().wait())
+
+
+class Exchange(Errand):
+    def far(self):
+        return self.remote(0, self.source, self.target, partner())
+
+    def start(self):
+        pl.when(is_moved())(lambda: self.far().start())
+        self.start_here()
+
+    def middle(self):
+        self.pass_here()
+
+    def finish(self):
+        pl.when(is_moved())(lambda: self.far().wait())
+        self.finish_here()
+
+
+class Swap(Errand):
+    sems = 2
+
+    def first(self):
+        mine = row_half(self.target, self.y)
+        return self.remote(0, row_half(self.source, self.y), mine, partner())
+
+    def second(self, landing=False):
+        half = row_half(self.target, 1 - self.y if landing else self.y)
+        return self.remote(1, half, half, neighbour("y"))
+
+    def start(self):
+        pl.when(is_moved())(lambda: self.first().start())
+        self.start_here()
+
+    def middle(self):
+        @pl.when(is_moved())
+        def _():
+            self.first().wait_recv()
+            self.second().start()
+
+        self.pass_here()
+
+    def finish(self):
+        @pl.when(is_moved())
+        def _():
+            self.first().wait_send()
+            self.second().wait_send()
+            self.second(True).wait_recv()
+
+        self.finish_here()
+
+
+class HalfOverY(Errand):
+    staged = False
+
+    def copy(self):
+        return self.remote(0, row_half(self.source, 1 - self.y), self.target, neighbour("y"))
+
+    def start(self):
+        self.copy().start()
+
+    def middle(self):
+        pass
+
+    def finish(self):
+        self.copy().wait()
+
+
+class Across(Errand):
+    staged = False
+
+    def copy(self):
+        return self.remote(0, self.source, self.target, neighbour("zh"))
+
+    def start(self):
+        pl.when(is_moved())(lambda: self.copy().start())
+
+    def middle(self):
+        pass
+
+    def finish(self):
+        pl.when(is_moved())(lambda: self.copy().wait_send())
+        self.stays(lambda: self.copy().wait_recv())
+
+
+class ExchangeGather(Errand):
+    sems = 12
+
+    def moves(self):
+        own = slot_of(0, 0, 0)
+        wide, deep, far = slot_of(0, 0, 1), slot_of(0, 1, 0), slot_of(0, 1, 1)
+        rows = self.source.shape[0]
+        half = rows // 2
+        return {
+            0: ("x", own, wide, 0, half), 1: ("zl", own, deep, half, half),
+            2: ("x", own, wide, half, half), 3: ("zl", own, deep, 0, half),
+            4: ("core", own, slot_of(1, 0, 0), 0, rows),
+            5: ("zl", wide, far, 0, half), 6: ("x", deep, far, half, half),
+            7: ("core", wide, slot_of(1, 0, 1), 0, rows),
+            8: ("core", deep, slot_of(1, 1, 0), 0, rows),
+            9: ("core", far, slot_of(1, 1, 1), 0, half),
+            10: ("core", far, slot_of(1, 1, 1), half, half),
+        }
+
+    def move(self, index, landing=False):
+        axis, source, target, start, size = self.moves()[index]
+        view = self.target.at[target if landing else source, pl.ds(start, size)]
+        return self.remote(index, view, view, neighbour(axis))
+
+    def launch(self, *indices):
+        for index in indices:
+            self.move(index).start()
+
+    def arrived(self, *indices):
+        for index in indices:
+            self.move(index, True).wait_recv()
+
+    def own_target(self):
+        return self.target.at[slot_of(0, 0, 0)]
+
+    def far(self, landing=False):
+        there = slot_of(0, 0, 0)
+        if not landing:
+            there = there + (lax.axis_index("zh") - lax.axis_index("core")) * 4
+        return self.remote(11, self.source, self.target.at[there], partner())
+
+    def start(self):
+        pl.when(is_moved())(lambda: self.far().start())
+        self.start_here()
+
+    def settle(self):
+        self.pass_here()
+
+    def spread(self):
+        pl.when(is_moved())(lambda: self.far(True).wait_recv())
+        self.finish_here()
+        self.launch(0, 1, 2, 3, 4)
+
+    def middle(self):
+        self.arrived(0)
+        self.launch(5)
+        self.arrived(1)
+        self.launch(6)
+        self.arrived(2)
+        self.launch(7)
+        self.arrived(3)
+        self.launch(8)
+
+    def late(self):
+        self.arrived(5)
+        self.launch(9)
+        self.arrived(6)
+        self.launch(10)
+
+    def finish(self):
+        self.arrived(4, 7, 8, 9, 10)
+        pl.when(is_moved())(lambda: self.far().wait_send())
+        for index in range(11):
+            self.move(index).wait_send()
+
+
+class Spread(Errand):
+    sems = 3
+
+    def own_target(self):
+        return row_half(self.target, self.y)
+
+    def over(self):
+        return self.remote(0, self.source, self.own_target(), neighbour("y"))
+
+    def other(self, index, axis):
+        view = row_half(self.target, 1 - self.y)
+        return self.remote(index, view, view, neighbour(axis))
+
+    def cross(self):
+        return self.remote(1, self.source, self.own_target(), neighbour("core"))
+
+    def start(self):
+        @pl.when(jnp.logical_not(is_moved()))
+        def _():
+            self.over().start()
+            self.cross().start()
+
+        self.start_here()
+
+    def middle(self):
+        @pl.when(jnp.logical_not(is_moved()))
+        def _():
+            self.other(0, "y").wait_recv()
+            self.other(2, "core").start()
+
+        self.pass_here()
+
+    def finish(self):
+        @pl.when(jnp.logical_not(is_moved()))
+        def _():
+            self.over().wait_send()
+            self.cross().wait_send()
+            self.other(2, "core").wait_send()
+
+        @pl.when(is_moved())
+        def _():
+            self.cross().wait_recv()
+            self.other(2, "core").wait_recv()
+
+        self.finish_here()
+
+
+def errand_target(kind, source):
+    if kind is ExchangeGather:
+        return jax.ShapeDtypeStruct((8, *source.shape), source.dtype)
+    rows = source.shape[0]
+    rows = {HalfOverY: rows // 2, Spread: 2 * rows}.get(kind, rows)
+    return jax.ShapeDtypeStruct((rows, *source.shape[1:]), source.dtype)
+
+
+def errand_scratch(kinds, sources=()):
+    total = max(1, sum(kind.sems for kind in kinds))
+    stages = [
+        pltpu.VMEM(source.shape if kind.staged else (16, 128), BF16)
+        for kind, source in zip(kinds, sources)
+    ]
+    return [
+        *stages,
+        pltpu.SemaphoreType.DMA((total,)),
+        pltpu.SemaphoreType.DMA((total,)),
+        pltpu.SemaphoreType.DMA((max(1, len(kinds)),)),
+    ]
+
+
+def make_errands(kinds, sources, targets, send, recv, local, stages=None):
+    made, at = [], 0
+    for index, (kind, source, target) in enumerate(zip(kinds, sources, targets)):
+        view = pl.ds(at, kind.sems)
+        stage = stages[index] if stages and kind.staged else None
+        made.append(kind(source, target, send.at[view], recv.at[view], local.at[index], stage))
+        at += kind.sems
+    return made
+
+
+def neighbour(axis):
+    return {axis: 1 - lax.axis_index(axis)}
+
+
+def column_tile(columns):
+    for size in (512, 384, 256, 128):
+        if columns % size == 0:
+            return size
+    return columns
+
+
+def column_parts(columns):
+    tile = column_tile(columns)
+    if tile != columns or columns <= 512:
+        return [(0, tile, columns // tile)]
+    whole = columns // 256 * 256
+    return [(0, 256, whole // 256), (whole, columns - whole, 1)]
+
+
+def by_columns(columns, body):
+    for start, size, steps in column_parts(columns):
+        if steps == 1:
+            body(pl.ds(start, size))
+        else:
+
+            def column(step, _, start=start, size=size):
+                body(pl.ds(pl.multiple_of(start + step * size, 128), size))
+                return 0
+
+            lax.fori_loop(0, steps, column, 0)
+
+
+def take_errands(kinds, refs, inputs, outputs):
+    extra = len(kinds)
+    sources = refs[inputs : inputs + extra]
+    targets = refs[inputs + extra + outputs : inputs + 2 * extra + outputs]
+    errands = make_errands(kinds, sources, targets, *refs[-3:], refs[-3 - extra : -3])
+    rest = (
+        *refs[:inputs], *refs[inputs + extra : inputs + extra + outputs],
+        *refs[inputs + 2 * extra + outputs : -3 - extra],
+    )
+    return rest[0], rest[1:], errands
+
+
+def gather_body(dims, count, kinds, block_ref, *refs):
+    block_ref, refs, errands = take_errands(kinds, (block_ref, *refs), 1 + count, 1 + count)
+    weight_refs, gathered_ref, product_refs = refs[:count], refs[count], refs[count + 1 : 2 * count + 1]
+    held = refs[2 * count + 1]
+    weights, results = refs[2 * count + 2 : 3 * count + 2], refs[3 * count + 2 : 4 * count + 2]
+    send, recv, local = refs[4 * count + 2 :]
+    rows = block_ref.shape[0]
+    half = rows // 2
+    own = slot_of(0, 0, 0)
+    load_own = pltpu.make_async_copy(block_ref, held.at[own], local.at[0])
+    load_own.start()
+    loads = [
+        pltpu.make_async_copy(ref, weight, local.at[1 + i])
+        for i, (ref, weight) in enumerate(zip(weight_refs, weights))
+    ]
+    for load in loads:
+        load.start()
+    greet(bool(kinds))
+    load_own.wait()
+
+    def move(index, axis, slot, start, size):
+        view = held.at[slot, pl.ds(start, size)]
+        return pltpu.make_async_remote_copy(
+            src_ref=view, dst_ref=view, send_sem=send.at[index], recv_sem=recv.at[index],
+            device_id=neighbour(axis), device_id_type=MESH,
+        )
+
+    def arrived(index, axis, slot, start, size):
+        move(index, axis, slot, start, size).wait_recv()
+
+    wide_slot, deep_slot, far_slot = slot_of(0, 0, 1), slot_of(0, 1, 0), slot_of(0, 1, 1)
+    sends = []
+
+    def launch(*args):
+        copy = move(*args)
+        copy.start()
+        sends.append(copy)
+
+    launch(0, "x", own, 0, half)
+    launch(1, "zl", own, half, half)
+    launch(2, "x", own, half, half)
+    launch(3, "zl", own, 0, half)
+    launch(4, "core", own, 0, rows)
+    for errand in errands:
+        errand.start()
+
+    stores = []
+
+    def store(ref, out, slot):
+        copy = pltpu.make_async_copy(ref.at[slot], out.at[slot], local.at[1 + count + len(stores)])
+        copy.start()
+        stores.append(copy)
+
+    def multiply(slot):
+        store(held, gathered_ref, slot)
+        for weight, result, product_ref in zip(weights, results, product_refs):
+
+            def column(at):
+                right = weight[:, at] if dims == NN else weight[at, :]
+                result[slot, :, at] = dot(held[slot], right, dims).astype(result.dtype)
+
+            by_columns(result.shape[2], column)
+            store(result, product_ref, slot)
+
+    for load in loads:
+        load.wait()
+    multiply(own)
+    arrived(0, "x", wide_slot, 0, half)
+    launch(5, "zl", wide_slot, 0, half)
+    arrived(1, "zl", deep_slot, half, half)
+    launch(6, "x", deep_slot, half, half)
+    other = slot_of(1, 0, 0)
+    arrived(4, "core", other, 0, rows)
+    multiply(other)
+    arrived(2, "x", wide_slot, half, half)
+    launch(7, "core", wide_slot, 0, rows)
+    arrived(3, "zl", deep_slot, 0, half)
+    launch(8, "core", deep_slot, 0, rows)
+    multiply(wide_slot)
+    multiply(deep_slot)
+    other_wide, other_deep, other_far = slot_of(1, 0, 1), slot_of(1, 1, 0), slot_of(1, 1, 1)
+    arrived(7, "core", other_wide, 0, rows)
+    multiply(other_wide)
+    arrived(8, "core", other_deep, 0, rows)
+    multiply(other_deep)
+    for errand in errands:
+        errand.middle()
+    arrived(5, "zl", far_slot, 0, half)
+    launch(9, "core", far_slot, 0, half)
+    arrived(6, "x", far_slot, half, half)
+    launch(10, "core", far_slot, half, half)
+    multiply(far_slot)
+    arrived(9, "core", other_far, 0, half)
+    arrived(10, "core", other_far, half, half)
+    multiply(other_far)
+    for copy in sends:
+        copy.wait_send()
+    for copy in stores:
+        copy.wait()
+    for errand in errands:
+        errand.finish()
+
+
+def gather_multiply(block, weights, dims, collective_id, name, errands=(), out_type=F32):
+    rows, depth = block.shape
+    widths = [w.shape[1] if dims == NN else w.shape[0] for w in weights]
+    count = len(weights)
+    kinds, sources = [e[0] for e in errands], [e[1] for e in errands]
+    gathered, *products = pl.pallas_call(
+        functools.partial(gather_body, dims, count, kinds),
+        in_specs=[pl.BlockSpec(memory_space=pl.ANY)] * (1 + count + len(kinds)),
+        out_specs=[pl.BlockSpec(memory_space=pl.ANY)] * (1 + count + len(kinds)),
+        out_shape=[jax.ShapeDtypeStruct((8, rows, depth), BF16)]
+        + [jax.ShapeDtypeStruct((8, rows, width), out_type) for width in widths]
+        + [errand_target(*errand) for errand in errands],
+        scratch_shapes=[pltpu.VMEM((8, rows, depth), BF16)]
+        + [pltpu.VMEM(w.shape, BF16) for w in weights]
+        + [pltpu.VMEM((8, rows, width), out_type) for width in widths]
+        + [
+            pltpu.SemaphoreType.DMA((11,)),
+            pltpu.SemaphoreType.DMA((11,)),
+            pltpu.SemaphoreType.DMA((1 + count + 8 * (1 + count),)),
+            *errand_scratch(kinds, sources),
+        ],
+        compiler_params=pltpu.CompilerParams(
+            collective_id=collective_id, has_side_effects=True, vmem_limit_bytes=56 * 2**20
+        ),
+        name=name,
+    )(block, *weights, *sources)
+    flat = [v.reshape(8 * rows, v.shape[2]) for v in (gathered, *products[:count])]
+    return (*flat, *products[count:])
+
+
+def scatter_core(dims, lefts, weights, buffers, beside):
+    sending, crossing, partial, far_recv, side_recv, total, send, recv = buffers
+    rows, width = total.shape
+    half = rows // 2
+
+    def move(index, axis, src, dst):
+        return pltpu.make_async_remote_copy(
+            src_ref=src, dst_ref=dst, send_sem=send.at[index], recv_sem=recv.at[index],
+            device_id=neighbour(axis), device_id_type=MESH,
+        )
+
+    sends = []
+
+    def launch(*args):
+        copy = move(*args)
+        copy.start()
+        sends.append(copy)
+
+    def multiply(slot, write):
+        def column(at):
+            value = None
+            for left, weight in zip(lefts, weights):
+                right = weight[:, at] if dims == NN else weight[at, :]
+                term = dot(left[slot], right, dims)
+                value = term if value is None else value + term
+            write(at, value)
+
+        by_columns(width, column)
+
+    places = ((1, 1), (0, 1), (1, 0), (0, 0))
+
+    def cross(index):
+        def write(at, value):
+            sending[index, :, at] = value.astype(BF16)
+
+        multiply(slot_of(1, *places[index]), write)
+        launch(index, "core", sending.at[index], crossing.at[index])
+
+    def crossed(index):
+        move(index, "core", sending.at[index], crossing.at[index]).wait_recv()
+
+    def local_sum(index):
+        crossed(index)
+
+        def write(at, value):
+            partial[index, :, at] = (value + crossing[index, :, at].astype(F32)).astype(BF16)
+
+        multiply(slot_of(0, *places[index]), write)
+
+    first, second = pl.ds(0, half), pl.ds(half, half)
+    cross(0)
+    beside(0)
+    cross(1)
+    local_sum(0)
+    launch(4, "x", partial.at[0, first], far_recv.at[0])
+    launch(5, "zl", partial.at[0, second], far_recv.at[1])
+    cross(2)
+    local_sum(1)
+    launch(6, "x", partial.at[1, first], side_recv.at[0, first])
+    local_sum(2)
+    launch(7, "zl", partial.at[2, second], side_recv.at[1, second])
+    cross(3)
+    beside(1)
+    move(4, "x", partial.at[0, first], far_recv.at[0]).wait_recv()
+    partial[2, first] = (partial[2, first].astype(F32) + far_recv[0].astype(F32)).astype(BF16)
+    launch(8, "zl", partial.at[2, first], side_recv.at[1, first])
+    move(5, "zl", partial.at[0, second], far_recv.at[1]).wait_recv()
+    partial[1, second] = (partial[1, second].astype(F32) + far_recv[1].astype(F32)).astype(BF16)
+    launch(9, "x", partial.at[1, second], side_recv.at[0, second])
+    beside(2)
+    crossed(3)
+
+    def write(at, value):
+        total[:, at] = value + crossing[3, :, at].astype(F32)
+
+    multiply(slot_of(0, 0, 0), write)
+    move(6, "x", partial.at[1, first], side_recv.at[0, first]).wait_recv()
+    total[first] += side_recv[0, first].astype(F32)
+    move(7, "zl", partial.at[2, second], side_recv.at[1, second]).wait_recv()
+    total[second] += side_recv[1, second].astype(F32)
+    beside(3)
+    move(8, "zl", partial.at[2, first], side_recv.at[1, first]).wait_recv()
+    total[first] += side_recv[1, first].astype(F32)
+    move(9, "x", partial.at[1, second], side_recv.at[0, second]).wait_recv()
+    total[second] += side_recv[0, second].astype(F32)
+    return sends
+
+
+def scatter_scratch(rows, width):
+    return [
+        pltpu.VMEM((4, rows, width), BF16),
+        pltpu.VMEM((4, rows, width), BF16),
+        pltpu.VMEM((3, rows, width), BF16),
+        pltpu.VMEM((2, rows // 2, width), BF16),
+        pltpu.VMEM((2, rows, width), BF16),
+        pltpu.VMEM((rows, width), F32),
+        pltpu.SemaphoreType.DMA((10,)),
+        pltpu.SemaphoreType.DMA((10,)),
+    ]
+
+
+def scatter_body(dims, count, kinds, *refs):
+    first_ref, refs, errands = take_errands(kinds, refs, 2 * count, 1)
+    refs = (first_ref, *refs)
+    total_ref = refs[2 * count]
+    operands = refs[2 * count + 1 : 4 * count + 1]
+    buffers, local = refs[4 * count + 1 : -1], refs[-1]
+    loads = [
+        pltpu.make_async_copy(ref, operand, local.at[i])
+        for i, (ref, operand) in enumerate(zip(refs[: 2 * count], operands))
+    ]
+    for load in loads:
+        load.start()
+    greet(bool(kinds))
+    for load in loads:
+        load.wait()
+
+    def beside(point):
+        for errand in errands:
+            if point == 0:
+                errand.start()
+            elif point == 3:
+                errand.middle()
+
+    sends = scatter_core(dims, operands[:count], operands[count:], buffers, beside)
+    store = pltpu.make_async_copy(buffers[5], total_ref, local.at[2 * count])
+    store.start()
+    for copy in sends:
+        copy.wait_send()
+    store.wait()
+    for errand in errands:
+        errand.finish()
+
+
+def multiply_scatter(lefts, weights, dims, collective_id, name, errands=()):
+    rows = lefts[0].shape[0] // 8
+    width = weights[0].shape[1] if dims == NN else weights[0].shape[0]
+    count = len(lefts)
+    lefts = [left.reshape(8, rows, left.shape[1]) for left in lefts]
+    kinds, sources = [e[0] for e in errands], [e[1] for e in errands]
+    return pl.pallas_call(
+        functools.partial(scatter_body, dims, count, kinds),
+        in_specs=[pl.BlockSpec(memory_space=pl.ANY)] * (2 * count + len(kinds)),
+        out_specs=[pl.BlockSpec(memory_space=pl.ANY)] * (1 + len(kinds)),
+        out_shape=[jax.ShapeDtypeStruct((rows, width), F32)]
+        + [errand_target(*errand) for errand in errands],
+        scratch_shapes=[pltpu.VMEM(v.shape, BF16) for v in (*lefts, *weights)]
+        + [
+            *scatter_scratch(rows, width),
+            pltpu.SemaphoreType.DMA((2 * count + 1,)),
+            *errand_scratch(kinds, sources),
+        ],
+        compiler_params=pltpu.CompilerParams(
+            collective_id=collective_id, has_side_effects=True, vmem_limit_bytes=56 * 2**20
+        ),
+        name=name,
+    )(*lefts, *weights, *sources)
+
+
+def begin_body(
+    tokens_ref, gain_ref, conv_ref, *refs,
+):
+    weight_refs, refs = refs[:5], refs[5:]
+    moved_ref, gathered_ref, product_ref, weights_ref, new_conv_ref, *refs = refs
+    tokens, held, weights, result, send, recv, errand_send, errand_recv, local = refs
+    rows = tokens_ref.shape[0]
+    half = rows // 2
+    starts = [0]
+    for ref in weight_refs:
+        starts.append(starts[-1] + ref.shape[1])
+    parts = [pl.ds(start, ref.shape[1]) for start, ref in zip(starts, weight_refs)]
+    greet(True)
+    kinds = [Exchange, Exchange] + [Swap] * 5
+    targets = [tokens, new_conv_ref] + [weights.at[:, part] for part in parts]
+    block, taps, *swaps = make_errands(
+        kinds, [tokens_ref, conv_ref, *weight_refs], targets, errand_send, errand_recv, local
+    )
+    block.start()
+    taps.start()
+    swaps[0].start()
+    block.finish()
+    for swap in swaps[1:]:
+        swap.start()
+    own = slot_of(0, 0, 0)
+    values = tokens[...].astype(F32)
+    scale = lax.rsqrt(jnp.mean(values * values, -1, keepdims=True) + 1e-05)
+    held[own] = (values * scale * gain_ref[...]).astype(BF16)
+    keep = pltpu.make_async_copy(tokens, moved_ref, local.at[7])
+    keep.start()
+
+    def move(index, axis, slot, start, size):
+        view = held.at[slot, pl.ds(start, size)]
+        return pltpu.make_async_remote_copy(
+            src_ref=view, dst_ref=view, send_sem=send.at[index], recv_sem=recv.at[index],
+            device_id=neighbour(axis), device_id_type=MESH,
+        )
+
+    def arrived(*args):
+        move(*args).wait_recv()
+
+    wide_slot, deep_slot, far_slot = slot_of(0, 0, 1), slot_of(0, 1, 0), slot_of(0, 1, 1)
+    sends = []
+
+    def launch(*args):
+        copy = move(*args)
+        copy.start()
+        sends.append(copy)
+
+    launch(0, "x", own, 0, half)
+    launch(1, "zl", own, half, half)
+    launch(2, "x", own, half, half)
+    launch(3, "zl", own, 0, half)
+    launch(4, "core", own, 0, rows)
+    arrived(0, "x", wide_slot, 0, half)
+    launch(5, "zl", wide_slot, 0, half)
+    arrived(1, "zl", deep_slot, half, half)
+    launch(6, "x", deep_slot, half, half)
+    swaps[0].middle()
+    arrived(2, "x", wide_slot, half, half)
+    launch(7, "core", wide_slot, 0, rows)
+    arrived(3, "zl", deep_slot, 0, half)
+    launch(8, "core", deep_slot, 0, rows)
+    swaps[1].middle()
+    arrived(5, "zl", far_slot, 0, half)
+    launch(9, "core", far_slot, 0, half)
+    arrived(6, "x", far_slot, half, half)
+    launch(10, "core", far_slot, half, half)
+    arrived(4, "core", slot_of(1, 0, 0), 0, rows)
+    arrived(7, "core", slot_of(1, 0, 1), 0, rows)
+    arrived(8, "core", slot_of(1, 1, 0), 0, rows)
+    arrived(9, "core", slot_of(1, 1, 1), 0, half)
+    arrived(10, "core", slot_of(1, 1, 1), half, half)
+    store = pltpu.make_async_copy(held, gathered_ref, local.at[8])
+    store.start()
+    stores = []
+    for index, (swap, part) in enumerate(zip(swaps, parts)):
+        if index + 2 < len(swaps):
+            swaps[index + 2].middle()
+        swap.finish()
+
+        def multiply(slot, _, part=part):
+            result[slot, :, part] = dot(held[slot], weights[:, part], NN)
+            return 0
+
+        lax.fori_loop(0, 8, multiply, 0)
+        for view, out, sem in (
+            (result.at[:, :, part], product_ref.at[:, :, part], 9 + 2 * index),
+            (weights.at[:, part], weights_ref.at[:, part], 10 + 2 * index),
+        ):
+            copy = pltpu.make_async_copy(view, out, local.at[sem])
+            copy.start()
+            stores.append(copy)
+    taps.finish()
+    for copy in sends:
+        copy.wait_send()
+    keep.wait()
+    store.wait()
+    for copy in stores:
+        copy.wait()
+
+
+def begin(tokens, gain, conv, weights, collective_id):
+    rows, depth = tokens.shape
+    width = sum(w.shape[1] for w in weights)
+    hbm = pl.BlockSpec(memory_space=pl.ANY)
+    moved, gathered, product, weights, conv = pl.pallas_call(
+        begin_body,
+        in_specs=[hbm, pl.BlockSpec(memory_space=pltpu.VMEM)] + [hbm] * (1 + len(weights)),
+        out_specs=[hbm] * 5,
+        out_shape=[
+            jax.ShapeDtypeStruct(tokens.shape, BF16),
+            jax.ShapeDtypeStruct((8, rows, depth), BF16),
+            jax.ShapeDtypeStruct((8, rows, width), F32),
+            jax.ShapeDtypeStruct((depth, width), BF16),
+            jax.ShapeDtypeStruct(conv.shape, conv.dtype),
+        ],
+        scratch_shapes=[
+            pltpu.VMEM((rows, depth), BF16),
+            pltpu.VMEM((8, rows, depth), BF16),
+            pltpu.VMEM((depth, width), BF16),
+            pltpu.VMEM((8, rows, width), F32),
+            pltpu.SemaphoreType.DMA((11,)),
+            pltpu.SemaphoreType.DMA((11,)),
+            pltpu.SemaphoreType.DMA((12,)),
+            pltpu.SemaphoreType.DMA((12,)),
+            pltpu.SemaphoreType.DMA((19,)),
+        ],
+        compiler_params=pltpu.CompilerParams(
+            collective_id=collective_id, has_side_effects=True, vmem_limit_bytes=56 * 2**20
+        ),
+        name="begin",
+    )(tokens, gain, conv, *weights)
+    return moved, gathered.reshape(8 * rows, depth), product.reshape(8 * rows, width), weights, conv
+
+
+CHUNKS = 4
+
+
+def finish_body(kinds, *refs):
+    first_ref, refs, errands = take_errands(kinds, refs, 7, 3)
+    left_ref, weight_ref, grad_ref, tokens_ref, resid_ref, gain_ref, small_ref = first_ref, *refs[:6]
+    tokens_grad_ref, total_grad_ref, small_out_ref, *refs = refs[6:]
+    left, weight, mine, came, far, tokens, resid, moving, small, small_recv = refs[:10]
+    buffers, refs = refs[10:18], refs[18:]
+    chain_send, chain_recv, small_send, small_recv_sem, move_send, move_recv, local = refs
+    loads = [
+        pltpu.make_async_copy(source, target, local.at[i])
+        for i, (source, target) in enumerate(
+            (
+                (left_ref, left), (weight_ref, weight), (tokens_ref, tokens), (resid_ref, resid),
+                (small_ref, small), (row_half(grad_ref, lax.axis_index("y")), mine),
+            )
+        )
+    ]
+    for load in loads:
+        load.start()
+    greet(True)
+    y = lax.axis_index("y")
+    moved = is_moved()
+    stays = jnp.logical_not(moved)
+    size = mine.shape[0] // CHUNKS
+
+    def chain(stage, index, source, target, axis):
+        return pltpu.make_async_remote_copy(
+            src_ref=source, dst_ref=target, send_sem=chain_send.at[stage, index],
+            recv_sem=chain_recv.at[stage, index], device_id=neighbour(axis), device_id_type=MESH,
+        )
+
+    def rows_in(ref, index, other=False):
+        owner = 1 - y if other else y
+        start = owner * (size * CHUNKS) + index * size
+        return ref.at[pl.ds(pl.multiple_of(start, 16), size)]
+
+    def chunk(ref, index):
+        return ref.at[pl.ds(index * size, size)]
+
+    def over(index):
+        return chain(0, index, rows_in(grad_ref, index, True), chunk(came, index), "y")
+
+    def across(index):
+        return chain(1, index, chunk(mine, index), chunk(far, index), "zh")
+
+    def back(index):
+        return chain(2, index, chunk(mine, index), rows_in(total_grad_ref, index), "y")
+
+    def landing(index):
+        view = rows_in(total_grad_ref, index, True)
+        return chain(2, index, view, view, "y")
+
+    def cross(index):
+        return chain(3, index, chunk(mine, index), rows_in(total_grad_ref, index), "core")
+
+    def pass_on(index):
+        view = rows_in(total_grad_ref, index, True)
+        return chain(4, index, view, view, "core")
+
+    def near(index):
+        return pltpu.make_async_copy(
+            chunk(mine, index), rows_in(total_grad_ref, index), local.at[6 + index]
+        )
+
+    def add(index, other):
+        at = pl.ds(index * size, size)
+        mine[at] = (mine[at].astype(F32) + other[at].astype(F32)).astype(BF16)
+
+    def sum_y(index):
+        over(index).wait_recv()
+        add(index, came)
+        pl.when(moved)(across(index).start)
+
+    def sum_z(index):
+        @pl.when(stays)
+        def _():
+            across(index).wait_recv()
+            add(index, far)
+            back(index).start()
+            cross(index).start()
+            near(index).start()
+
+    def forward(index):
+        @pl.when(stays)
+        def _():
+            landing(index).wait_recv()
+            pass_on(index).start()
+
+    for index in range(CHUNKS):
+        over(index).start()
+    for load in loads:
+        load.wait()
+
+    def beside(point):
+        if point == 0:
+            for errand in errands:
+                errand.start()
+            sum_y(0)
+        elif point == 1:
+            sum_y(1)
+        elif point == 2:
+            sum_z(0)
+            sum_y(2)
+        elif point == 3:
+            for errand in errands:
+                errand.middle()
+            sum_z(1)
+
+    sends = scatter_core(NT, [left], [weight], buffers, beside)
+    total = buffers[5]
+    gain = gain_ref[...]
+
+    def backward(step, along):
+        at = pl.ds(pl.multiple_of(step * 32, 32), 32)
+        values = tokens[at].astype(F32)
+        scale = lax.rsqrt(jnp.mean(values * values, -1, keepdims=True) + 1e-05)
+        grad = total[at]
+        scaled = grad * gain
+        mean = jnp.mean(values * scaled, -1, keepdims=True)
+        change = scale * scaled - values * (scale * scale * scale * mean)
+        moving[at] = (resid[at] + change).astype(BF16)
+        return along + jnp.sum(grad * values * scale, 0, keepdims=True)
+
+    along = lax.fori_loop(
+        0, total.shape[0] // 32, backward, jnp.zeros((1, total.shape[1]), F32)
+    )
+    small[0:1, :] = along
+    move = make_errands([Exchange], [moving], [tokens_grad_ref], move_send, move_recv, local.at[pl.ds(6 + CHUNKS, 1)])[0]
+    move.start()
+    sum_y(3)
+    axes = ("core", "x", "zl", "y", "zh")
+
+    def small_round(index):
+        copy = pltpu.make_async_remote_copy(
+            src_ref=small, dst_ref=small_recv.at[index], send_sem=small_send.at[index],
+            recv_sem=small_recv_sem.at[index], device_id=neighbour(axes[index]),
+            device_id_type=MESH,
+        )
+        copy.start()
+        copy.wait()
+        small[...] += small_recv[index]
+
+    small_round(0)
+    small_round(1)
+    small_round(2)
+    sum_z(2)
+    forward(0)
+    small_round(3)
+    small_round(4)
+    small_store = pltpu.make_async_copy(small, small_out_ref, local.at[7 + CHUNKS])
+    small_store.start()
+    forward(1)
+    sum_z(3)
+    forward(2)
+    forward(3)
+    for copy in sends:
+        copy.wait_send()
+    for index in range(CHUNKS):
+        over(index).wait_send()
+
+        @pl.when(moved)
+        def _(index=index):
+            across(index).wait_send()
+            cross(index).wait_recv()
+            pass_on(index).wait_recv()
+
+        @pl.when(stays)
+        def _(index=index):
+            back(index).wait_send()
+            cross(index).wait_send()
+            pass_on(index).wait_send()
+            near(index).wait()
+
+    for errand in errands:
+        errand.finish()
+    move.finish()
+    small_store.wait()
+
+
+def finish(left, weight, weight_grad, tokens, resid_grad, gain, small, collective_id, errands=()):
+    rows, width = tokens.shape
+    left = left.reshape(8, rows, left.shape[1])
+    kinds, sources = [e[0] for e in errands], [e[1] for e in errands]
+    hbm = pl.BlockSpec(memory_space=pl.ANY)
+    depth, columns = weight_grad.shape
+    half = pltpu.VMEM((depth // 2, columns), BF16)
+    return pl.pallas_call(
+        functools.partial(finish_body, kinds),
+        in_specs=[hbm] * 5 + [pl.BlockSpec(memory_space=pltpu.VMEM), hbm] + [hbm] * len(kinds),
+        out_specs=[hbm] * (3 + len(kinds)),
+        out_shape=[
+            jax.ShapeDtypeStruct(tokens.shape, BF16),
+            jax.ShapeDtypeStruct(weight_grad.shape, BF16),
+            jax.ShapeDtypeStruct(small.shape, F32),
+            *[errand_target(*errand) for errand in errands],
+        ],
+        scratch_shapes=[
+            pltpu.VMEM(left.shape, BF16),
+            pltpu.VMEM(weight.shape, BF16),
+            half,
+            half,
+            half,
+            pltpu.VMEM((rows, width), BF16),
+            pltpu.VMEM((rows, width), F32),
+            pltpu.VMEM((rows, width), BF16),
+            pltpu.VMEM(small.shape, F32),
+            pltpu.VMEM((5, *small.shape), F32),
+            *scatter_scratch(rows, width),
+            pltpu.SemaphoreType.DMA((5, CHUNKS)),
+            pltpu.SemaphoreType.DMA((5, CHUNKS)),
+            pltpu.SemaphoreType.DMA((5,)),
+            pltpu.SemaphoreType.DMA((5,)),
+            pltpu.SemaphoreType.DMA((1,)),
+            pltpu.SemaphoreType.DMA((1,)),
+            pltpu.SemaphoreType.DMA((8 + CHUNKS,)),
+            *errand_scratch(kinds, sources),
+        ],
+        compiler_params=pltpu.CompilerParams(
+            collective_id=collective_id, has_side_effects=True, vmem_limit_bytes=58 * 2**20
+        ),
+        name="finish",
+    )(left, weight, weight_grad, tokens, resid_grad, gain, small, *sources)
 
 
 def rms_scale(values, gain):
@@ -389,11 +1460,159 @@
 
 
 def left_product(left, right):
-    return lax.dot_general(left, right, (((0,), (0,)), ((), ())), preferred_element_type=F32)
+    return dot(left, right, TN)
+
+
+def token_scales(group_ids, mixture_counts):
+    group_cols = lax.broadcasted_iota(jnp.int32, (1, GROUPS), 1)
+    counts = mixture_counts.astype(F32)
+    group_scale = jnp.sqrt(jnp.mean(counts) / counts)
+    return jnp.sum(jnp.where(group_ids[:, None] == group_cols, group_scale[None, :], 0.0), 1)
+
+
+def mixer_weights(w_query, w_key, w_value, w_gate_mix, w_beta):
+    padded = jnp.pad(w_beta, ((0, 0), (0, 128 - w_beta.shape[1])))
+    return jnp.concatenate([w_query, w_key, w_value, w_gate_mix, padded], 1)
+
+
+ALL = ("y", "core", "zh", "zl", "x")
+SIZES = (2, 2, 2, 2, 2)
+
+
+FORWARD_PLAN = (
+    (0, 0, "start"), (0, 1, "start"), (1, 0, "settle"), (3, 0, "spread"), (3, 2, "start"),
+    (4, 1, "middle"), (6, 0, "middle"), (7, 0, "late"), (7, 2, "middle"),
+    (7, 0, "finish"), (7, 1, "finish"), (7, 2, "finish"),
+)
+BACKWARD_PLAN = (
+    (0, 0, "start"), (0, 1, "start"), (0, 2, "start"), (0, 3, "start"), (4, 2, "middle"),
+    (7, 0, "finish"), (7, 1, "finish"), (7, 2, "finish"), (7, 3, "finish"),
+)
+
+
+def halves_sum(values, came):
+    rows = came.shape[0]
+    mine = lax.dynamic_slice_in_dim(values, lax.axis_index("y") * rows, rows, 0)
+    return (mine.astype(F32) + came.astype(F32)).astype(BF16)
+
+
+def total_of(part, far):
+    return (part.astype(F32) + far.astype(F32)).astype(BF16)
+
+
+def shards_ring(
+    tokens, group_ids, mixture_counts, grad_out, norm1_gain, w_query, w_key, w_value, w_gate_mix,
+    w_beta, conv_query, conv_key, conv_value, out_gain, w_out, norm2_gain, w_gate, w_up, w_down,
+):
+    heads = w_beta.shape[1]
+    head_cols = w_query.shape[1]
+    gain = out_gain.astype(F32)[None]
+    gain1 = norm1_gain.astype(F32)[None]
+    conv = jnp.concatenate([conv_query, conv_key, conv_value], 1).astype(F32)
+    conv = jnp.pad(conv, ((0, 4), (0, 0)))
+    grad_mlp = grad_out.astype(F32) * token_scales(group_ids, mixture_counts)[:, None]
+    padded_beta = jnp.pad(w_beta, ((0, 0), (0, 128 - heads)))
+    tokens, gathered, projected, mix_weights, conv = begin(
+        tokens, gain1, conv, [w_query, w_key, w_value, w_gate_mix, padded_beta], 1
+    )
+    inputs = tokens.astype(F32)
+    mixed, *kept, gathered_grad, w_out, w_gate = mixer_forward(
+        projected, conv, gain, heads,
+        [(ExchangeGather, grad_mlp.astype(BF16)), (Swap, w_out), (Swap, w_gate)],
+        FORWARD_PLAN, 2,
+    )
+    gathered_grad = gathered_grad.reshape(-1, gathered_grad.shape[2])
+    own = (lax.axis_index("core") * 2 + lax.axis_index("zl")) * 2 + lax.axis_index("x")
+    rows = tokens.shape[0]
+    grad_rows = lax.dynamic_slice_in_dim(gathered_grad, own * rows, rows, 0).astype(F32)
+    attn, w_up = multiply_scatter([mixed], [w_out], NN, 3, "scatter_attn", [(Swap, w_up)])
+    resid = inputs + attn
+    normed_mlp, norm2_back = jax.vjp(rms_scale, resid, norm2_gain.astype(F32))
+    gathered_mlp, gate, up_vals, w_down = gather_multiply(
+        normed_mlp.astype(BF16), [w_gate, w_up], NN, 4, "gather_normed_mlp", [(Swap, w_down)]
+    )
+    hidden_full, swiglu_back = jax.vjp(swiglu, gate, up_vals)
+    hidden = hidden_full.astype(BF16)
+    hidden_grad = dot(gathered_grad, w_down, NT)
+    gate_grad, up_grad = (v.astype(BF16) for v in swiglu_back(hidden_grad))
+    down_grad = left_product(hidden, gathered_grad).astype(BF16)
+    gate_wgrad = left_product(gathered_mlp, gate_grad).astype(BF16)
+    up_wgrad = left_product(gathered_mlp, up_grad).astype(BF16)
+    normed_mlp_grad, down_came, gate_came = multiply_scatter(
+        [gate_grad, up_grad], [w_gate, w_up], NT, 5, "scatter_normed_mlp_grad",
+        [(HalfOverY, down_grad), (HalfOverY, gate_wgrad)],
+    )
+    resid_norm_grad, norm2_grad = norm2_back(normed_mlp_grad)
+    resid_grad = grad_rows + resid_norm_grad
+    down_part = halves_sum(down_grad, down_came)
+    gate_part = halves_sum(gate_wgrad, gate_came)
+    gathered_attn, mixed_grad, up_came, down_far = gather_multiply(
+        resid_grad.astype(BF16), [w_out], NT, 6, "gather_attn_grad",
+        [(HalfOverY, up_wgrad), (Across, down_part)],
+    )
+    up_part = halves_sum(up_wgrad, up_came)
+    out_grad = left_product(mixed, gathered_attn).astype(BF16)
+    raw_grad, conv_grad, gain_grad, gate_far, up_far, down_total, out_came = mixer_backward(
+        projected, conv, gain, mixed_grad, *kept, heads,
+        [
+            (Across, gate_part), (Across, up_part), (Spread, total_of(down_part, down_far)),
+            (HalfOverY, out_grad),
+        ],
+        BACKWARD_PLAN, 7,
+    )
+    out_part = halves_sum(out_grad, out_came)
+    mlp_out, gate_total, up_total, out_far = multiply_scatter(
+        [hidden], [w_down], NN, 8, "scatter_mlp",
+        [
+            (Spread, total_of(gate_part, gate_far)), (Spread, total_of(up_part, up_far)),
+            (Across, out_part),
+        ],
+    )
+    output = (resid + mlp_out).astype(BF16)
+    mix_weight_grad = left_product(gathered, raw_grad).astype(BF16)
+    width = tokens.shape[1]
+    placed = jnp.where(
+        lax.broadcasted_iota(jnp.int32, (8, 1, 1), 0) == own, conv_grad[None, :4], 0.0
+    ).reshape(-1, width)
+    small = jnp.concatenate(
+        [
+            jnp.zeros((1, width), F32), norm2_grad[None],
+            jnp.pad(gain_grad[:1], ((0, 0), (0, width - gain_grad.shape[1]))), placed,
+        ],
+        0,
+    )
+    small = jnp.pad(small, ((0, -small.shape[0] % 8), (0, 0)))
+    grad_tokens, mix_total, small, output, out_total = finish(
+        raw_grad, mix_weights, mix_weight_grad, tokens, resid_grad, gain1, small, 9,
+        [(Exchange, output), (Spread, total_of(out_part, out_far))],
+    )
+    shard = (lax.axis_index("zh") * 2 + lax.axis_index("zl")) * 2 + lax.axis_index("x")
+    placed = small[3 : 3 + 4 * 24 * head_cols // width].reshape(8, 4, 3 * head_cols)
+    conv_total = lax.dynamic_index_in_dim(placed, shard, 0, keepdims=False)
+    mix_total = mix_total.astype(F32)
+    return (
+        output,
+        grad_tokens,
+        small[0],
+        mix_total[:, 0:head_cols],
+        mix_total[:, head_cols : 2 * head_cols],
+        mix_total[:, 2 * head_cols : 3 * head_cols],
+        mix_total[:, 3 * head_cols : 4 * head_cols],
+        mix_total[:, 4 * head_cols : 4 * head_cols + heads],
+        conv_total[:, 0:head_cols],
+        conv_total[:, head_cols : 2 * head_cols],
+        conv_total[:, 2 * head_cols :],
+        small[2, :HEAD_DIM],
+        out_total.astype(F32),
+        small[1],
+        gate_total.astype(F32),
+        up_total.astype(F32),
+        down_total.astype(F32),
+    )
 
 
 def right_product(left, right):
-    return lax.dot_general(left, right, (((1,), (1,)), ((), ())), preferred_element_type=F32)
+    return dot(left, right, NT)
 
 
 def make_fold(kept_rows, weight, piece):
@@ -433,8 +1652,7 @@
     normed, norm1_back = jax.vjp(rms_scale, inputs, norm1_gain.astype(F32))
     gathered = lax.all_gather(normed.astype(BF16), "tp", axis=0, tiled=True)
     heads = w_beta.shape[1]
-    w_beta = jnp.pad(w_beta, ((0, 0), (0, 128 - heads)))
-    mix_weights = jnp.concatenate([w_query, w_key, w_value, w_gate_mix, w_beta], 1)
+    mix_weights = mixer_weights(w_query, w_key, w_value, w_gate_mix, w_beta)
     projected = jnp.dot(gathered, mix_weights, preferred_element_type=F32)
     head_cols = w_query.shape[1]
     conv = jnp.concatenate([conv_query, conv_key, conv_value], 1).astype(F32)
@@ -455,10 +1673,7 @@
         make_rows(hidden, w_down, False).astype(jnp.bfloat16), "tp", scatter_dimension=0, tiled=True
     ).astype(jnp.float32)
     output = (resid + mlp_out).astype(BF16)
-    group_cols = lax.broadcasted_iota(jnp.int32, (1, GROUPS), 1)
-    counts = mixture_counts.astype(F32)
-    group_scale = jnp.sqrt(jnp.mean(counts) / counts)
-    token_scale = jnp.sum(jnp.where(group_ids[:, None] == group_cols, group_scale[None, :], 0.0), 1)
+    token_scale = token_scales(group_ids, mixture_counts)
     grad_rows = grad_out.astype(F32) * token_scale[:, None]
     grad_mlp = grad_rows.astype(BF16)
     grad_w_down, hidden_grad = make_fold(
@@ -523,48 +1738,24 @@
 
 
 def solution(mesh):
+    rows, cols, all_rows = "tp", "tp", ("dp", "tp")
+    body = shards
+    if dict(mesh.shape) == {"dp": 4, "tp": 8}:
+        mesh = Mesh(mesh.devices.reshape(SIZES), ALL)
+        rows = cols = ("zh", "zl", "x")
+        all_rows = ALL
+        body = shards_ring
+    by_row, by_col, by_token = P(rows, None), P(None, cols), P(all_rows, None)
     return jax.shard_map(
-        shards,
+        body,
         mesh=mesh,
         in_specs=(
-            P(("dp", "tp"), None),
-            P(("dp", "tp")),
-            P(),
-            P(("dp", "tp"), None),
-            P(),
-            P(None, "tp"),
-            P(None, "tp"),
-            P(None, "tp"),
-            P(None, "tp"),
-            P(None, "tp"),
-            P(None, "tp"),
-            P(None, "tp"),
-            P(None, "tp"),
-            P(),
-            P("tp", None),
-            P(),
-            P(None, "tp"),
-            P(None, "tp"),
-            P("tp", None),
+            by_token, P(all_rows), P(), by_token, P(), by_col, by_col, by_col, by_col, by_col,
+            by_col, by_col, by_col, P(), by_row, P(), by_col, by_col, by_row,
         ),
         out_specs=(
-            P(("dp", "tp"), None),
-            P(("dp", "tp"), None),
-            P(),
-            P(None, "tp"),
-            P(None, "tp"),
-            P(None, "tp"),
-            P(None, "tp"),
-            P(None, "tp"),
-            P(None, "tp"),
-            P(None, "tp"),
-            P(None, "tp"),
-            P(),
-            P("tp", None),
-            P(),
-            P(None, "tp"),
-            P(None, "tp"),
-            P("tp", None),
+            by_token, by_token, P(), by_col, by_col, by_col, by_col, by_col, by_col, by_col,
+            by_col, P(), by_row, P(), by_col, by_col, by_row,
         ),
         check_vma=False,
     )

time: 1640 us -> 935 us (0.57)
  waiting for transfers between devices: 1170 us -> 0 us
  Pallas kernels: 154 us -> 752 us
  matrix products: 158 us -> 67.4 us
  blocking collectives: 55 us -> 0 us
    pallas_call x2 -> x9, Pallas kernels: 154 us -> 752 us  [the longest x3 192 us: multiply_scatter(): pl.pallas_call(functools.partial(scatter_body, dims, count, kinds), in_sp...]
    reduce_scatter x4 -> x0, waiting for transfers between devices: 520 us -> none  [the longest x1 147 us: shards(): lax.psum_scatter(make_rows(pair_grad, pair_weights, True).astype(jnp.bflo...]
    all_gather x4 -> x0, waiting for transfers between devices: 436 us -> none  [the longest x1 119 us: shards(): gathered = lax.all_gather(normed.astype(BF16), 'tp', axis=0, tiled=True)]
    psum x1 -> x0, waiting for transfers between devices: 209 us -> none  [shards(): lax.psum(mix_weight_grad.astype(jnp.bfloat16), 'dp').astype(jnp.float32)]
    dot_general x12 -> x6, matrix products: 158 us -> 67.4 us  [dot(): lax.dot_general(left, right, (dims, ((), ())), preferred_element_type=F32)]
    psum x2 -> x0, blocking collectives: 55 us -> none  [the longest x1 42.8 us: shards(): gains = lax.psum((norm1_grad, gain_grad[0], norm2_grad), ('dp', 'tp'))]
    convert_element_type x10 -> x15, other arithmetic: 24.7 us -> 34 us  [the longest x3 6.85 us: halves_sum(): return (mine.astype(F32) + came.astype(F32)).astype(BF16)]
    unnamed x71 -> x64, local copies, waits for them, and re-layouts: 34.4 us -> 27.5 us
  transfers between devices with their start and end apart: 9 -> 0, of which waited for: 9 -> 0; matrix products, arithmetic and copies ran while one was open for 8% -> 0% of each run, Pallas kernels for 0% -> 0%
where the time goes in v2:
time: 935 us; the launch traced here: 926 us
  Pallas kernels  752 us (80%)
  matrix products  67.4 us (7%)
  local copies, waits for them, and re-layouts  62.2 us (7%)
  other arithmetic  42.9 us (5%)
    pallas_call x3, Pallas kernels, multiply_scatter(): pl.pallas_call(functools.partial(scatter_body, dims, count, kinds), in_sp...  192 us
    pallas_call x1, Pallas kernels, finish(): pl.pallas_call(functools.partial(finish_body, kinds), in_specs=[hbm] * 5...  151 us
    pallas_call x2, Pallas kernels, gather_multiply(): pl.pallas_call(functools.partial(gather_body, dims, count, kinds), in_spe...  131 us
    pallas_call x1, Pallas kernels, mixer_forward(): pl.pallas_call(functools.partial(mixer_forward_body, heads, kinds, plan),...  114 us
    pallas_call x1, Pallas kernels, begin(): pl.pallas_call(begin_body, in_specs=[hbm, pl.BlockSpec(memory_space=pltpu...  88.9 us
    pallas_call x1, Pallas kernels, mixer_backward(): pl.pallas_call(functools.partial(mixer_backward_body, heads, kinds, plan)...  75.5 us
    dot_general x6, matrix products, dot(): lax.dot_general(left, right, (dims, ((), ())), preferred_element_type=F32)  67.4 us
    unnamed x64, local copies, waits for them, and re-layouts  27.5 us

profile of v2, /device:TPU:0, one launch (start us, length us, event | category | flops | bytes accessed | tf_op | source)
XLA Modules:
  0.0 926.5 jit_solution(8357001705076264121)
XLA Ops:
  0.7 1.3 convert_reduce_fusion
  5.4 1.3 broadcast_in_dim.66
  6.7 1.3 fusion.11.conv_ref
  8.0 1.0 copy.51
  9.9 1.5 multiply_convert_fusion.3.refs_3_
  11.4 4.6 copy.52.refs_5_
  16.0 4.6 copy.53.refs_2_
  20.5 88.9 %begin.1 = (bf16[256,2048]{1,0:T(8,128)(2,1)}, bf16[8,256,2048]{2,1,0:T(8,128)(2,1)}, f32[8,256,1152]{2,1,0:T(8,128)}, bf16[2048,1152]{1,0:T(8,128)(2,1)}, f32[8,768]{1,0:T(8,128)}) custom-call(bf16[256,2048]{1,0:T(8,128)(2,1)} %tokens_ref.1, f32[1,2048]{1,0:T(1,128)} %bitcast.53, f32[8,768]{1,0:T(8,128)} %fusion.11.conv_ref, bf16[2048,256]{1,0:T(8,128)(2,1)} %refs_0_.1, ...), custom_call_target="tpu_custom_call" | custom-call | tf_op jit(solution)/shard_map/begin/pallas_call | solution.py:1198
  110.2 114.5 %mixer_forward.1 = (bf16[2048,256]{1,0:T(8,128)(2,1)S(1)}, f32[2048,512]{1,0:T(8,128)}, f32[2048,256]{1,0:T(8,128)}, f32[2048,256]{1,0:T(8,128)}, f32[32,2,128,1...) custom-call(f32[2048,1152]{1,0:T(8,128)} %bitcast.39, ...), custom_call_target="tpu_custom_call" | custom-call | tf_op jit(solution)/shard_map/mixer_forward/pallas_call | solution.py:186
  225.7 1.0 copy-done.2
  226.7 66.2 %scatter_attn.1 = (f32[256,2048]{1,0:T(8,128)}, bf16[2048,704]{1,0:T(8,128)(2,1)}) custom-call(bf16[8,256,256]{2,1,0:T(8,128)(2,1)} %bitcast.38, bf16[256,2048]{1,0:T(8,128)(2,1)} %copy-done.2, bf16[2048,704]{1,0:T(8,128)(2,1)} %copy.53.refs_2_), custom_call_target="tpu_custom_call" | custom-call | tf_op jit(solution)/shard_map/scatter_attn/pallas_call | solution.py:1073
  292.9 2.0 multiply_reduce_fusion.2
  294.9 1.2 multiply_convert_fusion.2.block_ref
  296.1 68.4 %gather_normed_mlp.1 = (bf16[8,256,2048]{2,1,0:T(8,128)(2,1)}, f32[8,256,704]{2,1,0:T(8,128)}, f32[8,256,704]{2,1,0:T(8,128)}, bf16[704,2048]{1,0:T(8,128)(2,1)}) custom-call(bf16[256,2048]{1,0:T(8,128)(2,1)} %multiply_convert_fusion.2.block_ref, bf16[2048,704]{1,0:T(8,128)(2,1)} %get-tuple-element.67.refs_0_.refs_2_, ...), custom_call_target="tpu_custom_call" | custom-call | tf_op jit(solution)/shard_map/gather_normed_mlp/pallas_call | solution.py:908
  364.6 5.7 multiply_convert_fusion.refs_0_
  370.3 1.6 copy-done.9
  371.9 8.0 bitcast_convert_fusion.refs_4_
  379.9 6.4 copy.55
  386.3 6.4 copy.54
  392.6 13.7 %multiply_convert_fusion.1 = (bf16[2048,704]{0,1:T(8,128)(2,1)S(1)}, bf16[2048,704]{0,1:T(8,128)(2,1)S(1)}) fusion(f32[2048,704]{0,1:T(8,128)} %copy.55, f32[2048,704]{0,1:T(8,128)} %copy.54, bf16[2048,2048]{1,0:T(8,128)(2,1)} %bitcast.49, bf16[704,2048]{1,0:T(8,128)(2,1)} %get-tuple-element.69.refs_1_), kind=kOutput, calls=%fused_computation.7 | convolution fusion | flops 5925765120 | bytes 28573696 | tf_op jit(solution)/shard_map/dot_general | solution.py:29
  406.4 12.6 %convolution_convert_fusion.1.refs_1_ = bf16[2048,704]{1,0:T(8,128)(2,1)} fusion(bf16[2048,2048]{1,0:T(8,128)(2,1)} %bitcast.59, bf16[2048,704]{0,1:T(8,128)(2,1)S(1)} %get-tuple-element.143), kind=kOutput, calls=%fused_computation.9 | convolution fusion | flops 5907021824 | bytes 14155776 | tf_op jit(solution)/shard_map/dot_general | solution.py:29
  418.9 10.6 %convolution_convert_fusion.2.refs_5_ = bf16[2048,704]{1,0:T(8,128)(2,1)} fusion(bf16[2048,2048]{1,0:T(8,128)(2,1)} %bitcast.60, bf16[2048,704]{0,1:T(8,128)(2,1)S(1)} %get-tuple-element.144), kind=kOutput, calls=%fused_computation.10 | convolution fusion | flops 5907021824 | bytes 14155776 | tf_op jit(solution)/shard_map/dot_general | solution.py:29
  429.5 4.6 copy.57
  434.1 4.6 copy.59
  438.7 77.7 %scatter_normed_mlp_grad.1 = (f32[256,2048]{1,0:T(8,128)}, bf16[352,2048]{1,0:T(8,128)(2,1)}, bf16[1024,704]{1,0:T(8,128)(2,1)}) custom-call(bf16[8,256,704]{2,1,0:T(8,128)(2,1)} %bitcast.45, bf16[8,256,704]{2,1,0:T(8,128)(2,1)} %bitcast.46, bf16[2048,704]{1,0:T(8,128)(2,1)} %get-tuple-element.67.refs_0_.refs_2_, ...), custom_call_target="tpu_custom_call" | custom-call | tf_op jit(solution)/shard_map/scatter_normed_mlp_grad/pallas_call | solution.py:1073
  516.4 3.2 add_convert_fusion.5.refs_2_
  520.4 3.6 fusion.13
  524.0 62.4 %gather_attn_grad.1 = (bf16[8,256,2048]{2,1,0:T(8,128)(2,1)}, f32[8,256,256]{2,1,0:T(8,128)}, bf16[1024,704]{1,0:T(8,128)(2,1)}, bf16[352,2048]{1,0:T(8,128)(2,1)}) custom-call(bf16[256,2048]{1,0:T(8,128)(2,1)} %get-tuple-element.139.block_ref, bf16[256,2048]{1,0:T(8,128)(2,1)} %copy-done.2, bf16[2048,704]{1,0:T(8,128)(2,1)} %convolution_convert_fusion.1.refs_1_, ...), custom_call_target="tpu_custom_call" | custom-call | tf_op jit(solution)/shard_map/gather_attn_grad/pallas_call | solution.py:908
  586.4 5.9 convolution_convert_fusion.3.refs_13_
  592.9 1.3 copy-done.11
  594.2 2.7 add_convert_fusion.2
  596.9 75.5 %mixer_backward.1 = (bf16[2048,1152]{1,0:T(8,128)(2,1)}, f32[8,768]{1,0:T(8,128)S(1)}, f32[8,128]{1,0:T(8,128)S(1)}, bf16[1024,704]{1,0:T(8,128)(2,1)S(1)}, bf16...) custom-call(f32[2048,1152]{1,0:T(8,128)} %bitcast.40, f32[2048,1152]{1,0:T(8,128)} %bitcast.41, ...), custom_call_target="tpu_custom_call" | custom-call | tf_op jit(solution)/shard_map/mixer_backward/pallas_call | solution.py:390
  672.4 16.7 %convolution_convert_fusion.refs_2_ = bf16[2048,1152]{1,0:T(8,128)(2,1)} fusion(bf16[2048,2048]{1,0:T(8,128)(2,1)} %bitcast.58, bf16[2048,1152]{1,0:T(8,128)(2,1)} %get-tuple-element.85), kind=kOutput, calls=%fused_computation.1 | convolution fusion | flops 9666035712 | bytes 17825792 | tf_op jit(solution)/shard_map/dot_general | solution.py:29
  690.1 1.6 add_convert_fusion.refs_3_
  691.7 1.6 add_convert_fusion.1.refs_2_
  693.4 47.7 %scatter_mlp.1 = (f32[256,2048]{1,0:T(8,128)}, bf16[2048,704]{1,0:T(8,128)(2,1)}, bf16[2048,704]{1,0:T(8,128)(2,1)}, bf16[128,2048]{1,0:T(8,128)(2,1)}) custom-call(bf16[8,256,704]{2,1,0:T(8,128)(2,1)} %copy-done.9, bf16[704,2048]{1,0:T(8,128)(2,1)} %get-tuple-element.69.refs_1_, bf16[1024,704]{1,0:T(8,128)(2,1)} %add_convert_fusion.1.refs_2_, ...), custom_call_target="tpu_custom_call" | custom-call | tf_op jit(solution)/shard_map/scatter_mlp/pallas_call | solution.py:1073
  741.1 2.9 add_convert_fusion.6.refs_7_
  745.9 150.7 %finish.1 = (bf16[256,2048]{1,0:T(8,128)(2,1)}, bf16[2048,1152]{1,0:T(8,128)(2,1)}, f32[16,2048]{1,0:T(8,128)}, bf16[256,2048]{1,0:T(8,128)(2,1)}, bf16[256,2048]{1,0:T(8,128)(2,1)}) custom-call(bf16[8,256,1152]{2,1,0:T(8,128)(2,1)} %bitcast.47, bf16[2048,1152]{1,0:T(8,128)(2,1)} %get-tuple-element.86.refs_1_, ...), custom_call_target="tpu_custom_call" | custom-call | tf_op jit(solution)/shard_map/finish/pallas_call | solution.py:1416
  896.6 1.3 slice_bitcast_fusion
  897.9 1.5 fusion.16
  901.0 1.1 slice.60
  903.1 1.6 convert_element_type.193
  904.6 5.7 fusion.15
  910.4 5.4 copy.64
  915.7 3.4 copy.65
  919.1 5.3 convert_element_type.196
  924.4 1.0 copy.71
  925.3 1.0 copy.72
  (78 shorter events, 12.0 us)
Async XLA Ops:
  20.5 89.0 %copy-start.3 = (bf16[256,2048]{1,0:T(8,128)(2,1)S(1)}, bf16[256,2048]{1,0:T(8,128)(2,1)}, u32[]{:S(2)}) copy-start(bf16[256,2048]{1,0:T(8,128)(2,1)} %refs_4_.1) | copy-start | bytes 3145732
  109.5 0.7 copy-start.4
  224.7 1.0 copy-start
  225.7 1.0 copy-start.2
  226.7 66.2 %copy-start.15 = (bf16[256,2048]{1,0:T(8,128)(2,1)S(1)}, bf16[256,2048]{1,0:T(8,128)(2,1)}, u32[]{:S(2)}) copy-start(bf16[256,2048]{1,0:T(8,128)(2,1)} %get-tuple-element.63.refs_3_) | copy-start | bytes 3145732
  296.1 75.8 %slice-start = ((s8[8388608]{0:T(1024)(128)(4,1)}), s8[4194304]{0:T(1024)(128)(4,1)S(1)}, s32[]{:S(2)}) async-start(s8[8388608]{0:T(1024)(128)(4,1)} %bitcast.51), calls=%async_computation | async-start | bytes 8388608
  364.6 7.4 slice-start.1
  370.3 1.7 copy-start.9
  406.3 12.6 %copy-start.17 = (bf16[2048,704]{0,1:T(8,128)(2,1)}, bf16[2048,704]{0,1:T(8,128)(2,1)S(1)}, u32[]{:S(2)}) copy-start(bf16[2048,704]{0,1:T(8,128)(2,1)S(1)} %get-tuple-element.143) | copy-start | bytes 8650756
  406.3 12.6 %copy-start.18 = (bf16[2048,704]{0,1:T(8,128)(2,1)}, bf16[2048,704]{0,1:T(8,128)(2,1)S(1)}, u32[]{:S(2)}) copy-start(bf16[2048,704]{0,1:T(8,128)(2,1)S(1)} %get-tuple-element.144) | copy-start | bytes 8650756
  438.7 77.7 %copy-start.13 = (bf16[704,2048]{1,0:T(8,128)(2,1)S(1)}, bf16[704,2048]{1,0:T(8,128)(2,1)}, u32[]{:S(2)}) copy-start(bf16[704,2048]{1,0:T(8,128)(2,1)} %bitcast_convert_fusion.refs_4_) | copy-start | bytes 8650756
  516.4 3.2 copy-start.10
  524.0 62.4 %copy-start.1 = (bf16[2048,256]{1,0:T(8,128)(2,1)S(1)}, bf16[2048,256]{1,0:T(8,128)(2,1)}, u32[]{:S(2)}) copy-start(bf16[2048,256]{1,0:T(8,128)(2,1)} %copy-done) | copy-start | bytes 3145732
  586.4 6.0 copy-start.8
  586.4 6.0 copy-start.21
  586.4 6.5 copy-start.12
  586.4 6.5 copy-start.19
  586.4 6.5 copy-start.20
  592.3 1.9 copy-start.11
  594.2 2.7 copy-start.5
  672.4 17.7 %copy-start.7 = (bf16[1024,704]{1,0:T(8,128)(2,1)S(1)}, bf16[1024,704]{1,0:T(8,128)(2,1)}, u32[]{:S(2)}) copy-start(bf16[1024,704]{1,0:T(8,128)(2,1)} %get-tuple-element.154.refs_11_) | copy-start | bytes 4325380
  689.1 2.6 copy-start.6
  741.1 3.0 copy-start.14
  741.1 3.0 copy-start.25
  896.6 6.5 copy-start.22
  910.4 5.4 copy-start.16
  919.1 5.3 copy-start.24
  919.1 6.2 copy-start.23

commit v3 on v2

v3 whole, which is shorter than its diff:
```python
import functools

import jax
import jax.numpy as jnp
from jax import lax
from jax.experimental import pallas as pl
from jax.experimental.pallas import tpu as pltpu
from jax.sharding import Mesh
from jax.sharding import PartitionSpec as P

GROUPS = 8
HEAD_DIM = 128
SPAN = 64
SEQ_LEN = 2048
TILE = 256
F32 = jnp.float32
BF16 = jnp.bfloat16
NN = ((1,), (0,))
NT = ((1,), (1,))
TN = ((0,), (0,))


def split(values):
    high = values.astype(BF16)
    return high, (values - high.astype(F32)).astype(BF16)


def dot(left, right, dims):
    return lax.dot_general(left, right, (dims, ((), ())), preferred_element_type=F32)


def product(left, right, dims):
    return (
        dot(left[0], right[0], dims)
        + (dot(left[0], right[1], dims) + dot(left[1], right[0], dims))
    )


def quick(left, right, dims):
    return dot(left[0], right[0], dims)


def rows_of(pair, start, size):
    return pair[0][start : start + size], pair[1][start : start + size]


def sigmoid(values):
    return 1.0 / (1.0 + jnp.exp(-values))


def tile_masks():
    row = lax.broadcasted_iota(jnp.int32, (TILE, TILE), 0)
    col = lax.broadcasted_iota(jnp.int32, (TILE, TILE), 1)
    return row, col


def invert_all(lowers, row, col, refine=False):
    def level(size):
        return (row // (2 * size) == col // (2 * size)) & (row // size > col // size)

    first = level(1)
    eye = jnp.where(row == col, 1.0, 0.0)
    inverses = [eye - jnp.where(first, lower, 0.0) for lower in lowers]
    size = 2
    while size < SPAN:
        mask = level(size)
        parts = [split(jnp.where(mask, lower, 0.0)) for lower in lowers]
        held = [split(inverse) for inverse in inverses]
        firsts = [quick(part, h, NN) for part, h in zip(parts, held)]
        seconds = [quick(h, split(f), NN) for h, f in zip(held, firsts)]
        inverses = [inverse - second for inverse, second in zip(inverses, seconds)]
        size *= 2
    if True:
        held = [split(inverse) for inverse in inverses]
        rest = [
            eye - inverse - product(split(lower), h, NN)
            for lower, inverse, h in zip(lowers, inverses, held)
        ]
        inverses = [
            inverse + quick(h, split(r), NN) for inverse, h, r in zip(inverses, held, rest)
        ]
    return inverses


def conv_rows(buffer, taps):
    total = taps[0:1] * buffer[pl.ds(5, TILE), :]
    for offset in range(1, 4):
        total = total + taps[offset : offset + 1] * buffer[pl.ds(5 + offset, TILE), :]
    return total


LATE_PHASES = ("settle_late", "forward", "finish")


def run_errands(errands, plan, step, late):
    if not errands:
        return
    if not late:
        pl.when(step == 0)(lambda: greet(True))
    for at in sorted({entry[0] for entry in plan}):

        @pl.when(step == at)
        def _(at=at):
            for when, index, phase in plan:
                if when == at and (phase in LATE_PHASES) == late:
                    getattr(errands[index], phase)()


def errand_operands(errands):
    kinds, sources = [e[0] for e in errands], [e[1] for e in errands]
    specs = [pl.BlockSpec(memory_space=pl.ANY)] * len(errands)
    shapes = [errand_target(*errand) for errand in errands]
    return kinds, sources, specs, shapes, errand_scratch(kinds, sources) if errands else []


def mixer_params(errands, collective_id):
    extra = {"collective_id": collective_id, "has_side_effects": True} if errands else {}
    return pltpu.CompilerParams(vmem_limit_bytes=48 * 2**20, **extra)


def mixer_forward_body(heads, kinds, plan, *refs):
    first_ref, refs, errands = take_errands(kinds, refs, 3, 6) if kinds else (refs[0], refs[1:], ())
    proj_ref = first_ref
    conv_ref, gain_ref, mixed_ref, wu_ref, fresh_ref, out_ref, state_ref, inverse_ref, *refs = refs
    rows_buf, state = refs
    tile = pl.program_id(1)
    run_errands(errands, plan, tile, False)
    wide = heads * HEAD_DIM

    @pl.when(tile == 0)
    def _():
        rows_buf[0:8, :] = jnp.zeros((8, 3 * wide), F32)
        state[...] = jnp.zeros_like(state)

    @pl.when(tile > 0)
    def _():
        rows_buf[0:8, :] = rows_buf[TILE : TILE + 8, :]

    rows_buf[8 : 8 + TILE, :] = proj_ref[:, : 3 * wide]
    summed = conv_rows(rows_buf, conv_ref[...])
    active = summed * sigmoid(summed)
    row, col = tile_masks()
    same = row // SPAN == col // SPAN
    held = []
    for head in range(heads):
        lo = head * HEAD_DIM
        query = active[:, lo : lo + HEAD_DIM]
        key = active[:, wide + lo : wide + lo + HEAD_DIM]
        value = active[:, 2 * wide + lo : 2 * wide + lo + HEAD_DIM]
        beta = sigmoid(proj_ref[:, 4 * wide + head : 4 * wide + head + 1])
        query = query * (
            lax.rsqrt(jnp.sum(query * query, -1, keepdims=True) + 1e-06) * HEAD_DIM ** (-0.5)
        )
        key = key * lax.rsqrt(jnp.sum(key * key, -1, keepdims=True) + 1e-06)
        key_beta = key * beta
        held.append((split(query), split(key), key_beta, value * beta))
    lowers = [
        jnp.where(same & (row > col), product(split(key_beta), key_s, NT), 0.0)
        for _, key_s, key_beta, _ in held
    ]
    inverses = invert_all(lowers, row, col)
    boths = [
        product(split(inverse), split(jnp.concatenate([key_beta, value_beta], 1)), NN)
        for inverse, (_, _, key_beta, value_beta) in zip(inverses, held)
    ]
    scores = [
        jnp.where(same & (row >= col), product(query_s, key_s, NT), 0.0)
        for query_s, key_s, _, _ in held
    ]
    weights = [split(both[:, :HEAD_DIM]) for both in boths]
    memories = [state[head] for head in range(heads)]
    fresh_all = [[] for _ in range(heads)]
    carried_all = [[] for _ in range(heads)]
    for block in range(TILE // SPAN):
        start = block * SPAN
        for head in range(heads):
            state_ref[block, head] = memories[head]
        reads = [
            product(
                tuple(
                    jnp.concatenate([a[start : start + SPAN], b[start : start + SPAN]], 0)
                    for a, b in zip(weights[head], held[head][0])
                ),
                split(memories[head]),
                NN,
            )
            for head in range(heads)
        ]
        for head in range(heads):
            fresh_all[head].append(boths[head][start : start + SPAN, HEAD_DIM:] - reads[head][:SPAN])
            carried_all[head].append(reads[head][SPAN:])
        memories = [
            memories[head]
            + product(rows_of(held[head][1], start, SPAN), split(fresh_all[head][-1]), TN)
            for head in range(heads)
        ]
    for head in range(heads):
        lo = head * HEAD_DIM
        state[head] = memories[head]
        inverse_ref[head] = inverses[head]
        wu_ref[:, 2 * lo : 2 * lo + 2 * HEAD_DIM] = boths[head]
        fresh = jnp.concatenate(fresh_all[head], 0)
        fresh_ref[:, lo : lo + HEAD_DIM] = fresh
        out = jnp.concatenate(carried_all[head], 0)
        out = out + product(split(scores[head]), split(fresh), NN)
        out_ref[:, lo : lo + HEAD_DIM] = out
        gate = proj_ref[:, 3 * wide + lo : 3 * wide + lo + HEAD_DIM]
        scale = lax.rsqrt(jnp.mean(out * out, -1, keepdims=True) + 1e-05)
        mixed = out * scale * gain_ref[...] * (gate * sigmoid(gate))
        mixed_ref[:, lo : lo + HEAD_DIM] = mixed.astype(BF16)
    run_errands(errands, plan, tile, True)


def mixer_forward(proj, conv, gain, heads, errands=(), plan=(), collective_id=None):
    rows = proj.shape[0]
    wide = heads * HEAD_DIM
    tiles = SEQ_LEN // TILE
    seqs = rows // SEQ_LEN
    blocks = TILE // SPAN

    def at(seq, tile):
        return (seq * tiles + tile, 0)

    kinds, sources, specs, shapes, scratch = errand_operands(errands)
    return pl.pallas_call(
        functools.partial(mixer_forward_body, heads, kinds, plan),
        grid=(seqs, tiles),
        in_specs=[
            pl.BlockSpec((TILE, proj.shape[1]), at),
            pl.BlockSpec(conv.shape, lambda seq, tile: (0, 0)),
            pl.BlockSpec(gain.shape, lambda seq, tile: (0, 0)),
            *specs,
        ],
        out_specs=[
            pl.BlockSpec((TILE, wide), at),
            pl.BlockSpec((TILE, 2 * wide), at),
            pl.BlockSpec((TILE, wide), at),
            pl.BlockSpec((TILE, wide), at),
            pl.BlockSpec((blocks, heads, HEAD_DIM, HEAD_DIM), lambda s, t: (s * tiles + t, 0, 0, 0)),
            pl.BlockSpec((None, heads, TILE, TILE), lambda s, t: (s * tiles + t, 0, 0, 0)),
            *specs,
        ],
        out_shape=[
            jax.ShapeDtypeStruct((rows, wide), BF16),
            jax.ShapeDtypeStruct((rows, 2 * wide), F32),
            jax.ShapeDtypeStruct((rows, wide), F32),
            jax.ShapeDtypeStruct((rows, wide), F32),
            jax.ShapeDtypeStruct((rows // SPAN, heads, HEAD_DIM, HEAD_DIM), F32),
            jax.ShapeDtypeStruct((rows // TILE, heads, TILE, TILE), F32),
            *shapes,
        ],
        scratch_shapes=[
            pltpu.VMEM((TILE + 8, 3 * wide), F32),
            pltpu.VMEM((heads, HEAD_DIM, HEAD_DIM), F32),
            *scratch,
        ],
        compiler_params=mixer_params(errands, collective_id),
        name="mixer_forward",
    )(proj, conv, gain, *sources)


def unit_back(raw, scale, grad):
    along = jnp.sum(raw * grad, -1, keepdims=True)
    return scale * grad - raw * (scale * scale * scale * along)


def mixer_backward_body(heads, kinds, plan, *refs):
    first_ref, refs, errands = take_errands(kinds, refs, 10, 3) if kinds else (refs[0], refs[1:], ())
    proj_ref = first_ref
    before_ref, conv_ref, gain_ref, grad_ref, wu_ref, fresh_ref, out_ref, *refs = refs
    state_ref, inverse_ref, raw_grad_ref, conv_grad_ref, gain_grad_ref, *refs = refs
    rows_buf, grad_buf, state_grad = refs
    step = pl.program_id(1)
    run_errands(errands, plan, step, False)
    steps = pl.num_programs(1)
    wide = heads * HEAD_DIM

    @pl.when((step == 0) & (pl.program_id(0) == 0))
    def _():
        conv_grad_ref[...] = jnp.zeros_like(conv_grad_ref)
        gain_grad_ref[...] = jnp.zeros_like(gain_grad_ref)

    @pl.when(step == 0)
    def _():
        grad_buf[TILE : TILE + 8, :] = jnp.zeros((8, 3 * wide), F32)
        state_grad[...] = jnp.zeros_like(state_grad)

    @pl.when(step > 0)
    def _():
        grad_buf[TILE : TILE + 8, :] = grad_buf[0:8, :]

    first = step == steps - 1
    rows_buf[0:8, :] = jnp.where(first, 0.0, before_ref[:, : 3 * wide])
    rows_buf[8 : 8 + TILE, :] = proj_ref[:, : 3 * wide]
    summed = conv_rows(rows_buf, conv_ref[...])
    smooth = sigmoid(summed)
    active = summed * smooth
    slope = smooth * (1.0 + summed * (1.0 - smooth))
    row, col = tile_masks()
    same = row // SPAN == col // SPAN
    lane = lax.broadcasted_iota(jnp.int32, (TILE, HEAD_DIM), 1)
    beta_grads = jnp.zeros((TILE, HEAD_DIM), F32)
    gain_total = jnp.zeros((1, HEAD_DIM), F32)
    within = same & (row >= col)
    below = same & (row > col)
    every = range(heads)
    at = [slice(head * HEAD_DIM, (head + 1) * HEAD_DIM) for head in every]
    query_raw = [active[:, lo] for lo in at]
    key_raw = [active[:, wide : 2 * wide][:, lo] for lo in at]
    value = [active[:, 2 * wide :][:, lo] for lo in at]
    beta = [sigmoid(proj_ref[:, 4 * wide + head : 4 * wide + head + 1]) for head in every]
    query_scale = [lax.rsqrt(jnp.sum(q * q, -1, keepdims=True) + 1e-06) for q in query_raw]
    key_scale = [lax.rsqrt(jnp.sum(k * k, -1, keepdims=True) + 1e-06) for k in key_raw]
    key = [k * scale for k, scale in zip(key_raw, key_scale)]
    key_s = [split(k) for k in key]
    query_s = [
        split(q * (scale * HEAD_DIM ** (-0.5))) for q, scale in zip(query_raw, query_scale)
    ]
    out_grad_s = []
    for head, lo in enumerate(at):
        gate = proj_ref[:, 3 * wide + head * HEAD_DIM : 3 * wide + (head + 1) * HEAD_DIM]
        grad = grad_ref[:, lo]
        out = out_ref[:, lo]
        scale = lax.rsqrt(jnp.mean(out * out, -1, keepdims=True) + 1e-05)
        gate_s = sigmoid(gate)
        normed = out * scale
        gain_total = gain_total + jnp.sum(grad * normed * (gate * gate_s), 0, keepdims=True)
        gate_grad = grad * normed * gain_ref[...] * (gate_s * (1.0 + gate * (1.0 - gate_s)))
        normed_grad = grad * gain_ref[...] * (gate * gate_s)
        out_grad = scale * normed_grad - out * (
            scale * scale * scale * jnp.mean(out * normed_grad, -1, keepdims=True)
        )
        out_grad_s.append(split(out_grad))
        raw_grad_ref[:, 3 * wide + head * HEAD_DIM : 3 * wide + (head + 1) * HEAD_DIM] = (
            gate_grad.astype(BF16)
        )
    fresh_s = [split(fresh_ref[:, lo]) for lo in at]
    both_s = [split(wu_ref[:, 2 * head * HEAD_DIM : 2 * (head + 1) * HEAD_DIM]) for head in every]
    weights_s = [(high[:, :HEAD_DIM], low[:, :HEAD_DIM]) for high, low in both_s]
    scores_s = [
        split(jnp.where(within, product(query_s[h], key_s[h], NT), 0.0)) for h in every
    ]
    fresh_grad_in = [product(scores_s[h], out_grad_s[h], TN) for h in every]
    carry = [state_grad[head] for head in every]
    blocks = TILE // SPAN
    parts = [[None] * blocks for _ in every]
    for block in range(blocks - 1, -1, -1):
        start = block * SPAN
        carry_s = [split(c) for c in carry]
        fresh_grad = [
            fresh_grad_in[h][start : start + SPAN]
            + product(rows_of(key_s[h], start, SPAN), carry_s[h], NN)
            for h in every
        ]
        fresh_grad_s = [split(f) for f in fresh_grad]
        out_rows = [rows_of(out_grad_s[h], start, SPAN) for h in every]
        carry = [
            carry[h]
            + (
                product(rows_of(query_s[h], start, SPAN), out_rows[h], TN)
                - product(rows_of(weights_s[h], start, SPAN), fresh_grad_s[h], TN)
            )
            for h in every
        ]
        for h in every:
            stacked = tuple(
                jnp.concatenate([a, b], 0) for a, b in zip(out_rows[h], fresh_grad_s[h])
            )
            back = product(stacked, split(state_ref[block, h]), NT)
            through = product(rows_of(fresh_s[h], start, SPAN), carry_s[h], NT)
            parts[h][block] = (fresh_grad[h], back[:SPAN], -back[SPAN:], through)
    for h in every:
        state_grad[h] = carry[h]
    scores_grad_s = [
        split(jnp.where(within, product(out_grad_s[h], fresh_s[h], NT), 0.0)) for h in every
    ]
    joined = [
        [jnp.concatenate([part[i] for part in parts[h]], 0) for i in range(4)] for h in every
    ]
    query_grad = [joined[h][1] + product(scores_grad_s[h], key_s[h], NN) for h in every]
    key_grad = [joined[h][3] + product(scores_grad_s[h], query_s[h], TN) for h in every]
    right_grad = [
        product(
            split(inverse_ref[h]),
            split(jnp.concatenate([joined[h][2], joined[h][0]], 1)),
            TN,
        )
        for h in every
    ]
    lower_grad_s = [
        split(jnp.where(below, -product(split(right_grad[h]), both_s[h], NT), 0.0)) for h in every
    ]
    key_beta_grad = [
        right_grad[h][:, :HEAD_DIM] + product(lower_grad_s[h], key_s[h], NN) for h in every
    ]
    key_grad = [
        key_grad[h]
        + product(lower_grad_s[h], split(key[h] * beta[h]), TN)
        + key_beta_grad[h] * beta[h]
        for h in every
    ]
    for h, lo in enumerate(at):
        value_beta_grad = right_grad[h][:, HEAD_DIM:]
        beta_grad = jnp.sum(
            key_beta_grad[h] * key[h] + value_beta_grad * value[h], -1, keepdims=True
        )
        beta_grad = beta_grad * (beta[h] * (1.0 - beta[h]))
        beta_grads = jnp.where(lane == h, beta_grad, beta_grads)
        query_back = unit_back(query_raw[h], query_scale[h], query_grad[h] * HEAD_DIM ** (-0.5))
        key_back = unit_back(key_raw[h], key_scale[h], key_grad[h])
        for index, grad in enumerate((query_back, key_back, value_beta_grad * beta[h])):
            first = index * wide + h * HEAD_DIM
            grad_buf[0:TILE, first : first + HEAD_DIM] = grad * slope[:, first : first + HEAD_DIM]
    raw_grad_ref[:, 4 * wide :] = beta_grads.astype(BF16)
    gain_grad_ref[0:1, :] += gain_total
    taps = conv_ref[...]
    here = grad_buf[0:TILE, :]
    total = taps[3:4] * here
    conv_grad_ref[3:4, :] += jnp.sum(here * rows_buf[8 : 8 + TILE, :], 0, keepdims=True)
    for offset in range(3):
        total = total + taps[offset : offset + 1] * grad_buf[pl.ds(3 - offset, TILE), :]
        conv_grad_ref[offset : offset + 1, :] += jnp.sum(
            here * rows_buf[pl.ds(5 + offset, TILE), :], 0, keepdims=True
        )
    raw_grad_ref[:, : 3 * wide] = total.astype(BF16)
    run_errands(errands, plan, step, True)


def mixer_backward(
    proj, conv, gain, grad, wu, fresh, out, states, inverses, heads,
    errands=(), plan=(), collective_id=None,
):
    rows = proj.shape[0]
    wide = heads * HEAD_DIM
    tiles = SEQ_LEN // TILE
    seqs = rows // SEQ_LEN
    blocks = TILE // SPAN

    def index(seq, step):
        return seq * tiles + tiles - 1 - step

    def at(seq, step):
        return (index(seq, step), 0)

    def ahead(seq, step):
        return (jnp.maximum(index(seq, step) * (TILE // 8) - 1, 0), 0)

    def fixed(seq, step):
        return (0, 0)

    kinds, sources, specs, shapes, scratch = errand_operands(errands)
    return pl.pallas_call(
        functools.partial(mixer_backward_body, heads, kinds, plan),
        grid=(seqs, tiles),
        in_specs=[
            pl.BlockSpec((TILE, proj.shape[1]), at),
            pl.BlockSpec((8, proj.shape[1]), ahead),
            pl.BlockSpec(conv.shape, fixed),
            pl.BlockSpec(gain.shape, fixed),
            pl.BlockSpec((TILE, wide), at),
            pl.BlockSpec((TILE, 2 * wide), at),
            pl.BlockSpec((TILE, wide), at),
            pl.BlockSpec((TILE, wide), at),
            pl.BlockSpec(
                (blocks, heads, HEAD_DIM, HEAD_DIM), lambda s, t: (index(s, t), 0, 0, 0)
            ),
            pl.BlockSpec((None, heads, TILE, TILE), lambda s, t: (index(s, t), 0, 0, 0)),
            *specs,
        ],
        out_specs=[
            pl.BlockSpec((TILE, 4 * wide + 128), at),
            pl.BlockSpec((8, 3 * wide), fixed),
            pl.BlockSpec((8, HEAD_DIM), fixed),
            *specs,
        ],
        out_shape=[
            jax.ShapeDtypeStruct((rows, 4 * wide + 128), BF16),
            jax.ShapeDtypeStruct((8, 3 * wide), F32),
            jax.ShapeDtypeStruct((8, HEAD_DIM), F32),
            *shapes,
        ],
        scratch_shapes=[
            pltpu.VMEM((TILE + 8, 3 * wide), F32),
            pltpu.VMEM((TILE + 8, 3 * wide), F32),
            pltpu.VMEM((heads, HEAD_DIM, HEAD_DIM), F32),
            *scratch,
        ],
        compiler_params=mixer_params(errands, collective_id),
        name="mixer_backward",
    )(proj, proj, conv, gain, grad, wu, fresh, out, states, inverses, *sources)


MESH = pl.DeviceIdType.MESH


def place():
    return lax.axis_index("core"), lax.axis_index("zl"), lax.axis_index("x")


def slot_of(core, deep, wide):
    own_core, own_deep, own_wide = place()
    return (
        jnp.where(core, 1 - own_core, own_core) * 4
        + jnp.where(deep, 1 - own_deep, own_deep) * 2
        + jnp.where(wide, 1 - own_wide, own_wide)
    )


def is_moved():
    return lax.axis_index("core") != lax.axis_index("zh")


def greet(everyone=False):
    barrier = pltpu.get_barrier_semaphore()
    axes = ("core", "zl", "x", "y", "zh") if everyone else ("core", "zl", "x")
    for axis in axes:
        pl.semaphore_signal(barrier, inc=1, device_id=neighbour(axis), device_id_type=MESH)
    peers = len(axes)
    if everyone:
        pl.when(is_moved())(
            lambda: pl.semaphore_signal(
                barrier, inc=1, device_id=partner(), device_id_type=MESH
            )
        )
        peers = peers + is_moved().astype(jnp.int32)
    pl.semaphore_wait(barrier, peers)


def partner():
    return {"core": lax.axis_index("zh"), "zh": lax.axis_index("core")}


def row_half(ref, index):
    rows = ref.shape[0] // 2
    return ref.at[pl.ds(pl.multiple_of(index * rows, 16), rows)]


class Errand:
    sems = 1
    buffers = 1

    def __init__(self, source, target, send, recv, local, buffers=()):
        self.source, self.target, self.held = source, target, buffers
        self.stage = buffers[0] if buffers else None
        self.send, self.recv, self.local = send, recv, local
        self.y = lax.axis_index("y")

    def remote(self, index, source, target, device):
        return pltpu.make_async_remote_copy(
            src_ref=source, dst_ref=target, send_sem=self.send.at[index],
            recv_sem=self.recv.at[index], device_id=device, device_id_type=MESH,
        )

    @staticmethod
    def buffer_shape(shape):
        return shape

    def stays(self, action):
        pl.when(jnp.logical_not(is_moved()))(action)

    def own_target(self):
        return self.target

    def here(self):
        source = self.source if self.stage is None else self.stage
        return pltpu.make_async_copy(source, self.own_target(), self.local)

    def stage_in(self):
        return pltpu.make_async_copy(self.source, self.stage, self.local)

    def start_here(self):
        self.stays(lambda: (self.here() if self.stage is None else self.stage_in()).start())

    def pass_here(self):
        def action():
            self.stage_in().wait()
            self.here().start()

        if self.stage is not None:
            self.stays(action)

    def finish_here(self):
        self.stays(lambda: self.here().wait())


class Exchange(Errand):
    def far(self):
        return self.remote(0, self.source, self.target, partner())

    def start(self):
        pl.when(is_moved())(lambda: self.far().start())
        self.start_here()

    def middle(self):
        self.pass_here()

    def finish(self):
        pl.when(is_moved())(lambda: self.far().wait())
        self.finish_here()


class Swap(Errand):
    sems = 4

    def piece(self, ref, owner, index):
        rows = ref.shape[0] // 4
        return ref.at[pl.ds(pl.multiple_of((owner * 2 + index) * rows, 16), rows)]

    def first(self, index):
        return self.remote(
            index, self.piece(self.source, self.y, index), self.piece(self.target, self.y, index),
            partner(),
        )

    def second(self, index, landing=False):
        half = self.piece(self.target, 1 - self.y if landing else self.y, index)
        return self.remote(2 + index, half, half, neighbour("y"))

    def start(self):
        @pl.when(is_moved())
        def _():
            self.first(0).start()
            self.first(1).start()

        self.start_here()

    def pass_piece(self, index):
        @pl.when(is_moved())
        def _():
            self.first(index).wait_recv()
            self.second(index).start()

    def early(self):
        self.pass_piece(0)
        self.pass_here()

    def late(self):
        self.pass_piece(1)

    def middle(self):
        self.early()
        self.late()

    def finish(self):
        @pl.when(is_moved())
        def _():
            for index in range(2):
                self.first(index).wait_send()
                self.second(index).wait_send()
                self.second(index, True).wait_recv()

        self.finish_here()


class HalfOverY(Errand):
    buffers = 0

    def copy(self):
        return self.remote(0, row_half(self.source, 1 - self.y), self.target, neighbour("y"))

    def start(self):
        self.copy().start()

    def middle(self):
        pass

    def finish(self):
        self.copy().wait()


class Across(Errand):
    buffers = 0

    def copy(self):
        return self.remote(0, self.source, self.target, neighbour("zh"))

    def start(self):
        pl.when(is_moved())(lambda: self.copy().start())

    def middle(self):
        pass

    def finish(self):
        pl.when(is_moved())(lambda: self.copy().wait_send())
        self.stays(lambda: self.copy().wait_recv())


SCATTER_CUT = 192


class Gather(Errand):
    sems = 11

    def ring(self):
        return Ring(self.target, self.send, self.recv, 32, self.stage)

    def own(self):
        return pltpu.make_async_copy(self.stage, self.target.at[slot_of(0, 0, 0)], self.local)

    def start(self):
        self.stage_in().start()
        self.stage_in().wait()
        self.own().start()
        self.ring().launch(0, 1, 2, 3, 4)

    def early(self):
        ring = self.ring()
        ring.arrived(0)
        ring.launch(5)
        ring.arrived(1)
        ring.launch(6)

    def middle(self):
        ring = self.ring()
        ring.arrived(2)
        ring.launch(7)
        ring.arrived(3)
        ring.launch(8)

    def late(self):
        ring = self.ring()
        ring.arrived(5)
        ring.launch(9)
        ring.arrived(6)
        ring.launch(10)

    def finish(self):
        ring = self.ring()
        ring.arrived(4, 7, 8, 9, 10)
        ring.finish()
        self.own().wait()


class Spread(Errand):
    sems = 3

    def own_target(self):
        return row_half(self.target, self.y)

    def over(self):
        return self.remote(0, self.source, self.own_target(), neighbour("y"))

    def other(self, index, axis):
        view = row_half(self.target, 1 - self.y)
        return self.remote(index, view, view, neighbour(axis))

    def cross(self):
        return self.remote(1, self.source, self.own_target(), neighbour("core"))

    def start(self):
        @pl.when(jnp.logical_not(is_moved()))
        def _():
            self.over().start()
            self.cross().start()

        self.start_here()

    def middle(self):
        @pl.when(jnp.logical_not(is_moved()))
        def _():
            self.other(0, "y").wait_recv()
            self.other(2, "core").start()

        self.pass_here()

    def finish(self):
        @pl.when(jnp.logical_not(is_moved()))
        def _():
            self.over().wait_send()
            self.cross().wait_send()
            self.other(2, "core").wait_send()

        @pl.when(is_moved())
        def _():
            self.cross().wait_recv()
            self.other(2, "core").wait_recv()

        self.finish_here()


class Chain(Errand):
    sems = 5
    buffers = 2

    def mine(self):
        return self.held[0]

    def load(self):
        return pltpu.make_async_copy(self.source, self.mine(), self.local)

    def across(self):
        return self.remote(0, self.mine(), self.held[1], neighbour("zh"))

    def own_rows(self):
        return row_half(self.target, self.y)

    def near(self):
        return pltpu.make_async_copy(self.mine(), self.own_rows(), self.local)

    def over(self):
        return self.remote(1, self.mine(), self.own_rows(), neighbour("y"))

    def cross(self):
        return self.remote(2, self.mine(), self.own_rows(), neighbour("core"))

    def other(self, index, axis):
        view = row_half(self.target, 1 - self.y)
        return self.remote(index, view, view, neighbour(axis))

    def add(self, more):
        mine = self.mine()
        mine[...] = (mine[...].astype(F32) + more[...].astype(F32)).astype(BF16)

    def start(self):
        self.load().start()

    def launch(self):
        self.load().wait()
        pl.when(is_moved())(lambda: self.across().start())

    def settle(self):
        @pl.when(jnp.logical_not(is_moved()))
        def _():
            self.across().wait_recv()
            self.add(self.held[1])
            self.over().start()
            self.cross().start()
            self.near().start()

    def settle_late(self):
        self.settle()

    def forward(self):
        @pl.when(jnp.logical_not(is_moved()))
        def _():
            self.other(1, "y").wait_recv()
            self.other(3, "core").start()

    def finish(self):
        @pl.when(jnp.logical_not(is_moved()))
        def _():
            self.near().wait()
            self.over().wait_send()
            self.cross().wait_send()
            self.other(3, "core").wait_send()

        @pl.when(is_moved())
        def _():
            self.across().wait_send()
            self.cross().wait_recv()
            self.other(3, "core").wait_recv()


class FullChain(Chain):
    buffers = 3

    @staticmethod
    def buffer_shape(shape):
        return (shape[0] // 2, *shape[1:])

    def load(self):
        return pltpu.make_async_copy(row_half(self.source, self.y), self.mine(), self.local)

    def halves(self):
        return self.remote(4, row_half(self.source, 1 - self.y), self.held[2], neighbour("y"))

    def start(self):
        self.halves().start()
        self.load().start()

    def launch(self):
        self.load().wait()
        self.halves().wait()
        self.add(self.held[2])
        pl.when(is_moved())(lambda: self.across().start())


def errand_target(kind, source):
    if kind is Gather:
        return jax.ShapeDtypeStruct((8, *source.shape), source.dtype)
    rows = source.shape[0]
    rows = {HalfOverY: rows // 2, Spread: 2 * rows, Chain: 2 * rows}.get(kind, rows)
    return jax.ShapeDtypeStruct((rows, *source.shape[1:]), source.dtype)


def errand_scratch(kinds, sources=()):
    total = max(1, sum(kind.sems for kind in kinds))
    places = [
        pltpu.VMEM(kind.buffer_shape(source.shape), BF16)
        for kind, source in zip(kinds, sources)
        for _ in range(kind.buffers)
    ]
    return [
        *places,
        pltpu.SemaphoreType.DMA((total,)),
        pltpu.SemaphoreType.DMA((total,)),
        pltpu.SemaphoreType.DMA((max(1, len(kinds)),)),
    ]


def make_errands(kinds, sources, targets, send, recv, local, places=()):
    made, at, used = [], 0, 0
    for index, (kind, source, target) in enumerate(zip(kinds, sources, targets)):
        view = pl.ds(at, kind.sems)
        held = places[used : used + kind.buffers] if places else ()
        made.append(kind(source, target, send.at[view], recv.at[view], local.at[index], held))
        at += kind.sems
        used += kind.buffers
    return made


def neighbour(axis):
    return {axis: 1 - lax.axis_index(axis)}


def column_tile(columns):
    for size in (512, 384, 256, 128):
        if columns % size == 0:
            return size
    return columns


def column_parts(columns):
    tile = column_tile(columns)
    if tile != columns or columns <= 512:
        return [(0, tile, columns // tile)]
    whole = columns // 256 * 256
    return [(0, 256, whole // 256), (whole, columns - whole, 1)]


def by_columns(columns, body):
    for start, size, steps in column_parts(columns):
        if steps == 1:
            body(pl.ds(start, size))
        else:

            def column(step, _, start=start, size=size):
                body(pl.ds(pl.multiple_of(start + step * size, 128), size))
                return 0

            lax.fori_loop(0, steps, column, 0)


def take_errands(kinds, refs, inputs, outputs):
    extra = len(kinds)
    sources = refs[inputs : inputs + extra]
    targets = refs[inputs + extra + outputs : inputs + 2 * extra + outputs]
    last = len(refs) - 3 - sum(kind.buffers for kind in kinds)
    errands = make_errands(kinds, sources, targets, *refs[-3:], refs[last:-3])
    rest = (
        *refs[:inputs], *refs[inputs + extra : inputs + extra + outputs],
        *refs[inputs + 2 * extra + outputs : last],
    )
    return rest[0], rest[1:], errands


class Ring:
    def __init__(self, held, send, recv, cut=None, block=None):
        self.block = block
        self.held, self.send, self.recv = held, send, recv
        own, wide, deep, far = (slot_of(0, *at) for at in ((0, 0), (0, 1), (1, 0), (1, 1)))
        rows = held.shape[1]
        cut = cut or rows // 2
        rest = rows - cut
        self.moves = (
            ("x", own, wide, 0, cut), ("zl", own, deep, cut, rest),
            ("x", own, wide, cut, rest), ("zl", own, deep, 0, cut),
            ("core", own, slot_of(1, 0, 0), 0, rows),
            ("zl", wide, far, 0, cut), ("x", deep, far, cut, rest),
            ("core", wide, slot_of(1, 0, 1), 0, rows),
            ("core", deep, slot_of(1, 1, 0), 0, rows),
            ("core", far, slot_of(1, 1, 1), 0, cut),
            ("core", far, slot_of(1, 1, 1), cut, rest),
        )

    def move(self, index, landing=False):
        axis, source, target, start, size = self.moves[index]
        view = self.held.at[target if landing else source, pl.ds(start, size)]
        from_block = self.block is not None and index < 5
        return pltpu.make_async_remote_copy(
            src_ref=self.block.at[pl.ds(start, size)] if from_block else view,
            dst_ref=view, send_sem=self.send.at[index],
            recv_sem=self.recv.at[index], device_id=neighbour(axis), device_id_type=MESH,
        )

    def launch(self, *indices):
        for index in indices:
            self.move(index).start()

    def arrived(self, *indices):
        for index in indices:
            self.move(index, True).wait_recv()

    def run(self, work, beside):
        self.launch(0, 1, 2, 3, 4)
        beside(0)
        work(slot_of(0, 0, 0))
        self.arrived(4)
        work(slot_of(1, 0, 0))
        beside(1)
        self.arrived(0)
        self.launch(5)
        self.arrived(1)
        self.launch(6)
        self.arrived(2)
        self.launch(7)
        self.arrived(3)
        self.launch(8)
        work(slot_of(0, 0, 1))
        work(slot_of(0, 1, 0))
        self.arrived(7)
        work(slot_of(1, 0, 1))
        self.arrived(8)
        work(slot_of(1, 1, 0))
        beside(2)
        self.arrived(5)
        self.launch(9)
        self.arrived(6)
        self.launch(10)
        work(slot_of(0, 1, 1))
        self.arrived(9, 10)
        work(slot_of(1, 1, 1))

    def finish(self):
        for index in range(len(self.moves)):
            self.move(index).wait_send()


def ring_scratch(rows, depth):
    return [
        pltpu.VMEM((8, rows, depth), BF16),
        pltpu.SemaphoreType.DMA((11,)),
        pltpu.SemaphoreType.DMA((11,)),
    ]


class Stores:
    def __init__(self, sems):
        self.sems, self.made = sems, []

    def add(self, source, target):
        copy = pltpu.make_async_copy(source, target, self.sems.at[len(self.made)])
        copy.start()
        self.made.append(copy)

    def finish(self):
        for copy in self.made:
            copy.wait()


def run_beside(errands, starts, middles):
    def beside(point):
        for errand in errands:
            if point == starts:
                errand.start()
            if point == middles:
                errand.middle()

    return beside


def gather_body(dims, count, kinds, *refs):
    block_ref, refs, errands = take_errands(kinds, refs, 1 + count, 1 + count)
    weight_refs, gathered_ref, product_refs = refs[:count], refs[count], refs[count + 1 : 2 * count + 1]
    held, send, recv = refs[2 * count + 1 : 2 * count + 4]
    weights, results = refs[2 * count + 4 : 3 * count + 4], refs[3 * count + 4 : 4 * count + 4]
    (local,) = refs[4 * count + 4 :]
    own = slot_of(0, 0, 0)
    loads = [pltpu.make_async_copy(block_ref, held.at[own], local.at[0])]
    for i, (ref, weight) in enumerate(zip(weight_refs, weights)):
        loads.append(pltpu.make_async_copy(ref, weight, local.at[1 + i]))
    for load in loads:
        load.start()
    greet(bool(kinds))
    for load in loads:
        load.wait()
    ring = Ring(held, send, recv, None)
    stores = Stores(local.at[pl.ds(1 + count, 8 * (1 + count))])

    def work(slot):
        stores.add(held.at[slot], gathered_ref.at[slot])
        for weight, result, product_ref in zip(weights, results, product_refs):

            def column(at):
                right = weight[:, at] if dims == NN else weight[at, :]
                result[slot, :, at] = dot(held[slot], right, dims).astype(result.dtype)

            by_columns(result.shape[2], column)
            stores.add(result.at[slot], product_ref.at[slot])

    ring.run(work, run_beside(errands, 0, 2))
    ring.finish()
    stores.finish()
    for errand in errands:
        errand.finish()


def gather_multiply(block, weights, dims, collective_id, name, errands=(), out_type=F32):
    rows, depth = block.shape
    widths = [w.shape[1] if dims == NN else w.shape[0] for w in weights]
    count = len(weights)
    kinds, sources = [e[0] for e in errands], [e[1] for e in errands]
    gathered, *products = pl.pallas_call(
        functools.partial(gather_body, dims, count, kinds),
        in_specs=[pl.BlockSpec(memory_space=pl.ANY)] * (1 + count + len(kinds)),
        out_specs=[pl.BlockSpec(memory_space=pl.ANY)] * (1 + count + len(kinds)),
        out_shape=[jax.ShapeDtypeStruct((8, rows, depth), BF16)]
        + [jax.ShapeDtypeStruct((8, rows, width), out_type) for width in widths]
        + [errand_target(*errand) for errand in errands],
        scratch_shapes=ring_scratch(rows, depth)
        + [pltpu.VMEM(w.shape, BF16) for w in weights]
        + [pltpu.VMEM((8, rows, width), out_type) for width in widths]
        + [
            pltpu.SemaphoreType.DMA((1 + count + 8 * (1 + count),)),
            *errand_scratch(kinds, sources),
        ],
        compiler_params=pltpu.CompilerParams(
            collective_id=collective_id, has_side_effects=True, vmem_limit_bytes=56 * 2**20
        ),
        name=name,
    )(block, *weights, *sources)
    flat = [v.reshape(8 * rows, v.shape[2]) for v in (gathered, *products[:count])]
    return (*flat, *products[count:])


def feed_body(kinds, *refs):
    block_ref, refs, errands = take_errands(kinds, refs, 5, 4)
    sources, refs = refs[:4], refs[4:]
    gathered_ref, hidden_ref, gate_grad_ref, up_grad_ref, *refs = refs
    held, send, recv, w_gate, w_up, w_down, grads, hidden_grad, hidden, gate_grad, up_grad = refs[:11]
    (local,) = refs[11:]
    own = slot_of(0, 0, 0)
    loads = [pltpu.make_async_copy(block_ref, held.at[own], local.at[0])]
    for i, (source, target) in enumerate(zip(sources, (w_gate, w_up, w_down, grads))):
        loads.append(pltpu.make_async_copy(source, target, local.at[1 + i]))
    for load in loads:
        load.start()
    greet(bool(kinds))
    for load in loads:
        load.wait()
    ring = Ring(held, send, recv)
    stores = Stores(local.at[pl.ds(5, 32)])
    units = hidden.shape[2]

    def back(slot):
        def column(at):
            hidden_grad[slot, :, at] = dot(grads[slot], w_down[at, :], NT)

        by_columns(units, column)

    def work(slot):
        stores.add(held.at[slot], gathered_ref.at[slot])

        def column(at):
            gate = dot(held[slot], w_gate[at, :], NT)
            up = dot(held[slot], w_up[at, :], NT)
            smooth = sigmoid(gate)
            active = gate * smooth
            grad = hidden_grad[slot, :, at]
            hidden[slot, :, at] = (active * up).astype(BF16)
            gate_grad[slot, :, at] = (grad * up * smooth * (1.0 + gate * (1.0 - smooth))).astype(BF16)
            up_grad[slot, :, at] = (grad * active).astype(BF16)

        by_columns(units, column)
        stores.add(hidden.at[slot], hidden_ref.at[slot])
        stores.add(gate_grad.at[slot], gate_grad_ref.at[slot])
        stores.add(up_grad.at[slot], up_grad_ref.at[slot])

    def beside(point):
        for errand in errands:
            if point == 0:
                errand.start()
            elif point == 2:
                errand.middle()
        if point == 0:
            back(slot_of(0, 0, 0))
            back(slot_of(1, 0, 0))
        elif point == 1:
            for at in ((0, 0, 1), (0, 1, 0), (1, 0, 1), (1, 1, 0), (0, 1, 1), (1, 1, 1)):
                back(slot_of(*at))

    ring.run(work, beside)
    ring.finish()
    stores.finish()
    for errand in errands:
        errand.finish()


def feed(block, w_gate, w_up, w_down, grads, collective_id, errands=()):
    rows, depth = block.shape
    units = w_gate.shape[0]
    kinds, sources = [e[0] for e in errands], [e[1] for e in errands]
    hbm = pl.BlockSpec(memory_space=pl.ANY)
    by_unit = jax.ShapeDtypeStruct((8, rows, units), BF16)
    gathered, *parts = pl.pallas_call(
        functools.partial(feed_body, kinds),
        in_specs=[hbm] * (5 + len(kinds)),
        out_specs=[hbm] * (4 + len(kinds)),
        out_shape=[jax.ShapeDtypeStruct((8, rows, depth), BF16), by_unit, by_unit, by_unit]
        + [errand_target(*errand) for errand in errands],
        scratch_shapes=[
            *ring_scratch(rows, depth),
            *[pltpu.VMEM(w_gate.shape, BF16)] * 3,
            pltpu.VMEM((8, rows, depth), BF16),
            pltpu.VMEM((8, rows, units), F32),
            *[pltpu.VMEM((8, rows, units), BF16)] * 3,
            pltpu.SemaphoreType.DMA((37,)),
            *errand_scratch(kinds, sources),
        ],
        compiler_params=pltpu.CompilerParams(
            collective_id=collective_id, has_side_effects=True, vmem_limit_bytes=58 * 2**20
        ),
        name="feed",
    )(block, w_gate, w_up, w_down, grads, *sources)
    flat = [v.reshape(8 * rows, v.shape[2]) for v in (gathered, *parts[:3])]
    return (*flat, *parts[3:])


def block_of(ref, slot, rows):
    if len(ref.shape) == 3:
        return ref[slot]
    return ref[pl.ds(pl.multiple_of(slot * rows, rows), rows)]


def scatter_core(dims, lefts, weights, buffers, beside, cut=None):
    sending, crossing, partial, far_recv, side_recv, total, send, recv = buffers
    rows, width = total.shape
    cut = cut or rows // 2

    def move(index, axis, src, dst):
        return pltpu.make_async_remote_copy(
            src_ref=src, dst_ref=dst, send_sem=send.at[index], recv_sem=recv.at[index],
            device_id=neighbour(axis), device_id_type=MESH,
        )

    sends = []

    def launch(*args):
        copy = move(*args)
        copy.start()
        sends.append(copy)

    def multiply(slot, write):
        def column(at):
            value = None
            for left, weight in zip(lefts, weights):
                right = weight[:, at] if dims == NN else weight[at, :]
                term = dot(block_of(left, slot, rows), right, dims)
                value = term if value is None else value + term
            write(at, value)

        by_columns(width, column)

    places = ((1, 1), (0, 1), (1, 0), (0, 0))

    def cross(index):
        def write(at, value):
            sending[index, :, at] = value.astype(BF16)

        multiply(slot_of(1, *places[index]), write)
        launch(index, "core", sending.at[index], crossing.at[index])

    def crossed(index):
        move(index, "core", sending.at[index], crossing.at[index]).wait_recv()

    def local_sum(index):
        crossed(index)

        def write(at, value):
            partial[index, :, at] = (value + crossing[index, :, at].astype(F32)).astype(BF16)

        multiply(slot_of(0, *places[index]), write)

    first, second = pl.ds(0, cut), pl.ds(cut, rows - cut)
    cross(0)
    beside(0)
    cross(1)
    local_sum(0)
    launch(4, "x", partial.at[0, first], far_recv.at[0, first])
    launch(5, "zl", partial.at[0, second], far_recv.at[1, second])
    beside("far sent")
    cross(2)
    local_sum(1)
    launch(6, "x", partial.at[1, first], side_recv.at[0, first])
    local_sum(2)
    launch(7, "zl", partial.at[2, second], side_recv.at[1, second])
    beside("side sent")
    cross(3)
    beside(1)
    move(4, "x", partial.at[0, first], far_recv.at[0, first]).wait_recv()
    partial[2, first] = (partial[2, first].astype(F32) + far_recv[0, first].astype(F32)).astype(BF16)
    launch(8, "zl", partial.at[2, first], side_recv.at[1, first])
    move(5, "zl", partial.at[0, second], far_recv.at[1, second]).wait_recv()
    partial[1, second] = (partial[1, second].astype(F32) + far_recv[1, second].astype(F32)).astype(BF16)
    launch(9, "x", partial.at[1, second], side_recv.at[0, second])
    beside(2)
    crossed(3)

    def write(at, value):
        total[:, at] = value + crossing[3, :, at].astype(F32)

    multiply(slot_of(0, 0, 0), write)
    move(6, "x", partial.at[1, first], side_recv.at[0, first]).wait_recv()
    total[first] += side_recv[0, first].astype(F32)
    move(7, "zl", partial.at[2, second], side_recv.at[1, second]).wait_recv()
    total[second] += side_recv[1, second].astype(F32)
    beside(3)
    move(8, "zl", partial.at[2, first], side_recv.at[1, first]).wait_recv()
    total[first] += side_recv[1, first].astype(F32)
    move(9, "x", partial.at[1, second], side_recv.at[0, second]).wait_recv()
    total[second] += side_recv[0, second].astype(F32)
    return sends


def scatter_scratch(rows, width):
    return [
        pltpu.VMEM((4, rows, width), BF16),
        pltpu.VMEM((4, rows, width), BF16),
        pltpu.VMEM((3, rows, width), BF16),
        pltpu.VMEM((2, rows, width), BF16),
        pltpu.VMEM((2, rows, width), BF16),
        pltpu.VMEM((rows, width), F32),
        pltpu.SemaphoreType.DMA((10,)),
        pltpu.SemaphoreType.DMA((10,)),
    ]


def scatter_body(dims, count, kinds, *refs):
    first_ref, refs, errands = take_errands(kinds, refs, 2 * count, 1)
    refs = (first_ref, *refs)
    total_ref = refs[2 * count]
    operands = refs[2 * count + 1 : 4 * count + 1]
    buffers, local = refs[4 * count + 1 : -1], refs[-1]
    loads = [
        pltpu.make_async_copy(ref, operand, local.at[i])
        for i, (ref, operand) in enumerate(zip(refs[: 2 * count], operands))
    ]
    for load in loads:
        load.start()
    greet(bool(kinds))
    for load in loads:
        load.wait()

    def beside(point):
        for errand in errands:
            if point == 0:
                errand.start()
            elif point == 2 and hasattr(errand, "early"):
                errand.early()
            elif point == 3:
                errand.late() if hasattr(errand, "early") else errand.middle()

    cut = SCATTER_CUT if Across in kinds or Swap in kinds else None
    sends = scatter_core(dims, operands[:count], operands[count:], buffers, beside, cut)
    store = pltpu.make_async_copy(buffers[5], total_ref, local.at[2 * count])
    store.start()
    for copy in sends:
        copy.wait_send()
    store.wait()
    for errand in errands:
        errand.finish()


def multiply_scatter(lefts, weights, dims, collective_id, name, errands=()):
    rows = lefts[0].shape[0] // 8
    width = weights[0].shape[1] if dims == NN else weights[0].shape[0]
    count = len(lefts)
    lefts = [left.reshape(8, rows, left.shape[1]) for left in lefts]
    kinds, sources = [e[0] for e in errands], [e[1] for e in errands]
    return pl.pallas_call(
        functools.partial(scatter_body, dims, count, kinds),
        in_specs=[pl.BlockSpec(memory_space=pl.ANY)] * (2 * count + len(kinds)),
        out_specs=[pl.BlockSpec(memory_space=pl.ANY)] * (1 + len(kinds)),
        out_shape=[jax.ShapeDtypeStruct((rows, width), F32)]
        + [errand_target(*errand) for errand in errands],
        scratch_shapes=[pltpu.VMEM(v.shape, BF16) for v in (*lefts, *weights)]
        + [
            *scatter_scratch(rows, width),
            pltpu.SemaphoreType.DMA((2 * count + 1,)),
            *errand_scratch(kinds, sources),
        ],
        compiler_params=pltpu.CompilerParams(
            collective_id=collective_id, has_side_effects=True, vmem_limit_bytes=56 * 2**20
        ),
        name=name,
    )(*lefts, *weights, *sources)


def begin_body(kinds, *refs):
    tokens_ref, refs, errands = take_errands(kinds, refs, 8, 5)
    gain_ref, conv_ref, *refs = refs
    weight_refs, refs = refs[:5], refs[5:]
    moved_ref, gathered_ref, product_ref, weights_ref, new_conv_ref, *refs = refs
    tokens, held, weights, result, send, recv, errand_send, errand_recv, local = refs
    rows = tokens_ref.shape[0]
    half = rows // 2
    starts = [0]
    for ref in weight_refs:
        starts.append(starts[-1] + ref.shape[1])
    parts = [pl.ds(start, ref.shape[1]) for start, ref in zip(starts, weight_refs)]
    greet(True)
    own_kinds = [Exchange, Exchange] + [Swap] * 5
    targets = [tokens, new_conv_ref] + [weights.at[:, part] for part in parts]
    block, taps, *swaps = make_errands(
        own_kinds, [tokens_ref, conv_ref, *weight_refs], targets, errand_send, errand_recv, local
    )
    block.start()
    taps.start()
    swaps[0].start()
    block.finish()
    for swap in swaps[1:]:
        swap.start()
    for errand in errands:
        errand.start()
    own = slot_of(0, 0, 0)
    values = tokens[...].astype(F32)
    scale = lax.rsqrt(jnp.mean(values * values, -1, keepdims=True) + 1e-05)
    held[own] = (values * scale * gain_ref[...]).astype(BF16)
    keep = pltpu.make_async_copy(tokens, moved_ref, local.at[7])
    keep.start()

    ring = Ring(held, send, recv)
    ring.launch(0, 1, 2, 3, 4)
    ring.arrived(0)
    ring.launch(5)
    ring.arrived(1)
    ring.launch(6)
    swaps[0].middle()
    ring.arrived(2)
    ring.launch(7)
    ring.arrived(3)
    ring.launch(8)
    swaps[1].middle()
    ring.arrived(5)
    ring.launch(9)
    ring.arrived(6)
    ring.launch(10)
    ring.arrived(4, 7, 8, 9, 10)
    store = pltpu.make_async_copy(held, gathered_ref, local.at[8])
    store.start()
    stores = []
    for index, (swap, part) in enumerate(zip(swaps, parts)):
        if index + 2 < len(swaps):
            swaps[index + 2].middle()
        swap.finish()
        if index == len(swaps) - 1:
            for errand in errands:
                errand.middle()

        def multiply(slot, _, part=part):
            result[slot, :, part] = dot(held[slot], weights[:, part], NN)
            return 0

        lax.fori_loop(0, 8, multiply, 0)
        for view, out, sem in (
            (result.at[:, :, part], product_ref.at[:, :, part], 9 + 2 * index),
            (weights.at[:, part], weights_ref.at[:, part], 10 + 2 * index),
        ):
            copy = pltpu.make_async_copy(view, out, local.at[sem])
            copy.start()
            stores.append(copy)
    taps.finish()
    ring.finish()
    keep.wait()
    store.wait()
    for copy in stores:
        copy.wait()
    for errand in errands:
        errand.finish()


def begin(tokens, gain, conv, weights, collective_id, errands=()):
    rows, depth = tokens.shape
    width = sum(w.shape[1] for w in weights)
    kinds, sources = [e[0] for e in errands], [e[1] for e in errands]
    hbm = pl.BlockSpec(memory_space=pl.ANY)
    moved, gathered, product, weights, conv, *more = pl.pallas_call(
        functools.partial(begin_body, kinds),
        in_specs=[hbm, pl.BlockSpec(memory_space=pltpu.VMEM)]
        + [hbm] * (1 + len(weights) + len(kinds)),
        out_specs=[hbm] * (5 + len(kinds)),
        out_shape=[
            jax.ShapeDtypeStruct(tokens.shape, BF16),
            jax.ShapeDtypeStruct((8, rows, depth), BF16),
            jax.ShapeDtypeStruct((8, rows, width), F32),
            jax.ShapeDtypeStruct((depth, width), BF16),
            jax.ShapeDtypeStruct(conv.shape, conv.dtype),
            *[errand_target(*errand) for errand in errands],
        ],
        scratch_shapes=[
            pltpu.VMEM((rows, depth), BF16),
            pltpu.VMEM((8, rows, depth), BF16),
            pltpu.VMEM((depth, width), BF16),
            pltpu.VMEM((8, rows, width), F32),
            pltpu.SemaphoreType.DMA((11,)),
            pltpu.SemaphoreType.DMA((11,)),
            pltpu.SemaphoreType.DMA((22,)),
            pltpu.SemaphoreType.DMA((22,)),
            pltpu.SemaphoreType.DMA((19,)),
            *errand_scratch(kinds, sources),
        ],
        compiler_params=pltpu.CompilerParams(
            collective_id=collective_id, has_side_effects=True, vmem_limit_bytes=56 * 2**20
        ),
        name="begin",
    )(tokens, gain, conv, *weights, *sources)
    flat = gathered.reshape(8 * rows, depth), product.reshape(8 * rows, width)
    return (moved, *flat, weights, conv, *more)


def turned_product(turned, right, out, columns):
    def column(at):
        out[:, at] = dot(turned[...], right[:, at], NN).astype(BF16)

    by_columns(columns, column)


def mlp_body(kinds, *refs):
    first_ref, refs, errands = take_errands(kinds, refs, 6, 5)
    sources, refs = (first_ref, *refs[:5]), refs[5:]
    total_ref, down_ref, gate_ref, up_ref, came_ref, *refs = refs
    hidden, weight, rights, lefts, turned, outs = refs[:6]
    buffers, refs = refs[6:14], refs[14:]
    half_send, half_recv, local = refs
    hidden_ref, weight_ref, grads_ref, gate_grad_ref, up_grad_ref, rows_ref = sources

    def load(source, target, index):
        return pltpu.make_async_copy(source, target, local.at[index])

    early = [
        load(hidden_ref, hidden, 0), load(weight_ref, weight, 1), load(grads_ref, rights, 2),
        load(gate_grad_ref, lefts.at[0], 3), load(up_grad_ref, lefts.at[1], 4),
    ]
    reload = load(rows_ref, rights, 5)
    for copy in early:
        copy.start()
    greet(True)
    for copy in early:
        copy.wait()
    stores = Stores(local.at[pl.ds(6, 4)])
    rows = hidden.shape[1]
    columns = rights.shape[1]

    def turn(left):
        for slot in range(8):
            turned[:, slot * rows : (slot + 1) * rows] = left[slot].T

    y = lax.axis_index("y")
    half = pltpu.make_async_remote_copy(
        src_ref=row_half(outs.at[0], 1 - y), dst_ref=came_ref, send_sem=half_send.at[0],
        recv_sem=half_recv.at[0], device_id=neighbour("y"), device_id_type=MESH,
    )

    def beside(point):
        if point == 0:
            for errand in errands:
                errand.start()
        elif point == "side sent":
            turn(hidden)
            turned_product(turned, rights, outs.at[0], columns)
            reload.start()
            half.start()
            stores.add(outs.at[0], down_ref)
        elif point == 2:
            turn(lefts.at[0])
            reload.wait()
            turned_product(turned, rights, outs.at[1], columns)
            stores.add(outs.at[1], gate_ref)
            turn(lefts.at[1])
            turned_product(turned, rights, outs.at[2], columns)
            stores.add(outs.at[2], up_ref)
            for errand in errands:
                errand.middle()

    sends = scatter_core(NN, [hidden], [weight], buffers, beside)
    stores.add(buffers[5], total_ref)
    for copy in sends:
        copy.wait_send()
    half.wait()
    stores.finish()
    for errand in errands:
        errand.finish()


def mlp_scatter(hidden, weight, grads, gate_grad, up_grad, gathered, collective_id, errands=()):
    tokens, units = hidden.shape
    rows, depth = tokens // 8, weight.shape[1]
    kinds, sources = [e[0] for e in errands], [e[1] for e in errands]
    hbm = pl.BlockSpec(memory_space=pl.ANY)
    by_unit = jax.ShapeDtypeStruct(weight.shape, BF16)
    blocks = [v.reshape(8, rows, units) for v in (hidden, gate_grad, up_grad)]
    return pl.pallas_call(
        functools.partial(mlp_body, kinds),
        in_specs=[hbm] * (6 + len(kinds)),
        out_specs=[hbm] * (5 + len(kinds)),
        out_shape=[
            jax.ShapeDtypeStruct((rows, depth), F32), by_unit, by_unit, by_unit,
            jax.ShapeDtypeStruct((units // 2, depth), BF16),
            *[errand_target(*errand) for errand in errands],
        ],
        scratch_shapes=[
            pltpu.VMEM((8, rows, units), BF16),
            pltpu.VMEM(weight.shape, BF16),
            pltpu.VMEM((tokens, depth), BF16),
            pltpu.VMEM((2, 8, rows, units), BF16),
            pltpu.VMEM((units, tokens), BF16),
            pltpu.VMEM((3, *weight.shape), BF16),
            *scatter_scratch(rows, depth),
            pltpu.SemaphoreType.DMA((1,)),
            pltpu.SemaphoreType.DMA((1,)),
            pltpu.SemaphoreType.DMA((10,)),
            *errand_scratch(kinds, sources),
        ],
        compiler_params=pltpu.CompilerParams(
            collective_id=collective_id, has_side_effects=True, vmem_limit_bytes=60 * 2**20
        ),
        name="scatter_mlp",
    )(blocks[0], weight, grads, blocks[1], blocks[2], gathered, *sources)


CHUNKS = 8


def finish_body(kinds, *refs):
    first_ref, refs, errands = take_errands(kinds, refs, 8, 4)
    left_ref, (weight_ref, rows_ref, tokens_ref, resid_ref, gain_ref) = first_ref, refs[:5]
    small_refs, tokens_grad_ref, total_grad_ref = refs[5:7], *refs[7:9]
    taps_out_ref, gains_out_ref, *refs = refs[9:]
    left, weight, gathered, turned, mine, other, came, far, tokens = refs[:9]
    resid, moving, taps, taps_recv, gains, gains_recv, *refs = refs[9:]
    buffers, refs = refs[:8], refs[8:]
    chain_send, chain_recv, sum_send, sum_recv, move_send, move_recv, local = refs
    loads = [
        pltpu.make_async_copy(source, target, local.at[i])
        for i, (source, target) in enumerate(
            (
                (left_ref, left), (weight_ref, weight), (rows_ref, gathered), (tokens_ref, tokens),
                (resid_ref, resid), (small_refs[0], taps), (small_refs[1], gains),
            )
        )
    ]
    for load in loads:
        load.start()
    greet(True)
    y = lax.axis_index("y")
    moved = is_moved()
    stays = jnp.logical_not(moved)
    size = mine.shape[0] // CHUNKS

    def chain(stage, index, source, target, axis):
        return pltpu.make_async_remote_copy(
            src_ref=source, dst_ref=target, send_sem=chain_send.at[stage, index],
            recv_sem=chain_recv.at[stage, index], device_id=neighbour(axis), device_id_type=MESH,
        )

    def total_rows(index, owner):
        start = owner * (size * CHUNKS) + index * size
        return total_grad_ref.at[pl.ds(pl.multiple_of(start, 16), size)]

    def chunk(ref, index):
        return ref.at[pl.ds(index * size, size)]

    def over(index):
        return chain(0, index, chunk(other, index), chunk(came, index), "y")

    def across(index):
        return chain(1, index, chunk(mine, index), chunk(far, index), "zh")

    def back(index):
        return chain(2, index, chunk(mine, index), total_rows(index, y), "y")

    def landing(index):
        return chain(2, index, total_rows(index, 1 - y), total_rows(index, 1 - y), "y")

    def cross(index):
        return chain(3, index, chunk(mine, index), total_rows(index, y), "core")

    def pass_on(index):
        return chain(4, index, total_rows(index, 1 - y), total_rows(index, 1 - y), "core")

    def near(index):
        return pltpu.make_async_copy(chunk(mine, index), total_rows(index, y), local.at[8 + index])

    def add(index, source):
        at, more = chunk(mine, index), chunk(source, index)
        at[...] = (at[...].astype(F32) + more[...].astype(F32)).astype(BF16)

    def sum_y(index):
        over(index).wait_recv()
        add(index, came)
        pl.when(moved)(lambda: across(index).start())

    def sum_z(index):
        @pl.when(stays)
        def _():
            across(index).wait_recv()
            add(index, far)
            back(index).start()
            cross(index).start()
            near(index).start()

    def forward(index):
        @pl.when(stays)
        def _():
            landing(index).wait_recv()
            pass_on(index).start()

    def weight_grad(owner, index, target):
        start = pl.multiple_of(owner * (size * CHUNKS) + index * size, size)
        turned[...] = gathered[:, pl.ds(start, size)].T
        turned_product(turned, left, chunk(target, index), left.shape[1])

    def sum_step(values, received, first, axes, index):
        def round_of(index):
            return pltpu.make_async_remote_copy(
                src_ref=values, dst_ref=received.at[index], send_sem=sum_send.at[first + index],
                recv_sem=sum_recv.at[first + index], device_id=neighbour(axes[index]),
                device_id_type=MESH,
            )

        if index > 0:
            round_of(index - 1).wait()
            values[...] += received[index - 1]
        if index < len(axes):
            round_of(index).start()

    def taps_step(index):
        sum_step(taps, taps_recv, 0, ("y", "zh"), index)

    def gains_step(index):
        sum_step(gains, gains_recv, 2, ("zh", "y", "core", "x", "zl"), index)

    def far_part(index):
        weight_grad(1 - y, index, other)
        over(index).start()

    def near_part(index):
        weight_grad(y, index, mine)
        sum_y(index)

    for load in loads:
        load.wait()
    for errand in errands:
        errand.start()
    taps_step(0)
    far_part(0)
    far_part(1)

    def beside(point):
        if point == 0:
            far_part(2)
            far_part(3)
            taps_step(1)
        elif point == "far sent":
            far_part(4)
            far_part(5)
            near_part(0)
        elif point == "side sent":
            far_part(6)
            far_part(7)
            taps_step(2)
            near_part(1)
            for errand in errands:
                errand.middle()
        elif point == 1:
            near_part(2)
        elif point == 2:
            near_part(3)
            sum_z(0)
        elif point == 3:
            near_part(4)

    sends = scatter_core(NT, [left], [weight], buffers, beside, SCATTER_CUT)
    total = buffers[5]
    gain = gain_ref[...]

    def backward(step, along):
        at = pl.ds(pl.multiple_of(step * 32, 32), 32)
        values = tokens[at].astype(F32)
        scale = lax.rsqrt(jnp.mean(values * values, -1, keepdims=True) + 1e-05)
        grad = total[at]
        scaled = grad * gain
        mean = jnp.mean(values * scaled, -1, keepdims=True)
        change = scale * scaled - values * (scale * scale * scale * mean)
        moving[at] = (resid[at] + change).astype(BF16)
        return along + jnp.sum(grad * values * scale, 0, keepdims=True)

    along = lax.fori_loop(
        0, total.shape[0] // 32, backward, jnp.zeros((1, total.shape[1]), F32)
    )
    wide = gains.shape[1]
    for index in range(along.shape[1] // wide):
        gains[index : index + 1, :] = along[:, index * wide : (index + 1) * wide]
    gains_step(0)
    near_part(5)
    sum_z(1)
    near_part(6)
    gains_step(1)
    move = make_errands(
        [Exchange], [moving], [tokens_grad_ref], move_send, move_recv,
        local.at[pl.ds(9 + CHUNKS, 1)],
    )[0]
    stores = Stores(local.at[pl.ds(10 + CHUNKS, 2)])
    stores.add(taps, taps_out_ref)
    sum_z(2)
    near_part(7)
    move.start()
    gains_step(2)
    sum_z(3)
    forward(0)
    gains_step(3)
    forward(1)
    sum_z(4)
    gains_step(4)
    forward(2)
    sum_z(5)
    gains_step(5)
    stores.add(gains, gains_out_ref)
    forward(3)
    sum_z(6)
    forward(4)
    sum_z(7)
    forward(5)
    forward(6)
    forward(7)
    for copy in sends:
        copy.wait_send()
    for index in range(CHUNKS):
        over(index).wait_send()

        @pl.when(moved)
        def _(index=index):
            across(index).wait_send()
            cross(index).wait_recv()
            pass_on(index).wait_recv()

        @pl.when(stays)
        def _(index=index):
            back(index).wait_send()
            cross(index).wait_send()
            pass_on(index).wait_send()
            near(index).wait()

    move.finish()
    for errand in errands:
        errand.finish()
    stores.finish()


def finish(
    left, weight, gathered, tokens, resid_grad, gain, taps, gains, collective_id,
    errands=(),
):
    rows, width = tokens.shape
    kinds, sources = [e[0] for e in errands], [e[1] for e in errands]
    hbm = pl.BlockSpec(memory_space=pl.ANY)
    depth, columns = weight.shape
    half = pltpu.VMEM((depth // 2, columns), BF16)
    return pl.pallas_call(
        functools.partial(finish_body, kinds),
        in_specs=[hbm] * 5 + [pl.BlockSpec(memory_space=pltpu.VMEM)] + [hbm] * (2 + len(kinds)),
        out_specs=[hbm] * (4 + len(kinds)),
        out_shape=[
            jax.ShapeDtypeStruct(tokens.shape, BF16),
            jax.ShapeDtypeStruct(weight.shape, BF16),
            jax.ShapeDtypeStruct(taps.shape, F32),
            jax.ShapeDtypeStruct(gains.shape, F32),
            *[errand_target(*errand) for errand in errands],
        ],
        scratch_shapes=[
            pltpu.VMEM(left.shape, BF16),
            pltpu.VMEM(weight.shape, BF16),
            pltpu.VMEM(gathered.shape, BF16),
            pltpu.VMEM((depth // 2 // CHUNKS, gathered.shape[0]), BF16),
            half,
            half,
            half,
            half,
            pltpu.VMEM((rows, width), BF16),
            pltpu.VMEM((rows, width), F32),
            pltpu.VMEM((rows, width), BF16),
            pltpu.VMEM(taps.shape, F32),
            pltpu.VMEM((2, *taps.shape), F32),
            pltpu.VMEM(gains.shape, F32),
            pltpu.VMEM((5, *gains.shape), F32),
            *scatter_scratch(rows, width),
            pltpu.SemaphoreType.DMA((5, CHUNKS)),
            pltpu.SemaphoreType.DMA((5, CHUNKS)),
            pltpu.SemaphoreType.DMA((7,)),
            pltpu.SemaphoreType.DMA((7,)),
            pltpu.SemaphoreType.DMA((1,)),
            pltpu.SemaphoreType.DMA((1,)),
            pltpu.SemaphoreType.DMA((12 + CHUNKS,)),
            *errand_scratch(kinds, sources),
        ],
        compiler_params=pltpu.CompilerParams(
            collective_id=collective_id, has_side_effects=True, vmem_limit_bytes=60 * 2**20
        ),
        name="finish",
    )(left, weight, gathered, tokens, resid_grad, gain, taps, gains, *sources)


def rms_scale(values, gain):
    return values * lax.rsqrt(jnp.mean(values * values, -1, keepdims=True) + 1e-05) * gain


def swiglu(gate, up_vals):
    return jax.nn.silu(gate) * up_vals


def left_product(left, right):
    return dot(left, right, TN)


def token_scales(group_ids, mixture_counts):
    group_cols = lax.broadcasted_iota(jnp.int32, (1, GROUPS), 1)
    counts = mixture_counts.astype(F32)
    group_scale = jnp.sqrt(jnp.mean(counts) / counts)
    return jnp.sum(jnp.where(group_ids[:, None] == group_cols, group_scale[None, :], 0.0), 1)


def mixer_weights(w_query, w_key, w_value, w_gate_mix, w_beta):
    padded = jnp.pad(w_beta, ((0, 0), (0, 128 - w_beta.shape[1])))
    return jnp.concatenate([w_query, w_key, w_value, w_gate_mix, padded], 1)


ALL = ("y", "core", "zh", "zl", "x")
SIZES = (2, 2, 2, 2, 2)


CORE_PAIRS = [(i, i ^ 8) for i in range(32)]


FORWARD_PLAN = (
    (0, 0, "start"), (0, 1, "start"), (0, 2, "start"), (3, 1, "middle"), (4, 0, "early"),
    (5, 2, "early"), (6, 0, "middle"), (7, 2, "late"), (7, 0, "late"),
    (7, 0, "finish"), (7, 1, "finish"), (7, 2, "finish"),
)
BACKWARD_PLAN = (
    (0, 0, "start"), (0, 3, "start"), (0, 1, "start"), (0, 2, "start"),
    (1, 0, "launch"), (2, 3, "launch"), (4, 1, "middle"), (6, 2, "middle"), (7, 0, "settle"),
    (7, 3, "settle_late"), (7, 0, "forward"), (7, 3, "forward"),
    (7, 0, "finish"), (7, 1, "finish"), (7, 2, "finish"), (7, 3, "finish"),
)


def halves_sum(values, came):
    rows = came.shape[0]
    mine = lax.dynamic_slice_in_dim(values, lax.axis_index("y") * rows, rows, 0)
    return (mine.astype(F32) + came.astype(F32)).astype(BF16)


def total_of(part, far):
    return (part.astype(F32) + far.astype(F32)).astype(BF16)


def shards_ring(
    tokens, group_ids, mixture_counts, grad_out, norm1_gain, w_query, w_key, w_value, w_gate_mix,
    w_beta, conv_query, conv_key, conv_value, out_gain, w_out, norm2_gain, w_gate, w_up, w_down,
):
    heads = w_beta.shape[1]
    head_cols = w_query.shape[1]
    gain = out_gain.astype(F32)[None]
    gain1 = norm1_gain.astype(F32)[None]
    conv = jnp.concatenate([conv_query, conv_key, conv_value], 1).astype(F32)
    conv = jnp.pad(conv, ((0, 4), (0, 0)))
    grad_mlp = grad_out.astype(F32) * token_scales(group_ids, mixture_counts)[:, None]
    padded_beta = jnp.pad(w_beta, ((0, 0), (0, 128 - heads)))
    tokens, gathered, projected, mix_weights, conv, grad_mlp = begin(
        tokens, gain1, conv, [w_query, w_key, w_value, w_gate_mix, padded_beta], 1,
        [(Exchange, grad_mlp.astype(BF16))],
    )
    inputs = tokens.astype(F32)
    mixed, *kept, gathered_grad, w_out, w_gate = mixer_forward(
        projected, conv, gain, heads,
        [(Gather, grad_mlp), (Swap, w_out), (Swap, w_gate.T)], FORWARD_PLAN, 2,
    )
    grad_rows = grad_mlp.astype(F32)
    attn, w_up, w_down = multiply_scatter(
        [mixed], [w_out], NN, 3, "scatter_attn", [(Swap, w_up.T), (Swap, w_down)]
    )
    resid = inputs + attn
    normed_mlp, norm2_back = jax.vjp(rms_scale, resid, norm2_gain.astype(F32))
    gathered_mlp, hidden, gate_grad, up_grad = feed(
        normed_mlp.astype(BF16), w_gate, w_up, w_down, gathered_grad, 4
    )
    gathered_grad = gathered_grad.reshape(-1, gathered_grad.shape[2])
    mlp_out, down_grad, gate_wgrad, up_wgrad, down_came = mlp_scatter(
        hidden, w_down, gathered_grad, gate_grad, up_grad, gathered_mlp, 5
    )
    output = (resid + mlp_out).astype(BF16)
    down_part = halves_sum(down_grad, down_came)
    normed_mlp_grad, gate_came, down_far = multiply_scatter(
        [gate_grad, up_grad], [w_gate, w_up], NN, 6, "scatter_normed_mlp_grad",
        [(HalfOverY, gate_wgrad), (Across, down_part)],
    )
    resid_norm_grad, norm2_grad = norm2_back(normed_mlp_grad)
    resid_grad = grad_rows + resid_norm_grad
    gate_part = halves_sum(gate_wgrad, gate_came)
    gathered_attn, mixed_grad, up_came, gate_far = gather_multiply(
        resid_grad.astype(BF16), [w_out], NT, 7, "gather_attn_grad",
        [(HalfOverY, up_wgrad), (Across, gate_part)],
    )
    up_part = halves_sum(up_wgrad, up_came)
    out_grad = left_product(mixed, gathered_attn).astype(BF16)
    raw_grad, conv_grad, gain_grad, up_total, down_total, gate_total, out_total = (
        mixer_backward(
            projected, conv, gain, mixed_grad, *kept, heads,
            [
                (Chain, up_part), (Spread, total_of(down_part, down_far)),
                (Spread, total_of(gate_part, gate_far)), (FullChain, out_grad),
            ],
            BACKWARD_PLAN, 8,
        )
    )
    width = tokens.shape[1]
    wide = width // 2
    gains = jnp.concatenate(
        [
            jnp.zeros((2, wide), F32), norm2_grad.reshape(2, wide),
            jnp.pad(gain_grad[:1], ((0, 3), (0, wide - gain_grad.shape[1]))),
        ],
        0,
    )
    grad_tokens, mix_total, taps, gains, output = finish(
        raw_grad, mix_weights, gathered, tokens, resid_grad, gain1, conv_grad, gains, 9,
        [(Exchange, output)],
    )
    other_taps = lax.ppermute(taps, ALL, CORE_PAIRS)
    conv_total = jnp.where(lax.axis_index("core") == lax.axis_index("zh"), taps, other_taps)[:4]
    mix_total = mix_total.astype(F32)
    return (
        output,
        grad_tokens,
        gains[:2].reshape(width),
        mix_total[:, 0:head_cols],
        mix_total[:, head_cols : 2 * head_cols],
        mix_total[:, 2 * head_cols : 3 * head_cols],
        mix_total[:, 3 * head_cols : 4 * head_cols],
        mix_total[:, 4 * head_cols : 4 * head_cols + heads],
        conv_total[:, 0:head_cols],
        conv_total[:, head_cols : 2 * head_cols],
        conv_total[:, 2 * head_cols :],
        gains[4, :HEAD_DIM],
        out_total.astype(F32),
        gains[2:4].reshape(width),
        gate_total.astype(F32).T,
        up_total.astype(F32).T,
        down_total.astype(F32),
    )


def right_product(left, right):
    return dot(left, right, NT)


def make_fold(kept_rows, weight, piece):
    weight_grad = left_product(kept_rows, piece)
    rows_grad = right_product(piece, weight)
    return (weight_grad, rows_grad)


def make_rows(source, weight, transposed):
    if transposed:
        return right_product(source, weight)
    return jnp.dot(source, weight, preferred_element_type=F32)


def shards(
    tokens,
    group_ids,
    mixture_counts,
    grad_out,
    norm1_gain,
    w_query,
    w_key,
    w_value,
    w_gate_mix,
    w_beta,
    conv_query,
    conv_key,
    conv_value,
    out_gain,
    w_out,
    norm2_gain,
    w_gate,
    w_up,
    w_down,
):
    inputs = tokens.astype(F32)
    normed, norm1_back = jax.vjp(rms_scale, inputs, norm1_gain.astype(F32))
    gathered = lax.all_gather(normed.astype(BF16), "tp", axis=0, tiled=True)
    heads = w_beta.shape[1]
    mix_weights = mixer_weights(w_query, w_key, w_value, w_gate_mix, w_beta)
    projected = jnp.dot(gathered, mix_weights, preferred_element_type=F32)
    head_cols = w_query.shape[1]
    conv = jnp.concatenate([conv_query, conv_key, conv_value], 1).astype(F32)
    gain = out_gain.astype(F32)[None]
    mixed, *kept = mixer_forward(projected, conv, gain, heads)
    attn = lax.psum_scatter(
        make_rows(mixed, w_out, False).astype(jnp.bfloat16), "tp", scatter_dimension=0, tiled=True
    ).astype(jnp.float32)
    resid = inputs + attn
    normed_mlp, norm2_back = jax.vjp(rms_scale, resid, norm2_gain.astype(F32))
    gathered_mlp = lax.all_gather(normed_mlp.astype(BF16), "tp", axis=0, tiled=True)
    pair_weights = jnp.concatenate([w_gate, w_up], 1)
    ff_cols = w_gate.shape[1]
    paired = jnp.dot(gathered_mlp, pair_weights, preferred_element_type=F32)
    hidden_full, swiglu_back = jax.vjp(swiglu, paired[:, :ff_cols], paired[:, ff_cols:])
    hidden = hidden_full.astype(BF16)
    mlp_out = lax.psum_scatter(
        make_rows(hidden, w_down, False).astype(jnp.bfloat16), "tp", scatter_dimension=0, tiled=True
    ).astype(jnp.float32)
    output = (resid + mlp_out).astype(BF16)
    token_scale = token_scales(group_ids, mixture_counts)
    grad_rows = grad_out.astype(F32) * token_scale[:, None]
    grad_mlp = grad_rows.astype(BF16)
    grad_w_down, hidden_grad = make_fold(
        hidden, w_down, lax.all_gather(grad_mlp, "tp", axis=0, tiled=True)
    )
    gate_grad, up_grad = swiglu_back(hidden_grad)
    pair_grad = jnp.concatenate([gate_grad, up_grad], 1).astype(BF16)
    pair_weight_grad = left_product(gathered_mlp, pair_grad)
    normed_mlp_grad = lax.psum_scatter(
        make_rows(pair_grad, pair_weights, True).astype(jnp.bfloat16),
        "tp",
        scatter_dimension=0,
        tiled=True,
    ).astype(jnp.float32)
    resid_norm_grad, norm2_grad = norm2_back(normed_mlp_grad)
    resid_grad = grad_rows + resid_norm_grad
    attn_grad = resid_grad.astype(BF16)
    grad_w_out, mixed_grad = make_fold(
        mixed, w_out, lax.all_gather(attn_grad, "tp", axis=0, tiled=True)
    )
    raw_grad, conv_grad, gain_grad = mixer_backward(
        projected, conv, gain, mixed_grad, *kept, heads
    )
    mix_weight_grad = left_product(gathered, raw_grad)
    normed_grad = lax.psum_scatter(
        make_rows(raw_grad, mix_weights, True).astype(jnp.bfloat16),
        "tp",
        scatter_dimension=0,
        tiled=True,
    ).astype(jnp.float32)
    input_norm_grad, norm1_grad = norm1_back(normed_grad)
    grad_tokens = (resid_grad + input_norm_grad).astype(BF16)
    summed = (
        lax.psum(mix_weight_grad.astype(jnp.bfloat16), "dp").astype(jnp.float32),
        lax.psum(grad_w_out.astype(jnp.bfloat16), "dp").astype(jnp.float32),
        lax.psum(pair_weight_grad.astype(jnp.bfloat16), "dp").astype(jnp.float32),
        lax.psum(grad_w_down.astype(jnp.bfloat16), "dp").astype(jnp.float32),
    )
    conv_total = lax.psum(conv_grad[:4], "dp")
    gains = lax.psum((norm1_grad, gain_grad[0], norm2_grad), ("dp", "tp"))
    mix_total = summed[0]
    pair_total = summed[2]
    return (
        output,
        grad_tokens,
        gains[0],
        mix_total[:, 0:head_cols],
        mix_total[:, head_cols : 2 * head_cols],
        mix_total[:, 2 * head_cols : 3 * head_cols],
        mix_total[:, 3 * head_cols : 4 * head_cols],
        mix_total[:, 4 * head_cols : 4 * head_cols + heads],
        conv_total[:, 0:head_cols],
        conv_total[:, head_cols : 2 * head_cols],
        conv_total[:, 2 * head_cols :],
        gains[1],
        summed[1],
        gains[2],
        pair_total[:, :ff_cols],
        pair_total[:, ff_cols:],
        summed[3],
    )


def solution(mesh):
    rows, cols, all_rows = "tp", "tp", ("dp", "tp")
    body = shards
    if dict(mesh.shape) == {"dp": 4, "tp": 8}:
        mesh = Mesh(mesh.devices.reshape(SIZES), ALL)
        rows = cols = ("zh", "zl", "x")
        all_rows = ALL
        body = shards_ring
    by_row, by_col, by_token = P(rows, None), P(None, cols), P(all_rows, None)
    return jax.shard_map(
        body,
        mesh=mesh,
        in_specs=(
            by_token, P(all_rows), P(), by_token, P(), by_col, by_col, by_col, by_col, by_col,
            by_col, by_col, by_col, P(), by_row, P(), by_col, by_col, by_row,
        ),
        out_specs=(
            by_token, by_token, P(), by_col, by_col, by_col, by_col, by_col, by_col, by_col,
            by_col, P(), by_row, P(), by_col, by_col, by_row,
        ),
        check_vma=False,
    )
```

time: 935 us -> 774 us (0.83)
  matrix products: 67.4 us -> 5.87 us
  Pallas kernels: 752 us -> 697 us
  local copies, waits for them, and re-layouts: 62.2 us -> 20 us
    pallas_call x1 -> x3, Pallas kernels: 88.9 us -> 220 us  [the longest x1 101 us: begin(): pl.pallas_call(functools.partial(begin_body, kinds), in_specs=[hbm, pl.Bl...]
    pallas_call x2 -> x1, Pallas kernels: 131 us -> 54.6 us  [gather_multiply(): pl.pallas_call(functools.partial(gather_body, dims, count, kinds), in_spe...]
    dot_general x6 -> x1, matrix products: 67.4 us -> 5.87 us  [dot(): lax.dot_general(left, right, (dims, ((), ())), preferred_element_type=F32)]
    pallas_call x3 -> x2, Pallas kernels: 192 us -> 134 us  [multiply_scatter(): pl.pallas_call(functools.partial(scatter_body, dims, count, kinds), in_sp...]
    pallas_call x1, Pallas kernels: 114 us -> 83.5 us  [mixer_forward(): pl.pallas_call(functools.partial(mixer_forward_body, heads, kinds, plan),...]
    pallas_call x1, Pallas kernels: 151 us -> 123 us  [finish(): pl.pallas_call(functools.partial(finish_body, kinds), in_specs=[hbm] * 5...]
    unnamed x64 -> x63, local copies, waits for them, and re-layouts: 27.5 us -> 11 us
    reshape x3 -> x1, local copies, waits for them, and re-layouts: 12.8 us -> 0.01 us  [shards_ring(): norm2_grad.reshape(2, wide)]
  transfers between devices with their start and end apart: 0 -> 1, of which waited for: 0 -> 0; matrix products, arithmetic and copies ran while one was open for 0% -> 3% of each run, Pallas kernels for 0% -> 0%
where the time goes in v3:
time: 774 us; the launch traced here: 767 us
  Pallas kernels  697 us (90%)
  other arithmetic  40.3 us (5%)
  local copies, waits for them, and re-layouts  20 us (3%)
    pallas_call x2, Pallas kernels, multiply_scatter(): pl.pallas_call(functools.partial(scatter_body, dims, count, kinds), in_sp...  134 us
    pallas_call x1, Pallas kernels, finish(): pl.pallas_call(functools.partial(finish_body, kinds), in_specs=[hbm] * 5...  123 us
    pallas_call x1, Pallas kernels, begin(): pl.pallas_call(functools.partial(begin_body, kinds), in_specs=[hbm, pl.Bl...  101 us
    pallas_call x1, Pallas kernels, mixer_forward(): pl.pallas_call(functools.partial(mixer_forward_body, heads, kinds, plan),...  83.5 us
    pallas_call x1, Pallas kernels, mixer_backward(): pl.pallas_call(functools.partial(mixer_backward_body, heads, kinds, plan)...  81.9 us
    pallas_call x1, Pallas kernels, feed(): pl.pallas_call(functools.partial(feed_body, kinds), in_specs=[hbm] * (5 +...  59.7 us
    pallas_call x1, Pallas kernels, mlp_scatter(): pl.pallas_call(functools.partial(mlp_body, kinds), in_specs=[hbm] * (6 +...  59.4 us
    pallas_call x1, Pallas kernels, gather_multiply(): pl.pallas_call(functools.partial(gather_body, dims, count, kinds), in_spe...  54.6 us
  transfers between devices with their start and end apart: 1, of which 0 were waited for; matrix products, arithmetic and copies ran while one was open for 3% of the time, Pallas kernels for 0%

profile of v3, /device:TPU:0, one launch (start us, length us, event | category | flops | bytes accessed | tf_op | source)
XLA Modules:
  0.0 767.5 jit_solution(5011806443466020102)
XLA Ops:
  0.7 1.3 broadcast_in_dim.41
  2.0 1.3 convert_reduce_fusion
  3.9 0.7 divide_sqrt_fusion
  4.6 1.0 copy.38
  5.6 0.7 bitcast_convert_fusion.refs_2_.refs_3_
  6.3 0.8 select_reduce_fusion
  7.0 2.4 multiply_convert_fusion.1.refs_8_
  9.4 0.9 pad.16.refs_7_
  10.3 0.6 fusion.6.refs_2_
  11.0 100.5 %begin.1 = (bf16[256,2048]{1,0:T(8,128)(2,1)}, bf16[8,256,2048]{2,1,0:T(8,128)(2,1)}, f32[8,256,1152]{2,1,0:T(8,128)}, bf16[2048,1152]{1,0:T(8,128)(2,1)}, f32[8,768]{1,0:T(8,128)}, /*index=5*/bf16[256,2048]{1,0:T(8,128)(2,1)}) custom-call(bf16[256,2048]{1,0:T(8,128)(2,1)} %refs_0_.1, f32[1,2048]{1,0:T(1,128)} %bitcast.42, f32[8,768]{1,0:T(8,128)} %fusion.6.refs_2_, ...), custom_call_target="tpu_custom_call" | custom-call | tf_op jit(solution)/shard_map/begin/pallas_call | solution.py:1477
  111.5 1.2 copy-done.3
  112.7 0.7 copy-done.6
  113.5 83.5 %mixer_forward.1 = (bf16[2048,256]{1,0:T(8,128)(2,1)S(1)}, f32[2048,512]{1,0:T(8,128)}, f32[2048,256]{1,0:T(8,128)}, f32[2048,256]{1,0:T(8,128)}, f32[32,2,128,1...) custom-call(f32[2048,1152]{1,0:T(8,128)} %bitcast.32, ...), custom_call_target="tpu_custom_call" | custom-call | tf_op jit(solution)/shard_map/mixer_forward/pallas_call | solution.py:225
  197.0 1.0 copy-done
  198.0 1.0 copy-done.2
  198.9 72.5 %scatter_attn.1 = (f32[256,2048]{1,0:T(8,128)}, bf16[704,2048]{1,0:T(8,128)(2,1)}, bf16[704,2048]{1,0:T(8,128)(2,1)}) custom-call(bf16[8,256,256]{2,1,0:T(8,128)(2,1)} %bitcast.31, bf16[256,2048]{1,0:T(8,128)(2,1)} %copy-done.2, bf16[704,2048]{1,0:T(8,128)(2,1)} %bitcast.40, bf16[704,2048]{1,0:T(8,128)(2,1)} %refs_3_.3), custom_call_target="tpu_custom_call" | custom-call | tf_op jit(solution)/shard_map/scatter_attn/pallas_call | solution.py:1370
  271.5 2.0 multiply_reduce_fusion.2
  273.5 1.2 multiply_convert_fusion.refs_0_
  274.7 59.7 %feed.1 = (bf16[8,256,2048]{2,1,0:T(8,128)(2,1)}, bf16[8,256,704]{2,1,0:T(8,128)(2,1)}, bf16[8,256,704]{2,1,0:T(8,128)(2,1)}, bf16[8,256,704]{2,1,0:T(8,128)(2,1)}) custom-call(bf16[256,2048]{1,0:T(8,128)(2,1)} %multiply_convert_fusion.refs_0_, bf16[704,2048]{1,0:T(8,128)(2,1)} %get-tuple-element.70.refs_1_.refs_2_, ...), custom_call_target="tpu_custom_call" | custom-call | tf_op jit(solution)/shard_map/feed/pallas_call | solution.py:1195
  334.4 59.4 %scatter_mlp.1 = (f32[256,2048]{1,0:T(8,128)}, bf16[704,2048]{1,0:T(8,128)(2,1)}, bf16[704,2048]{1,0:T(8,128)(2,1)}, bf16[704,2048]{1,0:T(8,128)(2,1)}, bf16[352,2048]{1,0:T(8,128)(2,1)}) custom-call(bf16[8,256,704]{2,1,0:T(8,128)(2,1)} %get-tuple-element.76.refs_0_, bf16[704,2048]{1,0:T(8,128)(2,1)} %get-tuple-element.72.refs_3_.refs_1_, ...), custom_call_target="tpu_custom_call" | custom-call | tf_op jit(solution)/shard_map/scatter_mlp/pallas_call | solution.py:1592
  393.8 3.5 add_convert_fusion.4.refs_5_
  397.3 61.1 %scatter_normed_mlp_grad.1 = (f32[256,2048]{1,0:T(8,128)}, bf16[352,2048]{1,0:T(8,128)(2,1)}, bf16[352,2048]{1,0:T(8,128)(2,1)}) custom-call(bf16[8,256,704]{2,1,0:T(8,128)(2,1)} %get-tuple-element.74.refs_3_.refs_0_, bf16[8,256,704]{2,1,0:T(8,128)(2,1)} %get-tuple-element.75.refs_4_.refs_1_, bf16[704,2048]{1,0:T(8,128)(2,1)} %get-tuple-element.70.refs_1_.refs_2_, ...), custom_call_target="tpu_custom_call" | custom-call | tf_op jit(solution)/shard_map/scatter_normed_mlp_grad/pallas_call | solution.py:1370
  458.5 2.4 multiply_reduce_fusion
  460.9 4.5 add_convert_fusion.1
  465.4 3.0 fusion.8
  468.4 54.6 %gather_attn_grad.1 = (bf16[8,256,2048]{2,1,0:T(8,128)(2,1)}, f32[8,256,256]{2,1,0:T(8,128)}, bf16[352,2048]{1,0:T(8,128)(2,1)}, bf16[352,2048]{1,0:T(8,128)(2,1)}) custom-call(bf16[256,2048]{1,0:T(8,128)(2,1)} %get-tuple-element.145.refs_0_, bf16[256,2048]{1,0:T(8,128)(2,1)} %copy-done.2, bf16[704,2048]{1,0:T(8,128)(2,1)} %get-tuple-element.82.refs_2_, ...), custom_call_target="tpu_custom_call" | custom-call | tf_op jit(solution)/shard_map/gather_attn_grad/pallas_call | solution.py:1103
  523.1 5.9 convolution_convert_fusion.refs_13_
  529.0 1.6 add_convert_fusion.refs_12_
  530.6 0.7 copy-done.12
  531.7 0.5 add_convert_fusion.2.refs_10_
  532.4 81.9 %mixer_backward.1 = (bf16[2048,1152]{1,0:T(8,128)(2,1)}, f32[8,768]{1,0:T(8,128)S(1)}, f32[8,128]{1,0:T(8,128)S(1)}, bf16[704,2048]{1,0:T(8,128)(2,1)}, bf16[704...) custom-call(f32[2048,1152]{1,0:T(8,128)} %bitcast.33, f32[2048,1152]{1,0:T(8,128)} %bitcast.34, ...), custom_call_target="tpu_custom_call" | custom-call | tf_op jit(solution)/shard_map/mixer_backward/pallas_call | solution.py:452
  614.4 0.6 copy-done.8
  615.0 0.7 select_maximum_fusion.refs_7_
  615.7 123.5 %finish.1 = (bf16[256,2048]{1,0:T(8,128)(2,1)}, bf16[2048,1152]{1,0:T(8,128)(2,1)}, f32[8,768]{1,0:T(8,128)}, f32[8,1024]{1,0:T(8,128)}, bf16[256,2048]{1,0:T(8,128)(2,1)}) custom-call(bf16[2048,1152]{1,0:T(8,128)(2,1)} %get-tuple-element.94.refs_0_, bf16[2048,1152]{1,0:T(8,128)(2,1)} %get-tuple-element.95.refs_1_, bf16[2048,2048]{1,0:T(8,128)(2,1)} %bitcast.38, ...), custom_call_target="tpu_custom_call" | custom-call | tf_op jit(solution)/shard_map/finish/pallas_call | solution.py:1859
  739.2 2.3 collective-permute-start
  741.4 5.9 fusion.10
  747.3 3.3 convert_bitcast_fusion
  750.6 3.3 convert_bitcast_fusion.1
  753.9 0.5 slice_bitcast_fusion.2
  754.5 1.1 slice.56
  755.6 0.9 copy.39
  756.5 0.6 copy.44
  757.1 0.6 copy.45
  757.7 5.1 convert_element_type.122
  762.8 1.6 convert_element_type.121
  764.4 0.6 fusion.11
  765.0 1.0 copy.48
  766.0 1.0 copy.49
  (60 shorter events, 0.8 us)
Async XLA Ops:
  0.7 9.7 %copy-start.27 = (bf16[4,256]{1,0:T(4,128)(2,1)S(1)}, bf16[4,256]{1,0:T(4,128)(2,1)}, u32[]{:S(2)}) copy-start(bf16[4,256]{1,0:T(4,128)(2,1)} %param.29) | copy-start | bytes 6148
  0.7 9.7 %copy-start.26 = (bf16[4,256]{1,0:T(4,128)(2,1)S(1)}, bf16[4,256]{1,0:T(4,128)(2,1)}, u32[]{:S(2)}) copy-start(bf16[4,256]{1,0:T(4,128)(2,1)} %param.30) | copy-start | bytes 6148
  0.7 9.7 %copy-start.25 = (bf16[4,256]{1,0:T(4,128)(2,1)S(1)}, bf16[4,256]{1,0:T(4,128)(2,1)}, u32[]{:S(2)}) copy-start(bf16[4,256]{1,0:T(4,128)(2,1)} %param.31) | copy-start | bytes 6148
  11.0 100.5 %copy-start.5 = (bf16[256,2048]{1,0:T(8,128)(2,1)S(1)}, bf16[256,2048]{1,0:T(8,128)(2,1)}, u32[]{:S(2)}) copy-start(bf16[256,2048]{1,0:T(8,128)(2,1)} %refs_4_.3) | copy-start | bytes 3145732
  111.5 1.2 copy-start.3
  112.7 0.7 copy-start.6
  197.0 1.0 copy-start
  198.0 1.0 copy-start.2
  198.9 72.6 %copy-start.13 = (bf16[256,2048]{1,0:T(8,128)(2,1)S(1)}, bf16[256,2048]{1,0:T(8,128)(2,1)}, u32[]{:S(2)}) copy-start(bf16[256,2048]{1,0:T(8,128)(2,1)} %get-tuple-element.66.refs_3_) | copy-start | bytes 3145732
  271.5 2.0 copy-start.24
  458.4 2.4 copy-start.10
  458.5 2.4 copy-start.19
  460.9 4.5 copy-start.4
  460.9 4.5 copy-start.11
  460.9 4.5 copy-start.16
  468.4 54.6 %copy-start.1 = (bf16[2048,256]{1,0:T(8,128)(2,1)S(1)}, bf16[2048,256]{1,0:T(8,128)(2,1)}, u32[]{:S(2)}) copy-start(bf16[2048,256]{1,0:T(8,128)(2,1)} %copy-done) | copy-start | bytes 3145732
  523.0 5.9 copy-start.9
  523.0 5.9 copy-start.18
  529.0 2.3 copy-start.12
  529.0 2.7 copy-start.17
  531.7 0.7 copy-start.7
  614.3 0.6 copy-start.8
  739.2 25.2 %collective-permute-start = (f32[8,768]{1,0:T(8,128)}, f32[8,768]{1,0:T(8,128)S(1)}, u32[]{:S(2)}, u32[]{:S(2)}) collective-permute-start(f32[8,768]{1,0:T(8,128)} %get-tuple-element.104), channel_id=1, source_target_pairs={{0,8},{1,9},{2,10},{3,11},{4,12},{5,13},{6,14},{7,15},{8,0},{9,1},... | collective-permute-start | bytes 73736 | tf_op jit(solution)/shard_map/ppermute | solution.py:2029
  741.4 5.9 copy-start.23
  741.4 5.9 copy-start.15
  747.3 3.3 copy-start.14
  762.8 1.6 copy-start.22
  762.8 2.2 copy-start.21
  762.8 3.2 copy-start.20

commit v4 on v3

--- a/solution.py
+++ b/solution.py
@@ -89,7 +89,7 @@
     return total
 
 
-LATE_PHASES = ("settle_late", "forward", "finish")
+LATE_PHASES = ("settle_late", "late_after", "forward", "finish")
 
 
 def run_errands(errands, plan, step, late):
@@ -506,6 +506,11 @@
     )
 
 
+def on_part(outer):
+    at_end = lax.axis_index("zl") == lax.axis_index("zh")
+    return is_moved() & (at_end if outer else jnp.logical_not(at_end))
+
+
 def is_moved():
     return lax.axis_index("core") != lax.axis_index("zh")
 
@@ -555,6 +560,16 @@
     def buffer_shape(shape):
         return shape
 
+    def start_part(self, outer):
+        if outer:
+            self.start()
+
+    def start_outer(self):
+        self.start_part(True)
+
+    def start_inner(self):
+        self.start_part(False)
+
     def stays(self, action):
         pl.when(jnp.logical_not(is_moved()))(action)
 
@@ -617,12 +632,17 @@
         return self.remote(2 + index, half, half, neighbour("y"))
 
     def start(self):
-        @pl.when(is_moved())
+        self.start_part(True)
+        self.start_part(False)
+
+    def start_part(self, outer):
+        @pl.when(on_part(outer))
         def _():
             self.first(0).start()
             self.first(1).start()
 
-        self.start_here()
+        if outer:
+            self.start_here()
 
     def pass_piece(self, index):
         @pl.when(is_moved())
@@ -636,6 +656,9 @@
 
     def late(self):
         self.pass_piece(1)
+
+    def late_after(self):
+        self.late()
 
     def middle(self):
         self.early()
@@ -677,6 +700,9 @@
     def start(self):
         pl.when(is_moved())(lambda: self.copy().start())
 
+    def start_part(self, outer):
+        pl.when(on_part(outer))(lambda: self.copy().start())
+
     def middle(self):
         pass
 
@@ -685,14 +711,14 @@
         self.stays(lambda: self.copy().wait_recv())
 
 
-SCATTER_CUT = 192
+SCATTER_CUT = 208
 
 
 class Gather(Errand):
     sems = 11
 
     def ring(self):
-        return Ring(self.target, self.send, self.recv, 32, self.stage)
+        return Ring(self.target, self.send, self.recv, 0, self.stage)
 
     def own(self):
         return pltpu.make_async_copy(self.stage, self.target.at[slot_of(0, 0, 0)], self.local)
@@ -960,7 +986,7 @@
         self.held, self.send, self.recv = held, send, recv
         own, wide, deep, far = (slot_of(0, *at) for at in ((0, 0), (0, 1), (1, 0), (1, 1)))
         rows = held.shape[1]
-        cut = cut or rows // 2
+        cut = rows // 2 if cut is None else cut
         rest = rows - cut
         self.moves = (
             ("x", own, wide, 0, cut), ("zl", own, deep, cut, rest),
@@ -983,12 +1009,15 @@
             recv_sem=self.recv.at[index], device_id=neighbour(axis), device_id_type=MESH,
         )
 
+    def live(self, indices):
+        return [index for index in indices if self.moves[index][4]]
+
     def launch(self, *indices):
-        for index in indices:
+        for index in self.live(indices):
             self.move(index).start()
 
     def arrived(self, *indices):
-        for index in indices:
+        for index in self.live(indices):
             self.move(index, True).wait_recv()
 
     def run(self, work, beside):
@@ -1022,7 +1051,7 @@
         work(slot_of(1, 1, 1))
 
     def finish(self):
-        for index in range(len(self.moves)):
+        for index in self.live(range(len(self.moves))):
             self.move(index).wait_send()
 
 
@@ -1074,7 +1103,7 @@
     greet(bool(kinds))
     for load in loads:
         load.wait()
-    ring = Ring(held, send, recv, None)
+    ring = Ring(held, send, recv)
     stores = Stores(local.at[pl.ds(1 + count, 8 * (1 + count))])
 
     def work(slot):
@@ -1226,6 +1255,7 @@
     sending, crossing, partial, far_recv, side_recv, total, send, recv = buffers
     rows, width = total.shape
     cut = cut or rows // 2
+    rest = rows - cut
 
     def move(index, axis, src, dst):
         return pltpu.make_async_remote_copy(
@@ -1277,22 +1307,25 @@
     cross(1)
     local_sum(0)
     launch(4, "x", partial.at[0, first], far_recv.at[0, first])
-    launch(5, "zl", partial.at[0, second], far_recv.at[1, second])
+    if rest:
+        launch(5, "zl", partial.at[0, second], far_recv.at[1, second])
     beside("far sent")
     cross(2)
     local_sum(1)
     launch(6, "x", partial.at[1, first], side_recv.at[0, first])
     local_sum(2)
-    launch(7, "zl", partial.at[2, second], side_recv.at[1, second])
+    if rest:
+        launch(7, "zl", partial.at[2, second], side_recv.at[1, second])
     beside("side sent")
     cross(3)
     beside(1)
     move(4, "x", partial.at[0, first], far_recv.at[0, first]).wait_recv()
     partial[2, first] = (partial[2, first].astype(F32) + far_recv[0, first].astype(F32)).astype(BF16)
     launch(8, "zl", partial.at[2, first], side_recv.at[1, first])
-    move(5, "zl", partial.at[0, second], far_recv.at[1, second]).wait_recv()
-    partial[1, second] = (partial[1, second].astype(F32) + far_recv[1, second].astype(F32)).astype(BF16)
-    launch(9, "x", partial.at[1, second], side_recv.at[0, second])
+    if rest:
+        move(5, "zl", partial.at[0, second], far_recv.at[1, second]).wait_recv()
+        partial[1, second] = (partial[1, second].astype(F32) + far_recv[1, second].astype(F32)).astype(BF16)
+        launch(9, "x", partial.at[1, second], side_recv.at[0, second])
     beside(2)
     crossed(3)
 
@@ -1302,13 +1335,15 @@
     multiply(slot_of(0, 0, 0), write)
     move(6, "x", partial.at[1, first], side_recv.at[0, first]).wait_recv()
     total[first] += side_recv[0, first].astype(F32)
-    move(7, "zl", partial.at[2, second], side_recv.at[1, second]).wait_recv()
-    total[second] += side_recv[1, second].astype(F32)
+    if rest:
+        move(7, "zl", partial.at[2, second], side_recv.at[1, second]).wait_recv()
+        total[second] += side_recv[1, second].astype(F32)
     beside(3)
     move(8, "zl", partial.at[2, first], side_recv.at[1, first]).wait_recv()
     total[first] += side_recv[1, first].astype(F32)
-    move(9, "x", partial.at[1, second], side_recv.at[0, second]).wait_recv()
-    total[second] += side_recv[0, second].astype(F32)
+    if rest:
+        move(9, "x", partial.at[1, second], side_recv.at[0, second]).wait_recv()
+        total[second] += side_recv[0, second].astype(F32)
     return sends
 
 
@@ -1325,20 +1360,65 @@
     ]
 
 
-def scatter_body(dims, count, kinds, *refs):
-    first_ref, refs, errands = take_errands(kinds, refs, 2 * count, 1)
+def norm_back(values, grad, gain):
+    scale = lax.rsqrt(jnp.mean(values * values, -1, keepdims=True) + 1e-05)
+    scaled = grad * gain
+    mean = jnp.mean(values * scaled, -1, keepdims=True)
+    return scale * scaled - values * (scale * scale * scale * mean), grad * values * scale
+
+
+def by_rows(rows, body, carry=0):
+    def step(index, carry):
+        return body(pl.ds(pl.multiple_of(index * 32, 32), 32), carry)
+
+    return lax.fori_loop(0, rows // 32, step, carry)
+
+
+def attn_tail(total, extras, outs):
+    tokens, gain = extras
+    resid, normed = outs
+
+    def body(at, carry):
+        values = tokens[at].astype(F32) + total[at]
+        scale = lax.rsqrt(jnp.mean(values * values, -1, keepdims=True) + 1e-05)
+        resid[at] = values
+        normed[at] = (values * scale * gain[0:1]).astype(BF16)
+        return carry
+
+    by_rows(total.shape[0], body)
+
+
+def grad_tail(total, extras, outs):
+    resid, grad_rows, gain = extras
+    resid_grad, attn_grad, gain_grad = outs
+
+    def body(at, along):
+        change, terms = norm_back(resid[at], total[at], gain[0:1])
+        value = grad_rows[at].astype(F32) + change
+        resid_grad[at] = value
+        attn_grad[at] = value.astype(BF16)
+        return along + jnp.sum(terms, 0, keepdims=True)
+
+    along = by_rows(total.shape[0], body, jnp.zeros((1, total.shape[1]), F32))
+    gain_grad[...] = jnp.broadcast_to(along, gain_grad.shape)
+
+
+def scatter_body(dims, count, extra, out_count, tail, kinds, *refs):
+    first_ref, refs, errands = take_errands(kinds, refs, 2 * count + extra, out_count)
     refs = (first_ref, *refs)
-    total_ref = refs[2 * count]
-    operands = refs[2 * count + 1 : 4 * count + 1]
-    buffers, local = refs[4 * count + 1 : -1], refs[-1]
+    inputs = 2 * count + extra
+    out_refs, held = refs[inputs : inputs + out_count], refs[inputs + out_count :]
+    operands, extras = held[: 2 * count], held[2 * count : inputs]
+    outs, held = held[inputs : inputs + out_count], held[inputs + out_count :]
+    buffers, local = held[:-1], held[-1]
     loads = [
-        pltpu.make_async_copy(ref, operand, local.at[i])
-        for i, (ref, operand) in enumerate(zip(refs[: 2 * count], operands))
+        pltpu.make_async_copy(ref, place, local.at[i])
+        for i, (ref, place) in enumerate(zip(refs[:inputs], (*operands, *extras)))
     ]
     for load in loads:
         load.start()
     greet(bool(kinds))
-    for load in loads:
+    for load in loads[: 2 * count]:
         load.wait()
 
     def beside(point):
@@ -1352,38 +1432,43 @@
 
     cut = SCATTER_CUT if Across in kinds or Swap in kinds else None
     sends = scatter_core(dims, operands[:count], operands[count:], buffers, beside, cut)
-    store = pltpu.make_async_copy(buffers[5], total_ref, local.at[2 * count])
-    store.start()
+    for load in loads[2 * count :]:
+        load.wait()
+    tail(buffers[5], extras, outs)
+    stores = Stores(local.at[pl.ds(inputs, out_count)])
+    for place, ref in zip(outs, out_refs):
+        stores.add(place, ref)
     for copy in sends:
         copy.wait_send()
-    store.wait()
+    stores.finish()
     for errand in errands:
         errand.finish()
 
 
-def multiply_scatter(lefts, weights, dims, collective_id, name, errands=()):
+def multiply_scatter(lefts, weights, extras, outs, tail, dims, collective_id, name, errands=()):
     rows = lefts[0].shape[0] // 8
     width = weights[0].shape[1] if dims == NN else weights[0].shape[0]
     count = len(lefts)
     lefts = [left.reshape(8, rows, left.shape[1]) for left in lefts]
     kinds, sources = [e[0] for e in errands], [e[1] for e in errands]
+    inputs = (*lefts, *weights, *extras)
+    hbm = pl.BlockSpec(memory_space=pl.ANY)
     return pl.pallas_call(
-        functools.partial(scatter_body, dims, count, kinds),
-        in_specs=[pl.BlockSpec(memory_space=pl.ANY)] * (2 * count + len(kinds)),
-        out_specs=[pl.BlockSpec(memory_space=pl.ANY)] * (1 + len(kinds)),
-        out_shape=[jax.ShapeDtypeStruct((rows, width), F32)]
-        + [errand_target(*errand) for errand in errands],
-        scratch_shapes=[pltpu.VMEM(v.shape, BF16) for v in (*lefts, *weights)]
-        + [
+        functools.partial(scatter_body, dims, count, len(extras), len(outs), tail, kinds),
+        in_specs=[hbm] * (len(inputs) + len(kinds)),
+        out_specs=[hbm] * (len(outs) + len(kinds)),
+        out_shape=[*outs, *[errand_target(*errand) for errand in errands]],
+        scratch_shapes=[
+            *[pltpu.VMEM(v.shape, v.dtype) for v in (*inputs, *outs)],
             *scatter_scratch(rows, width),
-            pltpu.SemaphoreType.DMA((2 * count + 1,)),
+            pltpu.SemaphoreType.DMA((len(inputs) + len(outs),)),
             *errand_scratch(kinds, sources),
         ],
         compiler_params=pltpu.CompilerParams(
-            collective_id=collective_id, has_side_effects=True, vmem_limit_bytes=56 * 2**20
+            collective_id=collective_id, has_side_effects=True, vmem_limit_bytes=58 * 2**20
         ),
         name=name,
-    )(*lefts, *weights, *sources)
+    )(*inputs, *sources)
 
 
 def begin_body(kinds, *refs):
@@ -1406,12 +1491,7 @@
     )
     block.start()
     taps.start()
-    swaps[0].start()
     block.finish()
-    for swap in swaps[1:]:
-        swap.start()
-    for errand in errands:
-        errand.start()
     own = slot_of(0, 0, 0)
     values = tokens[...].astype(F32)
     scale = lax.rsqrt(jnp.mean(values * values, -1, keepdims=True) + 1e-05)
@@ -1419,8 +1499,12 @@
     keep = pltpu.make_async_copy(tokens, moved_ref, local.at[7])
     keep.start()
 
-    ring = Ring(held, send, recv)
+    ring = Ring(held, send, recv, 0)
     ring.launch(0, 1, 2, 3, 4)
+    for swap in swaps:
+        swap.start()
+    for errand in errands:
+        errand.start()
     ring.arrived(0)
     ring.launch(5)
     ring.arrived(1)
@@ -1629,7 +1713,7 @@
     left, weight, gathered, turned, mine, other, came, far, tokens = refs[:9]
     resid, moving, taps, taps_recv, gains, gains_recv, *refs = refs[9:]
     buffers, refs = refs[:8], refs[8:]
-    chain_send, chain_recv, sum_send, sum_recv, move_send, move_recv, local = refs
+    chain_send, chain_recv, sum_send, sum_recv, local = refs
     loads = [
         pltpu.make_async_copy(source, target, local.at[i])
         for i, (source, target) in enumerate(
@@ -1774,20 +1858,12 @@
     total = buffers[5]
     gain = gain_ref[...]
 
-    def backward(step, along):
-        at = pl.ds(pl.multiple_of(step * 32, 32), 32)
-        values = tokens[at].astype(F32)
-        scale = lax.rsqrt(jnp.mean(values * values, -1, keepdims=True) + 1e-05)
-        grad = total[at]
-        scaled = grad * gain
-        mean = jnp.mean(values * scaled, -1, keepdims=True)
-        change = scale * scaled - values * (scale * scale * scale * mean)
+    def backward(at, along):
+        change, terms = norm_back(tokens[at].astype(F32), total[at], gain)
         moving[at] = (resid[at] + change).astype(BF16)
-        return along + jnp.sum(grad * values * scale, 0, keepdims=True)
-
-    along = lax.fori_loop(
-        0, total.shape[0] // 32, backward, jnp.zeros((1, total.shape[1]), F32)
-    )
+        return along + jnp.sum(terms, 0, keepdims=True)
+
+    along = by_rows(total.shape[0], backward, jnp.zeros((1, total.shape[1]), F32))
     wide = gains.shape[1]
     for index in range(along.shape[1] // wide):
         gains[index : index + 1, :] = along[:, index * wide : (index + 1) * wide]
@@ -1796,15 +1872,11 @@
     sum_z(1)
     near_part(6)
     gains_step(1)
-    move = make_errands(
-        [Exchange], [moving], [tokens_grad_ref], move_send, move_recv,
-        local.at[pl.ds(9 + CHUNKS, 1)],
-    )[0]
-    stores = Stores(local.at[pl.ds(10 + CHUNKS, 2)])
+    stores = Stores(local.at[pl.ds(9 + CHUNKS, 3)])
     stores.add(taps, taps_out_ref)
     sum_z(2)
     near_part(7)
-    move.start()
+    stores.add(moving, tokens_grad_ref)
     gains_step(2)
     sum_z(3)
     forward(0)
@@ -1841,7 +1913,6 @@
             pass_on(index).wait_send()
             near(index).wait()
 
-    move.finish()
     for errand in errands:
         errand.finish()
     stores.finish()
@@ -1888,8 +1959,6 @@
             pltpu.SemaphoreType.DMA((5, CHUNKS)),
             pltpu.SemaphoreType.DMA((7,)),
             pltpu.SemaphoreType.DMA((7,)),
-            pltpu.SemaphoreType.DMA((1,)),
-            pltpu.SemaphoreType.DMA((1,)),
             pltpu.SemaphoreType.DMA((12 + CHUNKS,)),
             *errand_scratch(kinds, sources),
         ],
@@ -1929,18 +1998,20 @@
 
 
 CORE_PAIRS = [(i, i ^ 8) for i in range(32)]
+EXCHANGE_PAIRS = [(i, i & 19 | (i & 8) >> 1 | (i & 4) << 1) for i in range(32)]
 
 
 FORWARD_PLAN = (
-    (0, 0, "start"), (0, 1, "start"), (0, 2, "start"), (3, 1, "middle"), (4, 0, "early"),
-    (5, 2, "early"), (6, 0, "middle"), (7, 2, "late"), (7, 0, "late"),
-    (7, 0, "finish"), (7, 1, "finish"), (7, 2, "finish"),
+    (0, 0, "start"), (0, 1, "start"), (0, 2, "start"), (0, 3, "start"),
+    (3, 1, "middle"), (4, 0, "early"), (5, 2, "early"), (6, 0, "middle"), (7, 2, "late"),
+    (7, 0, "late"), (7, 3, "early"), (7, 3, "late_after"),
+    (7, 0, "finish"), (7, 1, "finish"), (7, 2, "finish"), (7, 3, "finish"),
 )
 BACKWARD_PLAN = (
-    (0, 0, "start"), (0, 3, "start"), (0, 1, "start"), (0, 2, "start"),
-    (1, 0, "launch"), (2, 3, "launch"), (4, 1, "middle"), (6, 2, "middle"), (7, 0, "settle"),
-    (7, 3, "settle_late"), (7, 0, "forward"), (7, 3, "forward"),
-    (7, 0, "finish"), (7, 1, "finish"), (7, 2, "finish"), (7, 3, "finish"),
+    (0, 0, "start"), (0, 2, "start"), (0, 0, "launch"), (0, 1, "start"), (4, 1, "middle"),
+    (6, 0, "settle"), (6, 2, "launch"),
+    (7, 0, "forward"), (7, 2, "settle_late"), (7, 2, "forward"),
+    (7, 0, "finish"), (7, 1, "finish"), (7, 2, "finish"),
 )
 
 
@@ -1970,19 +2041,19 @@
         tokens, gain1, conv, [w_query, w_key, w_value, w_gate_mix, padded_beta], 1,
         [(Exchange, grad_mlp.astype(BF16))],
     )
-    inputs = tokens.astype(F32)
-    mixed, *kept, gathered_grad, w_out, w_gate = mixer_forward(
+    mixed, *kept, gathered_grad, w_out, w_gate, w_up = mixer_forward(
         projected, conv, gain, heads,
-        [(Gather, grad_mlp), (Swap, w_out), (Swap, w_gate.T)], FORWARD_PLAN, 2,
+        [(Gather, grad_mlp), (Swap, w_out), (Swap, w_gate.T), (Swap, w_up.T)], FORWARD_PLAN, 2,
     )
-    grad_rows = grad_mlp.astype(F32)
-    attn, w_up, w_down = multiply_scatter(
-        [mixed], [w_out], NN, 3, "scatter_attn", [(Swap, w_up.T), (Swap, w_down)]
+    block = jax.ShapeDtypeStruct(tokens.shape, F32)
+    block_low = jax.ShapeDtypeStruct(tokens.shape, BF16)
+    gain2 = jnp.broadcast_to(norm2_gain.astype(F32), (8, norm2_gain.shape[0]))
+    resid, normed_mlp, w_down = multiply_scatter(
+        [mixed], [w_out], [tokens, gain2], [block, block_low], attn_tail, NN, 3, "scatter_attn",
+        [(Swap, w_down)],
     )
-    resid = inputs + attn
-    normed_mlp, norm2_back = jax.vjp(rms_scale, resid, norm2_gain.astype(F32))
     gathered_mlp, hidden, gate_grad, up_grad = feed(
-        normed_mlp.astype(BF16), w_gate, w_up, w_down, gathered_grad, 4
+        normed_mlp, w_gate, w_up, w_down, gathered_grad, 4
     )
     gathered_grad = gathered_grad.reshape(-1, gathered_grad.shape[2])
     mlp_out, down_grad, gate_wgrad, up_wgrad, down_came = mlp_scatter(
@@ -1990,25 +2061,23 @@
     )
     output = (resid + mlp_out).astype(BF16)
     down_part = halves_sum(down_grad, down_came)
-    normed_mlp_grad, gate_came, down_far = multiply_scatter(
-        [gate_grad, up_grad], [w_gate, w_up], NN, 6, "scatter_normed_mlp_grad",
-        [(HalfOverY, gate_wgrad), (Across, down_part)],
+    resid_grad, attn_grad, norm2_grad, gate_came, down_far = multiply_scatter(
+        [gate_grad, up_grad], [w_gate, w_up], [resid, grad_mlp, gain2],
+        [block, block_low, jax.ShapeDtypeStruct(gain2.shape, F32)], grad_tail, NN, 6,
+        "scatter_normed_mlp_grad", [(HalfOverY, gate_wgrad), (Across, down_part)],
     )
-    resid_norm_grad, norm2_grad = norm2_back(normed_mlp_grad)
-    resid_grad = grad_rows + resid_norm_grad
     gate_part = halves_sum(gate_wgrad, gate_came)
-    gathered_attn, mixed_grad, up_came, gate_far = gather_multiply(
-        resid_grad.astype(BF16), [w_out], NT, 7, "gather_attn_grad",
-        [(HalfOverY, up_wgrad), (Across, gate_part)],
+    gathered_attn, mixed_grad, up_came, gate_far, down_total = gather_multiply(
+        attn_grad, [w_out], NT, 7, "gather_attn_grad",
+        [(HalfOverY, up_wgrad), (Across, gate_part), (Spread, total_of(down_part, down_far))],
     )
     up_part = halves_sum(up_wgrad, up_came)
     out_grad = left_product(mixed, gathered_attn).astype(BF16)
-    raw_grad, conv_grad, gain_grad, up_total, down_total, gate_total, out_total = (
+    raw_grad, conv_grad, gain_grad, up_total, gate_total, out_total = (
         mixer_backward(
             projected, conv, gain, mixed_grad, *kept, heads,
             [
-                (Chain, up_part), (Spread, total_of(down_part, down_far)),
-                (Spread, total_of(gate_part, gate_far)), (FullChain, out_grad),
+                (Chain, up_part), (Spread, total_of(gate_part, gate_far)), (FullChain, out_grad),
             ],
             BACKWARD_PLAN, 8,
         )
@@ -2017,7 +2086,7 @@
     wide = width // 2
     gains = jnp.concatenate(
         [
-            jnp.zeros((2, wide), F32), norm2_grad.reshape(2, wide),
+            jnp.zeros((2, wide), F32), norm2_grad[0].reshape(2, wide),
             jnp.pad(gain_grad[:1], ((0, 3), (0, wide - gain_grad.shape[1]))),
         ],
         0,
@@ -2026,6 +2095,7 @@
         raw_grad, mix_weights, gathered, tokens, resid_grad, gain1, conv_grad, gains, 9,
         [(Exchange, output)],
     )
+    grad_tokens = lax.ppermute(grad_tokens, ALL, EXCHANGE_PAIRS)
     other_taps = lax.ppermute(taps, ALL, CORE_PAIRS)
     conv_total = jnp.where(lax.axis_index("core") == lax.axis_index("zh"), taps, other_taps)[:4]
     mix_total = mix_total.astype(F32)

time: 774 us -> 749 us (0.968)
  Pallas kernels: 697 us -> 674 us
    pallas_call x1, Pallas kernels: 83.5 us -> 98.3 us  [mixer_forward(): pl.pallas_call(functools.partial(mixer_forward_body, heads, kinds, plan),...]
    pallas_call x1, Pallas kernels: 59.7 us -> 48.3 us  [feed(): pl.pallas_call(functools.partial(feed_body, kinds), in_specs=[hbm] * (5 +...]
    pallas_call x1, Pallas kernels: 123 us -> 114 us  [finish(): pl.pallas_call(functools.partial(finish_body, kinds), in_specs=[hbm] * 5...]
    pallas_call x1, Pallas kernels: 101 us -> 92.1 us  [begin(): pl.pallas_call(functools.partial(begin_body, kinds), in_specs=[hbm, pl.Bl...]
  transfers between devices with their start and end apart: 1 -> 2, of which waited for: 0 -> 0; matrix products, arithmetic and copies ran while one was open for 3% -> 3% of each run, Pallas kernels for 0% -> 0%
where the time goes in v4:
time: 749 us; the launch traced here: 739 us
  Pallas kernels  674 us (90%)
  other arithmetic  33.5 us (4%)
  local copies, waits for them, and re-layouts  21.3 us (3%)
    pallas_call x2, Pallas kernels, multiply_scatter(): pl.pallas_call(functools.partial(scatter_body, dims, count, len(extras),...  134 us
    pallas_call x1, Pallas kernels, finish(): pl.pallas_call(functools.partial(finish_body, kinds), in_specs=[hbm] * 5...  114 us
    pallas_call x1, Pallas kernels, mixer_forward(): pl.pallas_call(functools.partial(mixer_forward_body, heads, kinds, plan),...  98.3 us
    pallas_call x1, Pallas kernels, begin(): pl.pallas_call(functools.partial(begin_body, kinds), in_specs=[hbm, pl.Bl...  92.1 us
    pallas_call x1, Pallas kernels, mixer_backward(): pl.pallas_call(functools.partial(mixer_backward_body, heads, kinds, plan)...  75.6 us
    pallas_call x1, Pallas kernels, mlp_scatter(): pl.pallas_call(functools.partial(mlp_body, kinds), in_specs=[hbm] * (6 +...  56.9 us
    pallas_call x1, Pallas kernels, gather_multiply(): pl.pallas_call(functools.partial(gather_body, dims, count, kinds), in_spe...  55.5 us
    pallas_call x1, Pallas kernels, feed(): pl.pallas_call(functools.partial(feed_body, kinds), in_specs=[hbm] * (5 +...  48.3 us
  transfers between devices with their start and end apart: 2, of which 0 were waited for; matrix products, arithmetic and copies ran while one was open for 3% of the time, Pallas kernels for 0%

profile of v4, /device:TPU:0, one launch (start us, length us, event | category | flops | bytes accessed | tf_op | source)
XLA Modules:
  0.0 739.2 jit_solution(13461912066262622974)
XLA Ops:
  0.7 1.3 broadcast_in_dim.39
  2.0 1.0 copy.38
  3.0 1.3 convert_reduce_fusion
  4.9 0.7 divide_sqrt_fusion
  5.6 0.7 bitcast_convert_fusion.refs_2_.refs_3_
  6.3 0.9 pad.16.refs_7_
  7.1 0.8 select_reduce_fusion
  7.9 2.4 multiply_convert_fusion.refs_8_
  10.4 0.6 fusion.5.refs_2_
  11.0 92.1 %begin.1 = (bf16[256,2048]{1,0:T(8,128)(2,1)}, bf16[8,256,2048]{2,1,0:T(8,128)(2,1)}, f32[8,256,1152]{2,1,0:T(8,128)}, bf16[2048,1152]{1,0:T(8,128)(2,1)}, f32[8,768]{1,0:T(8,128)}, /*index=5*/bf16[256,2048]{1,0:T(8,128)(2,1)}) custom-call(bf16[256,2048]{1,0:T(8,128)(2,1)} %refs_0_.1, f32[1,2048]{1,0:T(1,128)} %bitcast.42, f32[8,768]{1,0:T(8,128)} %fusion.5.refs_2_, ...), custom_call_target="tpu_custom_call" | custom-call | tf_op jit(solution)/shard_map/begin/pallas_call | solution.py:1561
  103.1 1.2 copy-done.3
  104.3 0.7 copy-done.5
  105.0 98.3 %mixer_forward.1 = (bf16[2048,256]{1,0:T(8,128)(2,1)S(1)}, f32[2048,512]{1,0:T(8,128)}, f32[2048,256]{1,0:T(8,128)}, f32[2048,256]{1,0:T(8,128)}, f32[32,2,128,1...) custom-call(f32[2048,1152]{1,0:T(8,128)} %bitcast.32, ...), custom_call_target="tpu_custom_call" | custom-call | tf_op jit(solution)/shard_map/mixer_forward/pallas_call | solution.py:225
  203.3 1.0 copy-done
  204.3 1.0 copy-done.2
  205.2 0.6 broadcast_in_dim.37.refs_3_.refs_6_
  205.9 70.2 %scatter_attn.1 = (f32[256,2048]{1,0:T(8,128)}, bf16[256,2048]{1,0:T(8,128)(2,1)}, bf16[704,2048]{1,0:T(8,128)(2,1)}) custom-call(bf16[8,256,256]{2,1,0:T(8,128)(2,1)} %bitcast.31, bf16[256,2048]{1,0:T(8,128)(2,1)} %copy-done.2, bf16[256,2048]{1,0:T(8,128)(2,1)} %get-tuple-element.71.refs_2_.refs_3_, f32[8,2048]{1,0:T(8,128)} %broadcast_in_dim.37.refs_3_.refs_6_, ...), custom_call_target="tpu_custom_call" | custom-call | tf_op jit(solution)/shard_map/scatter_attn/pallas_call | solution.py:1456
  276.1 48.3 %feed.1 = (bf16[8,256,2048]{2,1,0:T(8,128)(2,1)}, bf16[8,256,704]{2,1,0:T(8,128)(2,1)}, bf16[8,256,704]{2,1,0:T(8,128)(2,1)}, bf16[8,256,704]{2,1,0:T(8,128)(2,1)}) custom-call(bf16[256,2048]{1,0:T(8,128)(2,1)} %get-tuple-element.72.refs_0_, bf16[704,2048]{1,0:T(8,128)(2,1)} %get-tuple-element.73.refs_1_.refs_2_, ...), custom_call_target="tpu_custom_call" | custom-call | tf_op jit(solution)/shard_map/feed/pallas_call | solution.py:1224
  324.4 56.9 %scatter_mlp.1 = (f32[256,2048]{1,0:T(8,128)}, bf16[704,2048]{1,0:T(8,128)(2,1)}, bf16[704,2048]{1,0:T(8,128)(2,1)}, bf16[704,2048]{1,0:T(8,128)(2,1)}, bf16[352,2048]{1,0:T(8,128)(2,1)}) custom-call(bf16[8,256,704]{2,1,0:T(8,128)(2,1)} %get-tuple-element.80.refs_0_, bf16[704,2048]{1,0:T(8,128)(2,1)} %get-tuple-element.75.refs_3_.refs_1_, ...), custom_call_target="tpu_custom_call" | custom-call | tf_op jit(solution)/shard_map/scatter_mlp/pallas_call | solution.py:1676
  381.3 3.5 add_convert_fusion.4.refs_8_
  384.8 63.8 %scatter_normed_mlp_grad.1 = (f32[256,2048]{1,0:T(8,128)}, bf16[256,2048]{1,0:T(8,128)(2,1)}, f32[8,2048]{1,0:T(8,128)}, bf16[352,2048]{1,0:T(8,128)(2,1)}, bf16[352,2048]{1,0:T(8,128)(2,1)}) custom-call(bf16[8,256,704]{2,1,0:T(8,128)(2,1)} %get-tuple-element.77.refs_3_.refs_0_, bf16[8,256,704]{2,1,0:T(8,128)(2,1)} %get-tuple-element.78.refs_4_.refs_1_, ...), custom_call_target="tpu_custom_call" | custom-call | tf_op jit(solution)/shard_map/scatter_normed_mlp_grad/pallas_call | solution.py:1456
  448.6 4.6 add_convert_fusion.2
  453.3 55.5 %gather_attn_grad.1 = (bf16[8,256,2048]{2,1,0:T(8,128)(2,1)}, f32[8,256,256]{2,1,0:T(8,128)}, bf16[352,2048]{1,0:T(8,128)(2,1)}, bf16[352,2048]{1,0:T(8,128)(2,1)}, bf16[704,2048]{1,0:T(8,128)(2,1)}) custom-call(bf16[256,2048]{1,0:T(8,128)(2,1)} %get-tuple-element.85.refs_0_, bf16[256,2048]{1,0:T(8,128)(2,1)} %copy-done.2, ...), custom_call_target="tpu_custom_call" | custom-call | tf_op jit(solution)/shard_map/gather_attn_grad/pallas_call | solution.py:1132
  508.8 2.1 add_convert_fusion.1.refs_10_
  511.0 0.5 add_convert_fusion.refs_11_
  511.5 0.6 copy-done.1
  512.2 5.8 convolution_convert_fusion.refs_12_
  518.0 75.6 %mixer_backward.1 = (bf16[2048,1152]{1,0:T(8,128)(2,1)}, f32[8,768]{1,0:T(8,128)S(1)}, f32[8,128]{1,0:T(8,128)S(1)}, bf16[704,2048]{1,0:T(8,128)(2,1)}, bf16[704...) custom-call(f32[2048,1152]{1,0:T(8,128)} %bitcast.33, f32[2048,1152]{1,0:T(8,128)} %bitcast.34, f32[8,768]{1,0:T(8,128)S(1)} %copy-done.6, ...), custom_call_target="tpu_custom_call" | custom-call | tf_op jit(solution)/shard_map/mixer_backward/pallas_call | solution.py:452
  593.6 0.6 copy-done.7
  594.2 0.9 slice_reduce_fusion
  595.1 2.9 add_convert_fusion.5.refs_8_
  598.0 0.7 select_maximum_fusion.refs_7_
  598.6 113.6 %finish.1 = (bf16[256,2048]{1,0:T(8,128)(2,1)}, bf16[2048,1152]{1,0:T(8,128)(2,1)}, f32[8,768]{1,0:T(8,128)}, f32[8,1024]{1,0:T(8,128)}, bf16[256,2048]{1,0:T(8,128)(2,1)}) custom-call(bf16[2048,1152]{1,0:T(8,128)(2,1)} %get-tuple-element.98.refs_0_, bf16[2048,1152]{1,0:T(8,128)(2,1)} %get-tuple-element.99.refs_1_, bf16[2048,2048]{1,0:T(8,128)(2,1)} %bitcast.38, ...), custom_call_target="tpu_custom_call" | custom-call | tf_op jit(solution)/shard_map/finish/pallas_call | solution.py:1930
  712.2 1.9 collective-permute-start
  714.1 0.5 collective-permute-start.1
  714.6 5.9 fusion.6
  720.4 3.3 convert_bitcast_fusion.1
  723.8 3.3 convert_bitcast_fusion
  727.1 0.5 slice_bitcast_fusion.2
  727.6 1.1 slice.60
  728.7 0.6 copy.45
  729.3 0.9 copy.39
  730.2 1.6 convert_element_type.105
  731.8 0.6 copy.44
  732.8 3.3 convert_element_type.106
  736.1 0.6 fusion.7
  736.7 1.0 copy.48
  737.7 1.0 copy.49
  (50 shorter events, 0.6 us)
Async XLA Ops:
  0.7 9.7 %copy-start.21 = (bf16[4,256]{1,0:T(4,128)(2,1)S(1)}, bf16[4,256]{1,0:T(4,128)(2,1)}, u32[]{:S(2)}) copy-start(bf16[4,256]{1,0:T(4,128)(2,1)} %param.31) | copy-start | bytes 6148
  0.7 9.7 %copy-start.22 = (bf16[4,256]{1,0:T(4,128)(2,1)S(1)}, bf16[4,256]{1,0:T(4,128)(2,1)}, u32[]{:S(2)}) copy-start(bf16[4,256]{1,0:T(4,128)(2,1)} %param.30) | copy-start | bytes 6148
  0.7 9.7 %copy-start.23 = (bf16[4,256]{1,0:T(4,128)(2,1)S(1)}, bf16[4,256]{1,0:T(4,128)(2,1)}, u32[]{:S(2)}) copy-start(bf16[4,256]{1,0:T(4,128)(2,1)} %param.29) | copy-start | bytes 6148
  11.0 92.1 %copy-start.4 = (bf16[256,2048]{1,0:T(8,128)(2,1)S(1)}, bf16[256,2048]{1,0:T(8,128)(2,1)}, u32[]{:S(2)}) copy-start(bf16[256,2048]{1,0:T(8,128)(2,1)} %refs_4_.4) | copy-start | bytes 3145732
  103.0 1.2 copy-start.3
  104.3 0.7 copy-start.5
  105.0 100.2 %copy-start.20 = (bf16[2048]{0:T(1024)(128)(2,1)S(1)}, bf16[2048]{0:T(1024)(128)(2,1)}, u32[]{:S(2)}) copy-start(bf16[2048]{0:T(1024)(128)(2,1)} %param.34) | copy-start | bytes 12292
  203.3 1.0 copy-start
  204.3 1.0 copy-start.2
  384.8 63.8 %copy-start.8 = (bf16[352,2048]{1,0:T(8,128)(2,1)S(1)}, bf16[352,2048]{1,0:T(8,128)(2,1)}, u32[]{:S(2)}) copy-start(bf16[352,2048]{1,0:T(8,128)(2,1)} %add_convert_fusion.4.refs_8_) | copy-start | bytes 4325380
  384.8 63.8 %copy-start.11 = (bf16[704,2048]{1,0:T(8,128)(2,1)S(1)}, bf16[704,2048]{1,0:T(8,128)(2,1)}, u32[]{:S(2)}) copy-start(bf16[704,2048]{1,0:T(8,128)(2,1)} %get-tuple-element.82.refs_7_) | copy-start | bytes 8650756
  453.3 55.5 %copy-start.12 = (bf16[704,2048]{1,0:T(8,128)(2,1)S(1)}, bf16[704,2048]{1,0:T(8,128)(2,1)}, u32[]{:S(2)}) copy-start(bf16[704,2048]{1,0:T(8,128)(2,1)} %get-tuple-element.86.refs_2_) | copy-start | bytes 8650756
  508.8 2.2 copy-start.9
  508.8 2.2 copy-start.16
  510.9 1.2 copy-start.1
  512.2 5.8 copy-start.6
  518.0 77.1 %copy-start.10 = (f32[256,2048]{1,0:T(8,128)S(1)}, f32[256,2048]{1,0:T(8,128)}, u32[]{:S(2)}) copy-start(f32[256,2048]{1,0:T(8,128)} %get-tuple-element.79.refs_4_) | copy-start | bytes 6291460
  593.6 0.6 copy-start.7
  712.2 24.5 %collective-permute-start = (bf16[256,2048]{1,0:T(8,128)(2,1)}, bf16[256,2048]{1,0:T(8,128)(2,1)S(1)}, u32[]{:S(2)}, u32[]{:S(2)}) collective-permute-start(bf16[256,2048]{1,0:T(8,128)(2,1)} %get-tuple-element.107), channel_id=1, source_target_pairs={{0,0},{1,1},{2,2},{3,3},{4,8},{5,9},{6,10},{7,11},{8,4},{9,5},{10,... | collective-permute-start | bytes 3145736 | tf_op jit(solution)/shard_map/ppermute | solution.py:2098
  714.1 22.0 %collective-permute-start.1 = (f32[8,768]{1,0:T(8,128)}, f32[8,768]{1,0:T(8,128)S(1)}, u32[]{:S(2)}, u32[]{:S(2)}) collective-permute-start(f32[8,768]{1,0:T(8,128)} %get-tuple-element.110), channel_id=1, source_target_pairs={{0,8},{1,9},{2,10},{3,11},{4,12},{5,13},{6,14},{7,15},{8,0},{9,1},... | collective-permute-start | bytes 73736 | tf_op jit(solution)/shard_map/ppermute | solution.py:2099
  714.6 5.9 copy-start.15
  720.4 3.3 copy-start.14
  723.8 3.3 copy-start.19
  730.2 2.6 copy-start.13
  732.8 3.3 copy-start.18
  732.8 3.9 copy-start.17

commit v5 on v4

--- a/solution.py
+++ b/solution.py
@@ -89,7 +89,7 @@
     return total
 
 
-LATE_PHASES = ("settle_late", "late_after", "forward", "finish")
+LATE_PHASES = ("middle_late", "settle_late", "late_after", "forward", "finish")
 
 
 def run_errands(errands, plan, step, late):
@@ -115,7 +115,7 @@
 
 def mixer_params(errands, collective_id):
     extra = {"collective_id": collective_id, "has_side_effects": True} if errands else {}
-    return pltpu.CompilerParams(vmem_limit_bytes=48 * 2**20, **extra)
+    return pltpu.CompilerParams(vmem_limit_bytes=60 * 2**20, **extra)
 
 
 def mixer_forward_body(heads, kinds, plan, *refs):
@@ -609,6 +609,9 @@
     def middle(self):
         self.pass_here()
 
+    def middle_late(self):
+        self.middle()
+
     def finish(self):
         pl.when(is_moved())(lambda: self.far().wait())
         self.finish_here()
@@ -755,6 +758,61 @@
         ring.arrived(4, 7, 8, 9, 10)
         ring.finish()
         self.own().wait()
+
+
+class HalfSum(HalfOverY):
+    buffers = 2
+
+    @staticmethod
+    def buffer_shape(shape):
+        return (shape[0] // 2, *shape[1:])
+
+    def copy(self):
+        return self.remote(0, row_half(self.source, 1 - self.y), self.held[1], neighbour("y"))
+
+    def load(self):
+        return pltpu.make_async_copy(row_half(self.source, self.y), self.held[0], self.local)
+
+    def start(self):
+        self.copy().start()
+        self.load().start()
+
+    def store_sum(self):
+        mine, more = self.held
+        mine[...] = (mine[...].astype(F32) + more[...].astype(F32)).astype(BF16)
+        store = pltpu.make_async_copy(mine, self.target, self.local)
+        store.start()
+        store.wait()
+
+    def finish(self):
+        self.copy().wait()
+        self.load().wait()
+        self.store_sum()
+
+
+class AcrossTotal(HalfSum):
+    @staticmethod
+    def buffer_shape(shape):
+        return shape
+
+    def copy(self):
+        return self.remote(0, self.source, self.held[1], neighbour("zh"))
+
+    def load(self):
+        return pltpu.make_async_copy(self.source, self.held[0], self.local)
+
+    def start(self):
+        pl.when(is_moved())(lambda: self.copy().start())
+        self.stays(lambda: self.load().start())
+
+    def finish(self):
+        pl.when(is_moved())(lambda: self.copy().wait_send())
+
+        @pl.when(jnp.logical_not(is_moved()))
+        def _():
+            self.copy().wait_recv()
+            self.load().wait()
+            self.store_sum()
 
 
 class Spread(Errand):
@@ -905,7 +963,7 @@
     if kind is Gather:
         return jax.ShapeDtypeStruct((8, *source.shape), source.dtype)
     rows = source.shape[0]
-    rows = {HalfOverY: rows // 2, Spread: 2 * rows, Chain: 2 * rows}.get(kind, rows)
+    rows = {HalfSum: rows // 2, Spread: 2 * rows, Chain: 2 * rows}.get(kind, rows)
     return jax.ShapeDtypeStruct((rows, *source.shape[1:]), source.dtype)
 
 
@@ -1088,68 +1146,90 @@
     return beside
 
 
-def gather_body(dims, count, kinds, *refs):
-    block_ref, refs, errands = take_errands(kinds, refs, 1 + count, 1 + count)
-    weight_refs, gathered_ref, product_refs = refs[:count], refs[count], refs[count + 1 : 2 * count + 1]
-    held, send, recv = refs[2 * count + 1 : 2 * count + 4]
-    weights, results = refs[2 * count + 4 : 3 * count + 4], refs[3 * count + 4 : 4 * count + 4]
-    (local,) = refs[4 * count + 4 :]
+def gather_body(dims, kinds, block_ref, *refs):
+    block_ref, refs, errands = take_errands(kinds, (block_ref, *refs), 3, 2)
+    weight_ref, left_ref, product_ref, grad_ref, *refs = refs
+    held, send, recv, weight, result, left, turned, grad, local = refs
     own = slot_of(0, 0, 0)
-    loads = [pltpu.make_async_copy(block_ref, held.at[own], local.at[0])]
-    for i, (ref, weight) in enumerate(zip(weight_refs, weights)):
-        loads.append(pltpu.make_async_copy(ref, weight, local.at[1 + i]))
+    loads = [
+        pltpu.make_async_copy(source, place, local.at[i])
+        for i, (source, place) in enumerate(
+            ((block_ref, held.at[own]), (weight_ref, weight), (left_ref, left))
+        )
+    ]
     for load in loads:
         load.start()
     greet(bool(kinds))
     for load in loads:
         load.wait()
     ring = Ring(held, send, recv)
-    stores = Stores(local.at[pl.ds(1 + count, 8 * (1 + count))])
+    stores = Stores(local.at[pl.ds(3, 9)])
+    rows, depth = block_ref.shape
 
     def work(slot):
-        stores.add(held.at[slot], gathered_ref.at[slot])
-        for weight, result, product_ref in zip(weights, results, product_refs):
-
-            def column(at):
-                right = weight[:, at] if dims == NN else weight[at, :]
-                result[slot, :, at] = dot(held[slot], right, dims).astype(result.dtype)
-
-            by_columns(result.shape[2], column)
-            stores.add(result.at[slot], product_ref.at[slot])
-
-    ring.run(work, run_beside(errands, 0, 2))
+        def column(at):
+            right = weight[:, at] if dims == NN else weight[at, :]
+            result[slot, :, at] = dot(held[slot], right, dims)
+
+        by_columns(result.shape[2], column)
+        stores.add(result.at[slot], product_ref.at[slot])
+
+    def beside(point):
+        run_beside(errands, 0, 2)(point)
+        if point == 1:
+            for slot in range(8):
+                at = slice(slot * rows, (slot + 1) * rows)
+                turned[:, at] = left[at, :].T
+
+    ring.run(work, beside)
+
+    def column(at):
+        value = dot(turned[:, 0:rows], held[0, :, at], NN)
+        for slot in range(1, 8):
+            value = value + dot(
+                turned[:, slot * rows : (slot + 1) * rows], held[slot, :, at], NN
+            )
+        grad[:, at] = value.astype(BF16)
+
+    by_columns(depth, column)
+    stores.add(grad, grad_ref)
     ring.finish()
     stores.finish()
     for errand in errands:
         errand.finish()
 
 
-def gather_multiply(block, weights, dims, collective_id, name, errands=(), out_type=F32):
+def gather_multiply(block, weight, left, dims, collective_id, name, errands=()):
     rows, depth = block.shape
-    widths = [w.shape[1] if dims == NN else w.shape[0] for w in weights]
-    count = len(weights)
+    columns = weight.shape[1] if dims == NN else weight.shape[0]
     kinds, sources = [e[0] for e in errands], [e[1] for e in errands]
-    gathered, *products = pl.pallas_call(
-        functools.partial(gather_body, dims, count, kinds),
-        in_specs=[pl.BlockSpec(memory_space=pl.ANY)] * (1 + count + len(kinds)),
-        out_specs=[pl.BlockSpec(memory_space=pl.ANY)] * (1 + count + len(kinds)),
-        out_shape=[jax.ShapeDtypeStruct((8, rows, depth), BF16)]
-        + [jax.ShapeDtypeStruct((8, rows, width), out_type) for width in widths]
-        + [errand_target(*errand) for errand in errands],
-        scratch_shapes=ring_scratch(rows, depth)
-        + [pltpu.VMEM(w.shape, BF16) for w in weights]
-        + [pltpu.VMEM((8, rows, width), out_type) for width in widths]
-        + [
-            pltpu.SemaphoreType.DMA((1 + count + 8 * (1 + count),)),
+    hbm = pl.BlockSpec(memory_space=pl.ANY)
+    turned = (left.shape[1], left.shape[0])
+    product, grad, *more = pl.pallas_call(
+        functools.partial(gather_body, dims, kinds),
+        in_specs=[hbm] * (3 + len(kinds)),
+        out_specs=[hbm] * (2 + len(kinds)),
+        out_shape=[
+            jax.ShapeDtypeStruct((8, rows, columns), F32),
+            jax.ShapeDtypeStruct((left.shape[1], depth), BF16),
+            *[errand_target(*errand) for errand in errands],
+        ],
+        scratch_shapes=[
+            *ring_scratch(rows, depth),
+            pltpu.VMEM(weight.shape, BF16),
+            pltpu.VMEM((8, rows, columns), F32),
+            pltpu.VMEM(left.shape, BF16),
+            pltpu.VMEM(turned, BF16),
+            pltpu.VMEM((left.shape[1], depth), BF16),
+            pltpu.SemaphoreType.DMA((12,)),
             *errand_scratch(kinds, sources),
         ],
         compiler_params=pltpu.CompilerParams(
-            collective_id=collective_id, has_side_effects=True, vmem_limit_bytes=56 * 2**20
+            collective_id=collective_id, has_side_effects=True, vmem_limit_bytes=60 * 2**20
         ),
         name=name,
-    )(block, *weights, *sources)
-    flat = [v.reshape(8 * rows, v.shape[2]) for v in (gathered, *products[:count])]
-    return (*flat, *products[count:])
+    )(block, weight, left, *sources)
+    return (product.reshape(8 * rows, columns), grad, *more)
 
 
 def feed_body(kinds, *refs):
@@ -1237,7 +1317,7 @@
             *errand_scratch(kinds, sources),
         ],
         compiler_params=pltpu.CompilerParams(
-            collective_id=collective_id, has_side_effects=True, vmem_limit_bytes=58 * 2**20
+            collective_id=collective_id, has_side_effects=True, vmem_limit_bytes=60 * 2**20
         ),
         name="feed",
     )(block, w_gate, w_up, w_down, grads, *sources)
@@ -1389,8 +1469,8 @@
 
 
 def grad_tail(total, extras, outs):
-    resid, grad_rows, gain = extras
-    resid_grad, attn_grad, gain_grad = outs
+    resid, grad_rows, gain = extras[:3]
+    resid_grad, attn_grad, gain_grad = outs[:3]
 
     def body(at, along):
         change, terms = norm_back(resid[at], total[at], gain[0:1])
@@ -1403,14 +1483,14 @@
     gain_grad[...] = jnp.broadcast_to(along, gain_grad.shape)
 
 
-def scatter_body(dims, count, extra, out_count, tail, kinds, *refs):
+def scatter_body(dims, count, extra, out_count, tail, with_grad, kinds, *refs):
     first_ref, refs, errands = take_errands(kinds, refs, 2 * count + extra, out_count)
     refs = (first_ref, *refs)
     inputs = 2 * count + extra
     out_refs, held = refs[inputs : inputs + out_count], refs[inputs + out_count :]
     operands, extras = held[: 2 * count], held[2 * count : inputs]
     outs, held = held[inputs : inputs + out_count], held[inputs + out_count :]
-    buffers, local = held[:-1], held[-1]
+    buffers, local = held[:8], held[8]
     loads = [
         pltpu.make_async_copy(ref, place, local.at[i])
         for i, (ref, place) in enumerate(zip(refs[:inputs], (*operands, *extras)))
@@ -1429,10 +1509,17 @@
                 errand.early()
             elif point == 3:
                 errand.late() if hasattr(errand, "early") else errand.middle()
-
-    cut = SCATTER_CUT if Across in kinds or Swap in kinds else None
+        if point == 2 and with_grad:
+            turned, left = held[9], operands[count - 1]
+            rows = left.shape[1]
+            for slot in range(8):
+                turned[:, slot * rows : (slot + 1) * rows] = left[slot].T
+            loads[-1].wait()
+            turned_product(turned, extras[-1], outs[-1], outs[-1].shape[1])
+
+    cut = SCATTER_CUT if AcrossTotal in kinds or Swap in kinds else None
     sends = scatter_core(dims, operands[:count], operands[count:], buffers, beside, cut)
-    for load in loads[2 * count :]:
+    for load in loads[2 * count : len(loads) - with_grad]:
         load.wait()
     tail(buffers[5], extras, outs)
     stores = Stores(local.at[pl.ds(inputs, out_count)])
@@ -1445,16 +1532,26 @@
         errand.finish()
 
 
-def multiply_scatter(lefts, weights, extras, outs, tail, dims, collective_id, name, errands=()):
+def multiply_scatter(
+    lefts, weights, extras, outs, tail, dims, collective_id, name, errands=(), right=None,
+):
     rows = lefts[0].shape[0] // 8
     width = weights[0].shape[1] if dims == NN else weights[0].shape[0]
     count = len(lefts)
     lefts = [left.reshape(8, rows, left.shape[1]) for left in lefts]
     kinds, sources = [e[0] for e in errands], [e[1] for e in errands]
+    turned = []
+    if right is not None:
+        extras = (*extras, right)
+        units = lefts[-1].shape[2]
+        outs = (*outs, jax.ShapeDtypeStruct((units, right.shape[1]), BF16))
+        turned = [pltpu.VMEM((units, right.shape[0]), BF16)]
     inputs = (*lefts, *weights, *extras)
     hbm = pl.BlockSpec(memory_space=pl.ANY)
     return pl.pallas_call(
-        functools.partial(scatter_body, dims, count, len(extras), len(outs), tail, kinds),
+        functools.partial(
+            scatter_body, dims, count, len(extras), len(outs), tail, right is not None, kinds
+        ),
         in_specs=[hbm] * (len(inputs) + len(kinds)),
         out_specs=[hbm] * (len(outs) + len(kinds)),
         out_shape=[*outs, *[errand_target(*errand) for errand in errands]],
@@ -1462,10 +1559,11 @@
             *[pltpu.VMEM(v.shape, v.dtype) for v in (*inputs, *outs)],
             *scatter_scratch(rows, width),
             pltpu.SemaphoreType.DMA((len(inputs) + len(outs),)),
+            *turned,
             *errand_scratch(kinds, sources),
         ],
         compiler_params=pltpu.CompilerParams(
-            collective_id=collective_id, has_side_effects=True, vmem_limit_bytes=58 * 2**20
+            collective_id=collective_id, has_side_effects=True, vmem_limit_bytes=60 * 2**20
         ),
         name=name,
     )(*inputs, *sources)
@@ -1584,7 +1682,7 @@
             *errand_scratch(kinds, sources),
         ],
         compiler_params=pltpu.CompilerParams(
-            collective_id=collective_id, has_side_effects=True, vmem_limit_bytes=56 * 2**20
+            collective_id=collective_id, has_side_effects=True, vmem_limit_bytes=60 * 2**20
         ),
         name="begin",
     )(tokens, gain, conv, *weights, *sources)
@@ -1600,22 +1698,22 @@
 
 
 def mlp_body(kinds, *refs):
-    first_ref, refs, errands = take_errands(kinds, refs, 6, 5)
+    first_ref, refs, errands = take_errands(kinds, refs, 6, 3)
     sources, refs = (first_ref, *refs[:5]), refs[5:]
-    total_ref, down_ref, gate_ref, up_ref, came_ref, *refs = refs
-    hidden, weight, rights, lefts, turned, outs = refs[:6]
-    buffers, refs = refs[6:14], refs[14:]
+    output_ref, gate_ref, part_ref, *refs = refs
+    hidden, weight, rights, gate_grad, turned, outs, came, resid, output = refs[:9]
+    buffers, refs = refs[9:17], refs[17:]
     half_send, half_recv, local = refs
-    hidden_ref, weight_ref, grads_ref, gate_grad_ref, up_grad_ref, rows_ref = sources
+    hidden_ref, weight_ref, grads_ref, gate_grad_ref, rows_ref, resid_ref = sources
 
     def load(source, target, index):
         return pltpu.make_async_copy(source, target, local.at[index])
 
     early = [
         load(hidden_ref, hidden, 0), load(weight_ref, weight, 1), load(grads_ref, rights, 2),
-        load(gate_grad_ref, lefts.at[0], 3), load(up_grad_ref, lefts.at[1], 4),
+        load(gate_grad_ref, gate_grad, 3), load(resid_ref, resid, 5),
     ]
-    reload = load(rows_ref, rights, 5)
+    reload = load(rows_ref, rights, 4)
     for copy in early:
         copy.start()
     greet(True)
@@ -1631,7 +1729,7 @@
 
     y = lax.axis_index("y")
     half = pltpu.make_async_remote_copy(
-        src_ref=row_half(outs.at[0], 1 - y), dst_ref=came_ref, send_sem=half_send.at[0],
+        src_ref=row_half(outs.at[0], 1 - y), dst_ref=came, send_sem=half_send.at[0],
         recv_sem=half_recv.at[0], device_id=neighbour("y"), device_id_type=MESH,
     )
 
@@ -1639,46 +1737,52 @@
         if point == 0:
             for errand in errands:
                 errand.start()
-        elif point == "side sent":
+        elif point == "far sent":
             turn(hidden)
             turned_product(turned, rights, outs.at[0], columns)
             reload.start()
             half.start()
-            stores.add(outs.at[0], down_ref)
         elif point == 2:
-            turn(lefts.at[0])
+            turn(gate_grad)
             reload.wait()
             turned_product(turned, rights, outs.at[1], columns)
             stores.add(outs.at[1], gate_ref)
-            turn(lefts.at[1])
-            turned_product(turned, rights, outs.at[2], columns)
-            stores.add(outs.at[2], up_ref)
             for errand in errands:
                 errand.middle()
 
     sends = scatter_core(NN, [hidden], [weight], buffers, beside)
-    stores.add(buffers[5], total_ref)
+    total = buffers[5]
+
+    def body(at, carry):
+        output[at] = (resid[at] + total[at]).astype(BF16)
+        return carry
+
+    by_rows(rows, body)
+    stores.add(output, output_ref)
     for copy in sends:
         copy.wait_send()
     half.wait()
+    part = row_half(outs.at[0], y)
+    part[...] = (part[...].astype(F32) + came[...].astype(F32)).astype(BF16)
+    stores.add(part, part_ref)
     stores.finish()
     for errand in errands:
         errand.finish()
 
 
-def mlp_scatter(hidden, weight, grads, gate_grad, up_grad, gathered, collective_id, errands=()):
+def mlp_scatter(hidden, weight, grads, gate_grad, gathered, resid, collective_id, errands=()):
     tokens, units = hidden.shape
     rows, depth = tokens // 8, weight.shape[1]
     kinds, sources = [e[0] for e in errands], [e[1] for e in errands]
     hbm = pl.BlockSpec(memory_space=pl.ANY)
     by_unit = jax.ShapeDtypeStruct(weight.shape, BF16)
-    blocks = [v.reshape(8, rows, units) for v in (hidden, gate_grad, up_grad)]
+    blocks = [v.reshape(8, rows, units) for v in (hidden, gate_grad)]
     return pl.pallas_call(
         functools.partial(mlp_body, kinds),
         in_specs=[hbm] * (6 + len(kinds)),
-        out_specs=[hbm] * (5 + len(kinds)),
+        out_specs=[hbm] * (3 + len(kinds)),
         out_shape=[
-            jax.ShapeDtypeStruct((rows, depth), F32), by_unit, by_unit, by_unit,
+            jax.ShapeDtypeStruct((rows, depth), BF16), by_unit,
             jax.ShapeDtypeStruct((units // 2, depth), BF16),
             *[errand_target(*errand) for errand in errands],
         ],
@@ -1686,9 +1790,12 @@
             pltpu.VMEM((8, rows, units), BF16),
             pltpu.VMEM(weight.shape, BF16),
             pltpu.VMEM((tokens, depth), BF16),
-            pltpu.VMEM((2, 8, rows, units), BF16),
+            pltpu.VMEM((8, rows, units), BF16),
             pltpu.VMEM((units, tokens), BF16),
-            pltpu.VMEM((3, *weight.shape), BF16),
+            pltpu.VMEM((2, *weight.shape), BF16),
+            pltpu.VMEM((units // 2, depth), BF16),
+            pltpu.VMEM((rows, depth), F32),
+            pltpu.VMEM((rows, depth), BF16),
             *scatter_scratch(rows, depth),
             pltpu.SemaphoreType.DMA((1,)),
             pltpu.SemaphoreType.DMA((1,)),
@@ -1699,7 +1806,7 @@
             collective_id=collective_id, has_side_effects=True, vmem_limit_bytes=60 * 2**20
         ),
         name="scatter_mlp",
-    )(blocks[0], weight, grads, blocks[1], blocks[2], gathered, *sources)
+    )(blocks[0], weight, grads, blocks[1], gathered, resid, *sources)
 
 
 CHUNKS = 8
@@ -1854,7 +1961,7 @@
         elif point == 3:
             near_part(4)
 
-    sends = scatter_core(NT, [left], [weight], buffers, beside, SCATTER_CUT)
+    sends = scatter_core(NT, [left], [weight], buffers, beside, 224)
     total = buffers[5]
     gain = gain_ref[...]
 
@@ -2009,20 +2116,10 @@
 )
 BACKWARD_PLAN = (
     (0, 0, "start"), (0, 2, "start"), (0, 0, "launch"), (0, 1, "start"), (4, 1, "middle"),
-    (6, 0, "settle"), (6, 2, "launch"),
-    (7, 0, "forward"), (7, 2, "settle_late"), (7, 2, "forward"),
-    (7, 0, "finish"), (7, 1, "finish"), (7, 2, "finish"),
+    (6, 0, "settle"), (6, 2, "launch"), (7, 3, "start"),
+    (7, 3, "middle_late"), (7, 0, "forward"), (7, 2, "settle_late"), (7, 2, "forward"),
+    (7, 0, "finish"), (7, 1, "finish"), (7, 2, "finish"), (7, 3, "finish"),
 )
-
-
-def halves_sum(values, came):
-    rows = came.shape[0]
-    mine = lax.dynamic_slice_in_dim(values, lax.axis_index("y") * rows, rows, 0)
-    return (mine.astype(F32) + came.astype(F32)).astype(BF16)
-
-
-def total_of(part, far):
-    return (part.astype(F32) + far.astype(F32)).astype(BF16)
 
 
 def shards_ring(
@@ -2056,28 +2153,24 @@
         normed_mlp, w_gate, w_up, w_down, gathered_grad, 4
     )
     gathered_grad = gathered_grad.reshape(-1, gathered_grad.shape[2])
-    mlp_out, down_grad, gate_wgrad, up_wgrad, down_came = mlp_scatter(
-        hidden, w_down, gathered_grad, gate_grad, up_grad, gathered_mlp, 5
+    output, gate_wgrad, down_part = mlp_scatter(
+        hidden, w_down, gathered_grad, gate_grad, gathered_mlp, resid, 5
     )
-    output = (resid + mlp_out).astype(BF16)
-    down_part = halves_sum(down_grad, down_came)
-    resid_grad, attn_grad, norm2_grad, gate_came, down_far = multiply_scatter(
+    resid_grad, attn_grad, norm2_grad, up_wgrad, gate_part, down_half = multiply_scatter(
         [gate_grad, up_grad], [w_gate, w_up], [resid, grad_mlp, gain2],
         [block, block_low, jax.ShapeDtypeStruct(gain2.shape, F32)], grad_tail, NN, 6,
-        "scatter_normed_mlp_grad", [(HalfOverY, gate_wgrad), (Across, down_part)],
+        "scatter_normed_mlp_grad", [(HalfSum, gate_wgrad), (AcrossTotal, down_part)],
+        gathered_mlp,
     )
-    gate_part = halves_sum(gate_wgrad, gate_came)
-    gathered_attn, mixed_grad, up_came, gate_far, down_total = gather_multiply(
-        attn_grad, [w_out], NT, 7, "gather_attn_grad",
-        [(HalfOverY, up_wgrad), (Across, gate_part), (Spread, total_of(down_part, down_far))],
+    mixed_grad, out_grad, up_part, gate_half, down_total = gather_multiply(
+        attn_grad, w_out, mixed, NT, 7, "gather_attn_grad",
+        [(HalfSum, up_wgrad), (AcrossTotal, gate_part), (Spread, down_half)],
     )
-    up_part = halves_sum(up_wgrad, up_came)
-    out_grad = left_product(mixed, gathered_attn).astype(BF16)
-    raw_grad, conv_grad, gain_grad, up_total, gate_total, out_total = (
+    raw_grad, conv_grad, gain_grad, up_total, gate_total, out_total, output = (
         mixer_backward(
             projected, conv, gain, mixed_grad, *kept, heads,
             [
-                (Chain, up_part), (Spread, total_of(gate_part, gate_far)), (FullChain, out_grad),
+                (Chain, up_part), (Spread, gate_half), (FullChain, out_grad), (Exchange, output),
             ],
             BACKWARD_PLAN, 8,
         )
@@ -2091,9 +2184,8 @@
         ],
         0,
     )
-    grad_tokens, mix_total, taps, gains, output = finish(
-        raw_grad, mix_weights, gathered, tokens, resid_grad, gain1, conv_grad, gains, 9,
-        [(Exchange, output)],
+    grad_tokens, mix_total, taps, gains = finish(
+        raw_grad, mix_weights, gathered, tokens, resid_grad, gain1, conv_grad, gains, 9
     )
     grad_tokens = lax.ppermute(grad_tokens, ALL, EXCHANGE_PAIRS)
     other_taps = lax.ppermute(taps, ALL, CORE_PAIRS)

time: 749 us -> 732 us (0.977)
  other arithmetic: 33.5 us -> 21.1 us
    convert_element_type x5 -> x0, other arithmetic: 13.6 us -> none  [the longest x2 5.61 us: halves_sum(): return (mine.astype(F32) + came.astype(F32)).astype(BF16)]
    pallas_call x1, Pallas kernels: 114 us -> 103 us  [finish(): pl.pallas_call(functools.partial(finish_body, kinds), in_specs=[hbm] * 5...]
    ppermute x1, starting transfers between devices: 1.88 us -> 9.49 us  [shards_ring(): grad_tokens = lax.ppermute(grad_tokens, ALL, EXCHANGE_PAIRS)]
where the time goes in v5:
time: 732 us; the launch traced here: 724 us
  Pallas kernels  673 us (92%)
  other arithmetic  21.1 us (3%)
  local copies, waits for them, and re-layouts  18.4 us (3%)
  starting transfers between devices  9.49 us (1%)
    pallas_call x2, Pallas kernels, multiply_scatter(): pl.pallas_call(functools.partial(scatter_body, dims, count, len(extras),...  137 us
    pallas_call x1, Pallas kernels, finish(): pl.pallas_call(functools.partial(finish_body, kinds), in_specs=[hbm] * 5...  103 us
    pallas_call x1, Pallas kernels, mixer_forward(): pl.pallas_call(functools.partial(mixer_forward_body, heads, kinds, plan),...  99.4 us
    pallas_call x1, Pallas kernels, begin(): pl.pallas_call(functools.partial(begin_body, kinds), in_specs=[hbm, pl.Bl...  91.9 us
    pallas_call x1, Pallas kernels, mixer_backward(): pl.pallas_call(functools.partial(mixer_backward_body, heads, kinds, plan)...  78.8 us
    pallas_call x1, Pallas kernels, gather_multiply(): pl.pallas_call(functools.partial(gather_body, dims, kinds), in_specs=[hbm...  61.2 us
    pallas_call x1, Pallas kernels, mlp_scatter(): pl.pallas_call(functools.partial(mlp_body, kinds), in_specs=[hbm] * (6 +...  53 us
    pallas_call x1, Pallas kernels, feed(): pl.pallas_call(functools.partial(feed_body, kinds), in_specs=[hbm] * (5 +...  48.5 us
  transfers between devices with their start and end apart: 2, of which 0 were waited for; matrix products, arithmetic and copies ran while one was open for 3% of the time, Pallas kernels for 0%

profile of v5, /device:TPU:0, one launch (start us, length us, event | category | flops | bytes accessed | tf_op | source)
XLA Modules:
  0.0 724.4 jit_solution(15855615936341343343)
XLA Ops:
  0.7 0.0 copy-start.6
  0.7 0.0 copy-start.7
  0.7 0.0 copy-start.8
  0.7 1.3 broadcast_in_dim.39
  2.0 1.0 copy.38
  3.0 1.3 convert_reduce_fusion
  4.9 0.7 divide_sqrt_fusion
  5.6 1.2 bitcast_convert_fusion.refs_2_.refs_3_
  6.8 0.9 pad.16.refs_7_
  7.7 0.8 select_reduce_fusion
  8.4 2.4 multiply_convert_fusion.refs_8_
  10.9 0.0 copy-done.6
  10.9 0.0 copy-done.7
  10.9 0.0 copy-done.8
  10.9 0.6 fusion.5.refs_2_
  11.5 91.9 %begin.1 = (bf16[256,2048]{1,0:T(8,128)(2,1)}, bf16[8,256,2048]{2,1,0:T(8,128)(2,1)}, f32[8,256,1152]{2,1,0:T(8,128)}, bf16[2048,1152]{1,0:T(8,128)(2,1)}, f32[8,768]{1,0:T(8,128)}, /*index=5*/bf16[256,2048]{1,0:T(8,128)(2,1)}) custom-call(bf16[256,2048]{1,0:T(8,128)(2,1)} %refs_0_.1, f32[1,2048]{1,0:T(1,128)} %bitcast.37, f32[8,768]{1,0:T(8,128)} %fusion.5.refs_2_, ...), custom_call_target="tpu_custom_call" | custom-call | tf_op jit(solution)/shard_map/begin/pallas_call | solution.py:1659
  103.4 0.0 copy-start.5
  103.4 99.4 %mixer_forward.1 = (bf16[2048,256]{1,0:T(8,128)(2,1)}, f32[2048,512]{1,0:T(8,128)}, f32[2048,256]{1,0:T(8,128)}, f32[2048,256]{1,0:T(8,128)}, f32[32,2,128,128]{...) custom-call(f32[2048,1152]{1,0:T(8,128)} %bitcast.26, ...), custom_call_target="tpu_custom_call" | custom-call | tf_op jit(solution)/shard_map/mixer_forward/pallas_call | solution.py:225
  202.8 0.0 copy-done.5
  202.8 0.6 broadcast_in_dim.37.refs_3_.refs_6_
  203.4 70.2 %scatter_attn.1 = (f32[256,2048]{1,0:T(8,128)}, bf16[256,2048]{1,0:T(8,128)(2,1)}, bf16[704,2048]{1,0:T(8,128)(2,1)}) custom-call(bf16[8,256,256]{2,1,0:T(8,128)(2,1)} %bitcast.33, bf16[256,2048]{1,0:T(8,128)(2,1)} %get-tuple-element.69.refs_1_.refs_0_, bf16[256,2048]{1,0:T(8,128)(2,1)} %get-tuple-element.70.refs_2_.refs_3_, ...), custom_call_target="tpu_custom_call" | custom-call | tf_op jit(solution)/shard_map/scatter_attn/pallas_call | solution.py:1551
  273.7 48.5 %feed.1 = (bf16[8,256,2048]{2,1,0:T(8,128)(2,1)}, bf16[8,256,704]{2,1,0:T(8,128)(2,1)}, bf16[8,256,704]{2,1,0:T(8,128)(2,1)}, bf16[8,256,704]{2,1,0:T(8,128)(2,1)}) custom-call(bf16[256,2048]{1,0:T(8,128)(2,1)} %get-tuple-element.71.refs_0_, bf16[704,2048]{1,0:T(8,128)(2,1)} %get-tuple-element.72.refs_1_.refs_2_, ...), custom_call_target="tpu_custom_call" | custom-call | tf_op jit(solution)/shard_map/feed/pallas_call | solution.py:1304
  322.2 53.0 %scatter_mlp.1 = (bf16[256,2048]{1,0:T(8,128)(2,1)}, bf16[704,2048]{1,0:T(8,128)(2,1)}, bf16[352,2048]{1,0:T(8,128)(2,1)}) custom-call(bf16[8,256,704]{2,1,0:T(8,128)(2,1)} %get-tuple-element.80.refs_0_, bf16[704,2048]{1,0:T(8,128)(2,1)} %get-tuple-element.74.refs_3_.refs_1_, bf16[2048,2048]{1,0:T(8,128)(2,1)} %bitcast.29, ...), custom_call_target="tpu_custom_call" | custom-call | tf_op jit(solution)/shard_map/scatter_mlp/pallas_call | solution.py:1780
  375.2 67.0 %scatter_normed_mlp_grad.1 = (f32[256,2048]{1,0:T(8,128)}, bf16[256,2048]{1,0:T(8,128)(2,1)}, f32[8,2048]{1,0:T(8,128)}, bf16[704,2048]{1,0:T(8,128)(2,1)}, bf16...) custom-call(bf16[8,256,704]{2,1,0:T(8,128)(2,1)} %get-tuple-element.76.refs_3_.refs_0_, ...), custom_call_target="tpu_custom_call" | custom-call | tf_op jit(solution)/shard_map/scatter_normed_mlp_grad/pallas_call | solution.py:1551
  442.2 61.2 %gather_attn_grad.1 = (f32[8,256,256]{2,1,0:T(8,128)}, bf16[256,2048]{1,0:T(8,128)(2,1)}, bf16[352,2048]{1,0:T(8,128)(2,1)}, bf16[352,2048]{1,0:T(8,128)(2,1)}, bf16[704,2048]{1,0:T(8,128)(2,1)}) custom-call(bf16[256,2048]{1,0:T(8,128)(2,1)} %get-tuple-element.83.block_ref, bf16[256,2048]{1,0:T(8,128)(2,1)} %get-tuple-element.69.refs_1_.refs_0_, ...), custom_call_target="tpu_custom_call" | custom-call | tf_op jit(solution)/shard_map/gather_attn_grad/pallas_call | solution.py:1208
  503.5 78.8 %mixer_backward.1 = (bf16[2048,1152]{1,0:T(8,128)(2,1)}, f32[8,768]{1,0:T(8,128)}, f32[8,128]{1,0:T(8,128)}, bf16[704,2048]{1,0:T(8,128)(2,1)}, bf16[704,2048]{1...) custom-call(f32[2048,1152]{1,0:T(8,128)} %bitcast.27, f32[2048,1152]{1,0:T(8,128)} %bitcast.28, ...), custom_call_target="tpu_custom_call" | custom-call | tf_op jit(solution)/shard_map/mixer_backward/pallas_call | solution.py:452
  582.3 0.7 slice.44
  582.9 0.9 slice_reduce_fusion
  583.8 0.7 select_maximum_fusion.refs_7_
  584.5 103.4 %finish.1 = (bf16[256,2048]{1,0:T(8,128)(2,1)}, bf16[2048,1152]{1,0:T(8,128)(2,1)}, f32[8,768]{1,0:T(8,128)}, f32[8,1024]{1,0:T(8,128)}) custom-call(bf16[2048,1152]{1,0:T(8,128)(2,1)} %get-tuple-element.98.refs_0_, bf16[2048,1152]{1,0:T(8,128)(2,1)} %get-tuple-element.99.refs_1_, bf16[2048,2048]{1,0:T(8,128)(2,1)} %bitcast.32, ...), custom_call_target="tpu_custom_call" | custom-call | tf_op jit(solution)/shard_map/finish/pallas_call | solution.py:2037
  687.9 9.5 %collective-permute-start = (bf16[256,2048]{1,0:T(8,128)(2,1)}, bf16[256,2048]{1,0:T(8,128)(2,1)}, u32[]{:S(2)}, u32[]{:S(2)}) collective-permute-start(bf16[256,2048]{1,0:T(8,128)(2,1)} %get-tuple-element.105), channel_id=1, source_target_pairs={{0,0},{1,1},{2,2},{3,3},{4,8},{5,9},{6,10},{7,11},{8,4},{9,5},{10,... | collective-permute-start | bytes 3145736 | tf_op jit(solution)/shard_map/ppermute | solution.py:2190
  697.4 0.0 collective-permute-start.1
  697.4 5.9 fusion.6
  703.3 0.0 copy-done.1
  703.3 0.0 copy-done.2
  703.3 5.9 convert_bitcast_fusion
  709.2 0.0 copy-done.4
  709.2 0.6 copy_bitcast_fusion
  709.8 0.5 slice_bitcast_fusion.2
  710.4 1.1 slice.60
  711.5 0.9 copy.39
  712.4 2.9 convert_element_type.37
  715.4 3.3 convert_element_type.38
  718.7 0.0 collective-permute-done.1
  718.7 0.6 fusion.7
  719.3 0.0 collective-permute-done
  719.3 2.3 copy.46
  721.6 2.3 copy.47
  (12 shorter events, 0.0 us)
Async XLA Ops:
  0.7 10.2 %copy-start.6 = (bf16[4,256]{1,0:T(4,128)(2,1)S(1)}, bf16[4,256]{1,0:T(4,128)(2,1)}, u32[]{:S(2)}) copy-start(bf16[4,256]{1,0:T(4,128)(2,1)} %param.31) | copy-start | bytes 6148
  0.7 10.2 %copy-start.7 = (bf16[4,256]{1,0:T(4,128)(2,1)S(1)}, bf16[4,256]{1,0:T(4,128)(2,1)}, u32[]{:S(2)}) copy-start(bf16[4,256]{1,0:T(4,128)(2,1)} %param.30) | copy-start | bytes 6148
  0.7 10.2 %copy-start.8 = (bf16[4,256]{1,0:T(4,128)(2,1)S(1)}, bf16[4,256]{1,0:T(4,128)(2,1)}, u32[]{:S(2)}) copy-start(bf16[4,256]{1,0:T(4,128)(2,1)} %param.29) | copy-start | bytes 6148
  103.4 99.4 %copy-start.5 = (bf16[2048]{0:T(1024)(128)(2,1)S(1)}, bf16[2048]{0:T(1024)(128)(2,1)}, u32[]{:S(2)}) copy-start(bf16[2048]{0:T(1024)(128)(2,1)} %param.34) | copy-start | bytes 12292
  687.9 31.4 %collective-permute-start = (bf16[256,2048]{1,0:T(8,128)(2,1)}, bf16[256,2048]{1,0:T(8,128)(2,1)}, u32[]{:S(2)}, u32[]{:S(2)}) collective-permute-start(bf16[256,2048]{1,0:T(8,128)(2,1)} %get-tuple-element.105), channel_id=1, source_target_pairs={{0,0},{1,1},{2,2},{3,3},{4,8},{5,9},{6,10},{7,11},{8,4},{9,5},{10,... | collective-permute-start | bytes 3145736 | tf_op jit(solution)/shard_map/ppermute | solution.py:2190
  697.4 21.3 %collective-permute-start.1 = (f32[8,768]{1,0:T(8,128)}, f32[8,768]{1,0:T(8,128)S(1)}, u32[]{:S(2)}, u32[]{:S(2)}) collective-permute-start(f32[8,768]{1,0:T(8,128)} %get-tuple-element.108), channel_id=1, source_target_pairs={{0,8},{1,9},{2,10},{3,11},{4,12},{5,13},{6,14},{7,15},{8,0},{9,1},... | collective-permute-start | bytes 73736 | tf_op jit(solution)/shard_map/ppermute | solution.py:2191
  697.4 5.9 copy-start.1
  697.4 5.9 copy-start.2
  703.3 5.9 copy-start.4
  712.4 2.9 copy-start
  715.4 3.3 copy-start.3
